TPU v7x, 32 devices: a whole 2x2x4 slice. The times are simulated.
32 devices in a mesh: head: 2 (over x), blk: 16 (over z, y, core).
Axes of the slice: x: 2, y: 2, z: 4, core: 2. Of those that a mesh axis runs over, the one named last changes fastest.
Arguments:
- tokens: bfloat16 [2, 2048, 1536], P(None, ('head', 'blk')), may hold values from -10 to 10
- cotangent: bfloat16 [2, 2048, 1536], P(None, ('head', 'blk')), may hold values from -6 to 6
- lengths: int32 [2], replicated, may hold values from 1792 to 2048, as said below
- routes: int32 [2048, 2, 6], P(('head', 'blk')), may hold values from 0 to 15, all different within a row; in each aligned block of 128 rows (0 to 127, 128 to 255, ..., all dimensions but the last counted through in order) at most 96 rows name the same one
- w_qkv: float32 [1536, 2560], P(('head', 'blk')), may hold values from -0.15625 to 0.15625
- m_qkv: float32 [1536, 2560], P(('head', 'blk')), may hold values from -9.1552734e-05 to 9.1552734e-05
- v_qkv: float32 [1536, 2560], P(('head', 'blk')), may hold values from 2.0497503e-11 to 8.199001e-11
- w_out: float32 [1536, 1536], P(('head', 'blk')), may hold values from -1.25 to 1.25
- m_out: float32 [1536, 1536], P(('head', 'blk')), may hold values from -3.0517578e-05 to 3.0517578e-05
- v_out: float32 [1536, 1536], P(('head', 'blk')), may hold values from 1.0248751e-12 to 4.0995003e-12
- w_shgu: float32 [1536, 2048], P(('head', 'blk')), may hold values from -0.15625 to 0.15625
- m_shgu: float32 [1536, 2048], P(('head', 'blk')), may hold values from -9.1552734e-05 to 9.1552734e-05
- v_shgu: float32 [1536, 2048], P(('head', 'blk')), may hold values from 2.0497503e-11 to 8.199001e-11
- w_shdown: float32 [1024, 1536], P(('head', 'blk')), may hold values from -0.1875 to 0.1875
- m_shdown: float32 [1024, 1536], P(('head', 'blk')), may hold values from -9.1552734e-05 to 9.1552734e-05
- v_shdown: float32 [1024, 1536], P(('head', 'blk')), may hold values from 2.0497503e-11 to 8.199001e-11
- w_router: float32 [1536, 16], P(('head', 'blk')), may hold values from -0.078125 to 0.078125
- m_router: float32 [1536, 16], P(('head', 'blk')), may hold values from -0.0014648438 to 0.0014648438
- v_router: float32 [1536, 16], P(('head', 'blk')), may hold values from 2.0497501e-09 to 3.2796002e-08
- w_gains: float32 [2, 1536], P(None, ('head', 'blk')), may hold values from 0.5 to 1.5
- m_gains: float32 [2, 1536], P(None, ('head', 'blk')), may hold values from -9.1552734e-05 to 9.1552734e-05
- v_gains: float32 [2, 1536], P(None, ('head', 'blk')), may hold values from 2.0497503e-11 to 8.199001e-11
- w_expgu: float32 [16, 1536, 1024], P('blk', 'head'), may hold values from -0.15625 to 0.15625
- m_expgu: float32 [16, 1536, 1024], P('blk', 'head'), may hold values from -9.1552734e-05 to 9.1552734e-05
- v_expgu: float32 [16, 1536, 1024], P('blk', 'head'), may hold values from 2.0497503e-11 to 8.199001e-11
- w_expdown: float32 [16, 512, 1536], P('blk', 'head'), may hold values from -0.75 to 0.75
- m_expdown: float32 [16, 512, 1536], P('blk', 'head'), may hold values from -3.0517578e-05 to 3.0517578e-05
- v_expdown: float32 [16, 512, 1536], P('blk', 'head'), may hold values from 8.199001e-13 to 3.2796003e-12
Outputs:
- block_out: bfloat16 [2, 2048, 1536], P(None, ('head', 'blk'))
- token_grad: float32 [2, 2048, 1536], P(None, ('head', 'blk'))
- grad_qkv: float32 [1536, 2560], P(('head', 'blk'))
- mnew_qkv: float32 [1536, 2560], P(('head', 'blk'))
- vnew_qkv: float32 [1536, 2560], P(('head', 'blk'))
- step_qkv: float32 [1536, 2560], P(('head', 'blk'))
- grad_out: float32 [1536, 1536], P(('head', 'blk'))
- mnew_out: float32 [1536, 1536], P(('head', 'blk'))
- vnew_out: float32 [1536, 1536], P(('head', 'blk'))
- step_out: float32 [1536, 1536], P(('head', 'blk'))
- grad_shgu: float32 [1536, 2048], P(('head', 'blk'))
- mnew_shgu: float32 [1536, 2048], P(('head', 'blk'))
- vnew_shgu: float32 [1536, 2048], P(('head', 'blk'))
- step_shgu: float32 [1536, 2048], P(('head', 'blk'))
- grad_shdown: float32 [1024, 1536], P(('head', 'blk'))
- mnew_shdown: float32 [1024, 1536], P(('head', 'blk'))
- vnew_shdown: float32 [1024, 1536], P(('head', 'blk'))
- step_shdown: float32 [1024, 1536], P(('head', 'blk'))
- grad_router: float32 [1536, 16], P(('head', 'blk'))
- mnew_router: float32 [1536, 16], P(('head', 'blk'))
- vnew_router: float32 [1536, 16], P(('head', 'blk'))
- step_router: float32 [1536, 16], P(('head', 'blk'))
- grad_gains: float32 [2, 1536], P(None, ('head', 'blk'))
- mnew_gains: float32 [2, 1536], P(None, ('head', 'blk'))
- vnew_gains: float32 [2, 1536], P(None, ('head', 'blk'))
- step_gains: float32 [2, 1536], P(None, ('head', 'blk'))
- grad_expgu: float32 [16, 1536, 1024], P('blk', 'head')
- mnew_expgu: float32 [16, 1536, 1024], P('blk', 'head')
- vnew_expgu: float32 [16, 1536, 1024], P('blk', 'head')
- step_expgu: float32 [16, 1536, 1024], P('blk', 'head')
- grad_expdown: float32 [16, 512, 1536], P('blk', 'head')
- mnew_expdown: float32 [16, 512, 1536], P('blk', 'head')
- vnew_expdown: float32 [16, 512, 1536], P('blk', 'head')
- step_expdown: float32 [16, 512, 1536], P('blk', 'head')
- grad_norm: float32 [], replicated
- stats: float32 [3], replicated
Inputs may be any that keep to these rules, and one draw needn't show every extreme that they name: `lengths`: each slot holds one sequence from its first position, of 1792 positions or more; one slot, drawn from the seed, is full. `routes`: each row names 6 different experts. In the rows of one device (aligned blocks of 128 rows, the first two dimensions taken together in order) no expert is named by more than 96 rows, and in some block one expert is named by exactly 96 rows.
All inputs are finite; a program needn't handle non-finite values.
Results may differ from a plain program's by a relative error of at most 0.024.
Values may be sent and summed in bfloat16 or wider, within the bound.
No kernel may reach another device: no remote copies, remote signals or barrier semaphores. Data moves between devices by JAX's collectives and lax.ppermute only.
A program may use at most 256 MiB of HBM per device.

v0:
```python
import jax
import jax.numpy as jnp
from jax import lax
from jax.sharding import PartitionSpec as P

HEADS = 12
KV_HEADS = 4
HEAD_DIM = 128
EXPERT_FF = 512
SHARED = 1024
TOP = 6
ADAM_STEP = 10
GROUP = 3


norm_eps = 1e-05
adam_eps = 1e-08
learn_rate = 0.02
first_decay = 0.9
second_decay = 0.999
weight_decay = 0.1
clip_norm = 1.0
masked_score = -1e30
group_turn = 4


def to_experts(buffer):
    return lax.all_to_all(buffer, "blk", split_axis=0, concat_axis=0, tiled=True)


def from_experts(buffer):
    return lax.all_to_all(buffer, "blk", split_axis=0, concat_axis=0, tiled=True)


def outer_dot(left, right):
    return lax.dot_general(
        left, right, (((0,), (0,)), ((), ())), preferred_element_type=jnp.float32
    )


def back_dot(left, right):
    return lax.dot_general(
        left, right, (((1,), (1,)), ((), ())), preferred_element_type=jnp.float32
    )


def silu_grad(values):
    logistic = jax.nn.sigmoid(values)
    return logistic * (1.0 + values * (1.0 - logistic))


def local_fold(function, init, gathered):
    turns = gathered[0].shape[0] // group_turn

    def advance(turn, carry):
        start = turn * group_turn
        piece = (
            lax.dynamic_slice_in_dim(gathered[0], start, group_turn, 0),
            lax.dynamic_slice_in_dim(gathered[1], start, group_turn, 0),
        )
        return function(carry, piece, start)

    return lax.fori_loop(0, turns, advance, init)


def adam_update(weight, first, second, grad, factor):
    clipped = grad * factor
    first_new = first_decay * first + (1.0 - first_decay) * clipped
    second_new = second_decay * second + (1.0 - second_decay) * clipped * clipped
    first_fix = 1.0 - first_decay**ADAM_STEP
    second_fix = 1.0 - second_decay**ADAM_STEP
    change = -learn_rate * (
        first_new / first_fix / (jnp.sqrt(second_new / second_fix) + adam_eps)
        + weight_decay * weight
    )
    return (first_new, second_new, change)


def local(
    tokens,
    cotangent,
    lengths,
    routes,
    w_qkv,
    m_qkv,
    v_qkv,
    w_out,
    m_out,
    v_out,
    w_shgu,
    m_shgu,
    v_shgu,
    w_shdown,
    m_shdown,
    v_shdown,
    w_router,
    m_router,
    v_router,
    w_gains,
    m_gains,
    v_gains,
    w_expgu,
    m_expgu,
    v_expgu,
    w_expdown,
    m_expdown,
    v_expdown,
):
    low_type = jnp.bfloat16
    full_type = jnp.float32
    heads_axis = lax.axis_size("head")
    blocks_axis = lax.axis_size("blk")
    head_index = lax.axis_index("head")
    blk_index = lax.axis_index("blk")
    seqs, stretch, width = tokens.shape
    rows = seqs * stretch
    experts = w_router.shape[1]
    capacity = min(rows, max(2, 2 * rows * TOP // experts))
    kv_local = KV_HEADS // heads_axis
    span = blocks_axis * stretch
    scale = HEAD_DIM ** (-0.5)
    queries_rows = heads_axis * stretch
    dense = (
        lax.all_gather(w_qkv.astype(low_type), ("head", "blk"), axis=0, tiled=True),
        lax.all_gather(w_out.astype(low_type), ("head", "blk"), axis=0, tiled=True),
        lax.all_gather(w_shgu.astype(low_type), ("head", "blk"), axis=0, tiled=True),
        lax.all_gather(w_shdown.astype(low_type), ("head", "blk"), axis=0, tiled=True),
        lax.all_gather(w_router.astype(low_type), ("head", "blk"), axis=0, tiled=True),
        lax.all_gather(w_gains.astype(low_type), ("head", "blk"), axis=1, tiled=True),
    )
    qkv_full, out_full, shgu_full, shdown_full, router_full, gains_full = dense
    expert_full = (
        lax.all_gather(w_expgu.astype(low_type), "head", axis=1, tiled=True),
        lax.all_gather(w_expdown.astype(low_type), "head", axis=1, tiled=True),
    )
    expgu_full = expert_full[0][0]
    expdown_full = expert_full[1][0]
    gain_in = gains_full[0].astype(full_type)
    gain_mid = gains_full[1].astype(full_type)
    inputs = tokens.astype(full_type).reshape(rows, width)
    inverse_in = lax.rsqrt(jnp.mean(inputs * inputs, axis=1, keepdims=True) + norm_eps)
    normed_in = (inputs * inverse_in * gain_in).astype(low_type)
    projected = jnp.dot(normed_in, qkv_full, preferred_element_type=full_type).astype(low_type)
    stacked = projected.reshape(1, rows, heads_axis, kv_local * (GROUP + 2) * HEAD_DIM)
    by_head = lax.all_to_all(stacked, "head", split_axis=2, concat_axis=0, tiled=True)
    by_head = by_head.reshape(heads_axis, seqs, stretch, kv_local, GROUP + 2, HEAD_DIM)
    queries = by_head[:, :, :, :, :GROUP, :]
    keys = by_head[:, :, :, :, GROUP, :]
    values = by_head[:, :, :, :, GROUP + 1, :]
    query_pos = (
        jnp.arange(heads_axis)[:, None] * span + blk_index * stretch + jnp.arange(stretch)[None, :]
    ).reshape(-1)

    def piece_scores(key_piece, start):
        count = key_piece.shape[0]
        raw = jnp.einsum(
            "astkgd,nbsukd->skgatnbu", queries, key_piece, preferred_element_type=full_type
        )
        raw = raw.reshape(seqs, kv_local, GROUP, queries_rows, count * heads_axis * stretch) * scale
        key_pos = (
            (start + jnp.arange(count))[:, None, None] * stretch
            + jnp.arange(heads_axis)[None, :, None] * span
            + jnp.arange(stretch)[None, None, :]
        ).reshape(-1)
        allowed = (key_pos[None, None, :] <= query_pos[None, :, None]) & (
            key_pos[None, None, :] < lengths[:, None, None]
        )
        allowed = allowed[:, None, None]
        return (jnp.where(allowed, raw, masked_score), allowed)

    kept = (
        lax.all_gather(keys[None], "blk", axis=0, tiled=True),
        lax.all_gather(values[None], "blk", axis=0, tiled=True),
    )

    def norm_fold(carry, piece, start):
        top, total = carry
        scores, allowed = piece_scores(piece[0], start)
        new_top = jnp.maximum(top, jnp.max(scores, axis=-1))
        shifted = jnp.where(allowed, jnp.exp(scores - new_top[..., None]), 0.0)
        return (new_top, total * jnp.exp(top - new_top) + jnp.sum(shifted, axis=-1))

    stat_shape = (seqs, kv_local, GROUP, queries_rows)
    top, total = local_fold(
        norm_fold,
        (jnp.full(stat_shape, masked_score, full_type), jnp.zeros(stat_shape, full_type)),
        kept,
    )
    log_total = top + jnp.log(total)

    def out_fold(carry, piece, start):
        keys_part, values_part = piece
        count = keys_part.shape[0]
        scores, allowed = piece_scores(keys_part, start)
        weights = jnp.where(allowed, jnp.exp(scores - log_total[..., None]), 0.0).astype(low_type)
        weights = weights.reshape(
            seqs, kv_local, GROUP, heads_axis, stretch, count, heads_axis, stretch
        )
        return carry + jnp.einsum(
            "skgatnbu,nbsukd->astkgd", weights, values_part, preferred_element_type=full_type
        )

    outputs = local_fold(out_fold, jnp.zeros(queries.shape, full_type), kept)
    attended = outputs.astype(low_type).reshape(heads_axis, rows, 1, kv_local * GROUP * HEAD_DIM)
    attended_tok = lax.all_to_all(
        attended, "head", split_axis=0, concat_axis=2, tiled=True
    ).reshape(rows, HEADS * HEAD_DIM)
    branch = jnp.dot(attended_tok, out_full, preferred_element_type=full_type)
    middle = inputs + branch
    inverse_mid = lax.rsqrt(jnp.mean(middle * middle, axis=1, keepdims=True) + norm_eps)
    normed_mid = (middle * inverse_mid * gain_mid).astype(low_type)
    expert_ids = jnp.arange(experts, dtype=jnp.int32)
    hits_ts = routes[..., None] == expert_ids
    named_ts = jnp.sum(hits_ts.astype(jnp.int32), axis=2).reshape(rows, experts)
    before_ts = (jnp.cumsum(named_ts, axis=0) - named_ts).reshape(stretch, seqs, experts)
    route_rows = jnp.transpose(routes, (1, 0, 2)).reshape(rows, TOP)
    hits = jnp.transpose(hits_ts, (1, 0, 2, 3)).reshape(rows, TOP, experts)
    before = jnp.transpose(before_ts, (1, 0, 2)).reshape(rows, experts)
    slots = jnp.sum(jnp.where(hits, before[:, None, :], 0), axis=2)
    flat_route = route_rows.reshape(-1)
    flat_slot = slots.reshape(-1)
    logits = jnp.dot(normed_mid, router_full, preferred_element_type=full_type)
    picked = jnp.sum(jnp.where(hits, logits[:, None, :], 0.0), axis=2)
    gates = jax.nn.softmax(picked, axis=1)
    outgoing = (
        jnp.zeros((experts, capacity, width), low_type)
        .at[flat_route, flat_slot]
        .set(jnp.repeat(normed_mid, TOP, axis=0))
    )
    arrived = to_experts(outgoing)
    flat_in = arrived.reshape(-1, width)
    hidden = jnp.dot(flat_in, expgu_full, preferred_element_type=full_type)
    gate_part = hidden[:, :EXPERT_FF]
    up_part = hidden[:, EXPERT_FF:]
    middle_act = (jax.nn.silu(gate_part) * up_part).astype(low_type)
    expert_out = jnp.dot(middle_act, expdown_full, preferred_element_type=full_type).astype(
        low_type
    )
    returned = from_experts(expert_out.reshape(arrived.shape))
    gathered_out = returned[flat_route, flat_slot].reshape(rows, TOP, width).astype(full_type)
    routed = jnp.sum(gates[:, :, None] * gathered_out, axis=1)
    shared_hidden = jnp.dot(normed_mid, shgu_full, preferred_element_type=full_type)
    shared_gate = shared_hidden[:, :SHARED]
    shared_up = shared_hidden[:, SHARED:]
    shared_mid = (jax.nn.silu(shared_gate) * shared_up).astype(low_type)
    shared_out = jnp.dot(shared_mid, shdown_full, preferred_element_type=full_type)
    final = middle + routed + shared_out
    block_out = final.astype(low_type).reshape(seqs, stretch, width)
    own_pos = (head_index * blocks_axis + blk_index) * stretch + jnp.arange(stretch)
    valid = (own_pos[None, :] < lengths[:, None]).astype(full_type).reshape(rows, 1)
    stat_sums = jnp.stack(
        [
            jnp.sum(branch * branch * valid),
            jnp.sum(middle * middle * valid),
            jnp.sum(final * final * valid),
        ]
    )
    grad_final = cotangent.astype(full_type).reshape(rows, width) * valid
    grad_low = grad_final.astype(low_type)
    grad_shdown = outer_dot(shared_mid, grad_low)
    grad_shared_mid = back_dot(grad_low, shdown_full)
    grad_shared_hidden = jnp.concatenate(
        [
            grad_shared_mid * shared_up * silu_grad(shared_gate),
            grad_shared_mid * jax.nn.silu(shared_gate),
        ],
        axis=1,
    ).astype(low_type)
    grad_shgu = outer_dot(normed_mid, grad_shared_hidden)
    grad_normed = back_dot(grad_shared_hidden, shgu_full)
    grad_gates = jnp.sum(grad_final[:, None, :] * gathered_out, axis=2)
    grad_picked = gates * (grad_gates - jnp.sum(gates * grad_gates, axis=1, keepdims=True))
    grad_logits = jnp.sum(jnp.where(hits, grad_picked[:, :, None], 0.0), axis=1).astype(low_type)
    grad_router = outer_dot(normed_mid, grad_logits)
    grad_normed = grad_normed + back_dot(grad_logits, router_full)
    grad_outputs = (
        (gates[:, :, None] * grad_final[:, None, :]).astype(low_type).reshape(rows * TOP, width)
    )
    outgoing_grad = (
        jnp.zeros((experts, capacity, width), low_type).at[flat_route, flat_slot].set(grad_outputs)
    )
    arrived_grad = to_experts(outgoing_grad).reshape(-1, width)
    grad_expdown = outer_dot(middle_act, arrived_grad)
    grad_middle_act = back_dot(arrived_grad, expdown_full)
    grad_hidden = jnp.concatenate(
        [
            grad_middle_act * up_part * silu_grad(gate_part),
            grad_middle_act * jax.nn.silu(gate_part),
        ],
        axis=1,
    ).astype(low_type)
    grad_expgu = outer_dot(flat_in, grad_hidden)
    grad_in = back_dot(grad_hidden, expgu_full).astype(low_type).reshape(arrived.shape)
    returned_grad = from_experts(grad_in)
    grad_normed = grad_normed + jnp.sum(
        returned_grad[flat_route, flat_slot].reshape(rows, TOP, width).astype(full_type), axis=1
    )
    scaled_mid = grad_normed * gain_mid
    grad_gain_mid = jnp.sum(grad_normed * middle * inverse_mid, axis=0)
    grad_mid_total = (
        grad_final
        + inverse_mid * scaled_mid
        - middle * inverse_mid**3 * jnp.mean(scaled_mid * middle, axis=1, keepdims=True)
    )
    grad_branch = grad_mid_total.astype(low_type)
    grad_out_w = outer_dot(attended_tok, grad_branch)
    grad_attended = back_dot(grad_branch, out_full).astype(low_type)
    grad_heads = lax.all_to_all(
        grad_attended.reshape(1, rows, heads_axis, kv_local * GROUP * HEAD_DIM),
        "head",
        split_axis=2,
        concat_axis=0,
        tiled=True,
    )
    grad_heads = grad_heads.reshape(queries.shape)
    row_dot = jnp.sum(grad_heads.astype(full_type) * outputs, axis=-1)
    row_dot = jnp.transpose(row_dot, (1, 3, 4, 0, 2)).reshape(stat_shape)

    def piece_grads(grad_q, keys_part, values_part, start):
        count = keys_part.shape[0]
        scores, allowed = piece_scores(keys_part, start)
        weights = jnp.where(allowed, jnp.exp(scores - log_total[..., None]), 0.0)
        full_shape = (seqs, kv_local, GROUP, heads_axis, stretch, count, heads_axis, stretch)
        weights_low = weights.astype(low_type).reshape(full_shape)
        grad_weights = jnp.einsum(
            "astkgd,nbsukd->skgatnbu", grad_heads, values_part, preferred_element_type=full_type
        )
        grad_weights = grad_weights.reshape(weights.shape)
        grad_scores = (
            (weights * (grad_weights - row_dot[..., None])).astype(low_type).reshape(full_shape)
        )
        grad_q = (
            grad_q
            + jnp.einsum(
                "skgatnbu,nbsukd->astkgd", grad_scores, keys_part, preferred_element_type=full_type
            )
            * scale
        )
        piece_k = (
            jnp.einsum(
                "skgatnbu,astkgd->nbsukd", grad_scores, queries, preferred_element_type=full_type
            )
            * scale
        )
        piece_v = jnp.einsum(
            "skgatnbu,astkgd->nbsukd", weights_low, grad_heads, preferred_element_type=full_type
        )
        return (grad_q, piece_k, piece_v)

    def back_fold(carry, piece, start):
        grad_q, grad_k_all, grad_v_all = carry
        grad_q, piece_k, piece_v = piece_grads(grad_q, piece[0], piece[1], start)
        grad_k_all = lax.dynamic_update_slice_in_dim(grad_k_all, piece_k, start, 0)
        grad_v_all = lax.dynamic_update_slice_in_dim(grad_v_all, piece_v, start, 0)
        return (grad_q, grad_k_all, grad_v_all)

    buffer_shape = (blocks_axis,) + keys.shape
    start_carry = (
        jnp.zeros(queries.shape, full_type),
        jnp.zeros(buffer_shape, full_type),
        jnp.zeros(buffer_shape, full_type),
    )
    grad_q, grad_k_all, grad_v_all = local_fold(back_fold, start_carry, kept)
    key_sums = (
        lax.psum_scatter(grad_k_all, "blk", scatter_dimension=0, tiled=True),
        lax.psum_scatter(grad_v_all, "blk", scatter_dimension=0, tiled=True),
    )
    key_grad_sum = key_sums[0][0]
    value_grad_sum = key_sums[1][0]
    grad_stack = jnp.concatenate(
        [grad_q, key_grad_sum[:, :, :, :, None, :], value_grad_sum[:, :, :, :, None, :]], axis=4
    )
    grad_stack = grad_stack.astype(low_type).reshape(
        heads_axis, rows, 1, kv_local * (GROUP + 2) * HEAD_DIM
    )
    grad_projected = lax.all_to_all(
        grad_stack, "head", split_axis=0, concat_axis=2, tiled=True
    ).reshape(rows, qkv_full.shape[1])
    grad_qkv = outer_dot(normed_in, grad_projected)
    grad_normed_in = back_dot(grad_projected, qkv_full)
    scaled_in = grad_normed_in * gain_in
    grad_gain_in = jnp.sum(grad_normed_in * inputs * inverse_in, axis=0)
    grad_inputs = (
        grad_mid_total
        + inverse_in * scaled_in
        - inputs * inverse_in**3 * jnp.mean(scaled_in * inputs, axis=1, keepdims=True)
    )
    token_grad = grad_inputs.reshape(seqs, stretch, width)
    shares = (
        lax.psum_scatter(grad_qkv, ("head", "blk"), scatter_dimension=0, tiled=True),
        lax.psum_scatter(grad_out_w, ("head", "blk"), scatter_dimension=0, tiled=True),
        lax.psum_scatter(grad_shgu, ("head", "blk"), scatter_dimension=0, tiled=True),
        lax.psum_scatter(grad_shdown, ("head", "blk"), scatter_dimension=0, tiled=True),
        lax.psum_scatter(grad_router, ("head", "blk"), scatter_dimension=0, tiled=True),
        lax.psum_scatter(
            jnp.stack([grad_gain_in, grad_gain_mid]),
            ("head", "blk"),
            scatter_dimension=1,
            tiled=True,
        ),
    )
    g_qkv, g_out, g_shgu, g_shdown, g_router, g_gains = shares
    expert_shares = (
        lax.psum_scatter(
            grad_expgu[None].astype(jnp.bfloat16), "head", scatter_dimension=1, tiled=True
        ).astype(jnp.float32),
        lax.psum_scatter(
            grad_expdown[None].astype(jnp.bfloat16), "head", scatter_dimension=1, tiled=True
        ).astype(jnp.float32),
    )
    g_expgu, g_expdown = expert_shares
    local_squares = (
        jnp.sum(g_qkv * g_qkv)
        + jnp.sum(g_out * g_out)
        + jnp.sum(g_shgu * g_shgu)
        + jnp.sum(g_shdown * g_shdown)
        + jnp.sum(g_router * g_router)
        + jnp.sum(g_gains * g_gains)
        + jnp.sum(g_expgu * g_expgu)
        + jnp.sum(g_expdown * g_expdown)
    )
    squares, stat_total = lax.psum((local_squares, stat_sums), ("head", "blk"))
    count = jnp.sum(lengths).astype(full_type) * width
    stats = jnp.sqrt(stat_total / count)
    grad_norm = jnp.sqrt(squares)
    factor = clip_norm / jnp.maximum(grad_norm, clip_norm)
    a_qkv, b_qkv, c_qkv = adam_update(w_qkv, m_qkv, v_qkv, g_qkv, factor)
    a_out, b_out, c_out = adam_update(w_out, m_out, v_out, g_out, factor)
    a_shgu, b_shgu, c_shgu = adam_update(w_shgu, m_shgu, v_shgu, g_shgu, factor)
    a_shdown, b_shdown, c_shdown = adam_update(w_shdown, m_shdown, v_shdown, g_shdown, factor)
    a_router, b_router, c_router = adam_update(w_router, m_router, v_router, g_router, factor)
    a_gains, b_gains, c_gains = adam_update(w_gains, m_gains, v_gains, g_gains, factor)
    a_expgu, b_expgu, c_expgu = adam_update(w_expgu, m_expgu, v_expgu, g_expgu, factor)
    a_expdown, b_expdown, c_expdown = adam_update(
        w_expdown, m_expdown, v_expdown, g_expdown, factor
    )
    return (
        block_out,
        token_grad,
        g_qkv,
        a_qkv,
        b_qkv,
        c_qkv,
        g_out,
        a_out,
        b_out,
        c_out,
        g_shgu,
        a_shgu,
        b_shgu,
        c_shgu,
        g_shdown,
        a_shdown,
        b_shdown,
        c_shdown,
        g_router,
        a_router,
        b_router,
        c_router,
        g_gains,
        a_gains,
        b_gains,
        c_gains,
        g_expgu,
        a_expgu,
        b_expgu,
        c_expgu,
        g_expdown,
        a_expdown,
        b_expdown,
        c_expdown,
        grad_norm,
        stats,
    )


def solution(mesh):
    in_specs = (
        P(None, ("head", "blk"), None),
        P(None, ("head", "blk"), None),
        P(),
        P(("head", "blk"), None, None),
        P(("head", "blk"), None),
        P(("head", "blk"), None),
        P(("head", "blk"), None),
        P(("head", "blk"), None),
        P(("head", "blk"), None),
        P(("head", "blk"), None),
        P(("head", "blk"), None),
        P(("head", "blk"), None),
        P(("head", "blk"), None),
        P(("head", "blk"), None),
        P(("head", "blk"), None),
        P(("head", "blk"), None),
        P(("head", "blk"), None),
        P(("head", "blk"), None),
        P(("head", "blk"), None),
        P(None, ("head", "blk")),
        P(None, ("head", "blk")),
        P(None, ("head", "blk")),
        P("blk", "head", None),
        P("blk", "head", None),
        P("blk", "head", None),
        P("blk", "head", None),
        P("blk", "head", None),
        P("blk", "head", None),
    )
    out_specs = (
        P(None, ("head", "blk"), None),
        P(None, ("head", "blk"), None),
        P(("head", "blk"), None),
        P(("head", "blk"), None),
        P(("head", "blk"), None),
        P(("head", "blk"), None),
        P(("head", "blk"), None),
        P(("head", "blk"), None),
        P(("head", "blk"), None),
        P(("head", "blk"), None),
        P(("head", "blk"), None),
        P(("head", "blk"), None),
        P(("head", "blk"), None),
        P(("head", "blk"), None),
        P(("head", "blk"), None),
        P(("head", "blk"), None),
        P(("head", "blk"), None),
        P(("head", "blk"), None),
        P(("head", "blk"), None),
        P(("head", "blk"), None),
        P(("head", "blk"), None),
        P(("head", "blk"), None),
        P(None, ("head", "blk")),
        P(None, ("head", "blk")),
        P(None, ("head", "blk")),
        P(None, ("head", "blk")),
        P("blk", "head", None),
        P("blk", "head", None),
        P("blk", "head", None),
        P("blk", "head", None),
        P("blk", "head", None),
        P("blk", "head", None),
        P("blk", "head", None),
        P("blk", "head", None),
        P(),
        P(),
    )
    return jax.shard_map(local, mesh=mesh, in_specs=in_specs, out_specs=out_specs, check_vma=False)
```

profile of v0, /device:TPU:0, one launch (start us, length us, event | category | flops | bytes accessed | tf_op | source)
XLA Modules:
  0.0 2015.9 jit_solution(2347508027758956329)
XLA Ops:
  9.8 43.0 %all-gather.2 = bf16[32,48,2]{1,2,0:T(2,128)(2,1)S(1)} all-gather(bf16[1,48,2]{1,2,0:T(2,128)(2,1)S(1)} %convert_bitcast_fusion.1), channel_id=1, replica_groups=mesh['head'=2,'blk'=16] {'head','blk'}, dimensions={0}, use_global_device_ids=true | all-gather | bytes 6336 | tf_op jit(solution)/shard_map/all_gather | solution.py:129
  56.4 33.1 %all-gather.13.cloned.1.call-done = bf16[1536,2560]{1,0:T(8,128)(2,1)} async-done(((bf16[48,2560]{1,0:T(8,128)(2,1)}), bf16[1536,2560]{1,0:T(8,128)(2,1)}) %all-gather.13.cloned.1.call-update) | async-done | bytes 7864336 | tf_op jit(solution)/shard_map/all_gather | solution.py:124
  94.2 13.5 all_to_all.80
  120.8 33.1 %all-gather.27.cloned.1.call-done = bf16[32,2,64,2,1,128]{5,2,4,3,1,0:T(8,128)(2,1)} async-done(((bf16[2,2,64,2,1,128]{5,2,4,3,1,0:T(8,128)(2,1)}), bf16[32,2,64,2,1,128]{5,2,4,3,1,0:T(8,128)(2,1)}) %all-gather.27.cloned.1.call-update) | async-done | bytes 2097168 | tf_op jit(solution)/shard_map/all_gather | solution.py:172
  157.1 45.7 %while.48 = (s32[]{:T(128)}, f32[2,2,3,128]{3,1,2,0:T(2,128)S(1)}, f32[2,2,3,128]{3,1,2,0:T(2,128)S(1)}, s32[2]{0:T(128)S(1)}, bf16[16,2,2,64,2,128]{5,3,1,0,4,2...) while((s32[]{:T(128)}, f32[2,2,3,128]{3,1,2,0:T(2,128)S(1)}, ...), condition=%wide.region_4.5_spmd.clone, body=%wide.region_1.4_spmd.clone.sunk | while | flops 207824016 | bytes 7896366 | solution.py:63
  203.6 21.9 %while.49 = (s32[]{:T(128)}, f32[2,2,64,2,3,128]{5,2,0,4,3,1:T(8,128)S(1)}, bf16[16,2,2,64,2,128]{5,3,4,2,1,0:T(8,128)(2,1)}, s32[2]{0:T(128)S(1)}, bf16[16,2,2,...) while((s32[]{:T(128)}, ...), condition=%wide.region_6.7_spmd.clone, body=%wide.region_5.6_spmd.clone.sunk | while | flops 407176864 | bytes 5532981 | solution.py:63
  231.2 6.8 all-to-all-done.1
  238.2 24.4 %all-gather.15.cloned.1.call-done = bf16[1536,1536]{1,0:T(8,128)(2,1)} async-done(((bf16[48,1536]{1,0:T(8,128)(2,1)}), bf16[1536,1536]{1,0:T(8,128)(2,1)}) %all-gather.15.cloned.1.call-update) | async-done | bytes 4718608 | tf_op jit(solution)/shard_map/all_gather | solution.py:125
  273.4 120.1 %scatter_fusion = bf16[16,96,1536]{2,1,0:T(8,128)(2,1)} fusion(bf16[16,96,1536]{2,1,0:T(8,128)(2,1)} %broadcast.800.clone, s32[768]{0:T(1024)S(1)} %get-tuple-element.759, bf16[768,1536]{1,0:T(8,128)(2,1)S(1)} %copy-done.14), kind=kCustom, calls=%fused_computation.2 | custom fusion | bytes 7084032 | tf_op jit(solution)/shard_map/scatter | solution.py:228
  400.0 156.3 %all-gather.3 = bf16[32,48,16]{1,2,0:T(8,128)(2,1)S(1)} all-gather(bf16[1,48,16]{1,2,0:T(8,128)(2,1)S(1)} %convert_bitcast_fusion), channel_id=1, replica_groups=mesh['head'=2,'blk'=16] {'head','blk'}, dimensions={0}, use_global_device_ids=true | all-gather | bytes 50688 | tf_op jit(solution)/shard_map/all_gather | solution.py:128
  574.9 119.7 %scatter_fusion.1 = bf16[16,96,1536]{2,1,0:T(8,128)(2,1)} fusion(bf16[16,96,1536]{2,1,0:T(8,128)(2,1)} %broadcast.800.clone.1, s32[768]{0:T(1024)S(1)} %get-tuple-element.759, bf16[768,1536]{1,0:T(8,128)(2,1)S(1)} %multiply_convert_fusion), kind=kCustom, calls=%fused_computation.3 | custom fusion | bytes 7084032 | tf_op jit(solution)/shard_map/scatter | solution.py:280
  700.3 9.9 fusion.81
  710.2 82.1 %all-to-all-done.4 = bf16[16,96,1536]{2,1,0:T(8,128)(2,1)} async-done(((bf16[16,96,1536]{2,1,0:T(8,128)(2,1)}), bf16[16,96,1536]{2,1,0:T(8,128)(2,1)}, u32[]{:S(2)}, u32[]{:S(2)}) %all-to-all-start.4) | async-done | bytes 4718624 | tf_op jit(solution)/shard_map/all_to_all | solution.py:28
  792.4 10.0 multiply_convert_fusion.2
  806.7 30.1 %all-to-all-start.3 = ((bf16[16,96,1536]{2,1,0:T(8,128)(2,1)}), bf16[16,96,1536]{2,1,0:T(8,128)(2,1)}, u32[]{:S(2)}, u32[]{:S(2)}) async-start(bf16[16,96,1536]{2,1,0:T(8,128)(2,1)} %bitcast.369), calls=%async_computation.3 | async-start | bytes 9437184 | tf_op jit(solution)/shard_map/all_to_all | solution.py:32
  849.5 8.7 convolution_convert_fusion
  858.2 82.3 %all-to-all-done.3 = bf16[16,96,1536]{2,1,0:T(8,128)(2,1)} async-done(((bf16[16,96,1536]{2,1,0:T(8,128)(2,1)}), bf16[16,96,1536]{2,1,0:T(8,128)(2,1)}, u32[]{:S(2)}, u32[]{:S(2)}) %all-to-all-start.3) | async-done | bytes 4718624 | tf_op jit(solution)/shard_map/all_to_all | solution.py:32
  940.5 30.4 %all-to-all-start.5 = ((bf16[16,96,1536]{2,1,0:T(8,128)(2,1)}), bf16[16,96,1536]{2,1,0:T(8,128)(2,1)}, u32[]{:S(2)}, u32[]{:S(2)}) async-start(bf16[16,96,1536]{2,1,0:T(8,128)(2,1)} %bitcast.368), calls=%async_computation.5 | async-start | bytes 9437184 | tf_op jit(solution)/shard_map/all_to_all | solution.py:32
  977.3 9.1 fusion.78
  993.5 10.8 gather_fusion
  1013.3 48.6 %all-to-all-done.5 = bf16[16,96,1536]{2,1,0:T(8,128)(2,1)} async-done(((bf16[16,96,1536]{2,1,0:T(8,128)(2,1)}), bf16[16,96,1536]{2,1,0:T(8,128)(2,1)}, u32[]{:S(2)}, u32[]{:S(2)}) %all-to-all-start.5) | async-done | bytes 4718624 | tf_op jit(solution)/shard_map/all_to_all | solution.py:32
  1061.8 10.8 gather_fusion.1
  1111.4 83.2 %while.50 = (s32[]{:T(128)}, f32[2,2,64,2,3,128]{5,2,0,4,3,1:T(8,128)}, f32[16,2,2,64,2,128]{5,3,1,0,4,2:T(8,128)}, f32[16,2,2,64,2,128]{5,3,1,0,4,2:T(8,128)}, ...) while((s32[]{:T(128)}, ...), condition=%wide.region_24.25_spmd.clone, body=%wide.region_23.24_spmd.clone.sunk | while | flops 1017120384 | bytes 39515576 | solution.py:63
  1195.8 210.9 %all-reduce.5 = (bf16[16,2,2,64,2,128]{5,3,1,0,4,2:T(8,128)(2,1)S(1)}, bf16[16,2,2,64,2,128]{5,3,1,0,4,2:T(8,128)(2,1)}) all-reduce(f32[16,2,2,64,2,128]{5,3,1,0,4,2:T(8,128)} %get-tuple-element.506, f32[16,2,2,64,2,128]{5,3,1,0,4,2:T(8,128)} %get-tuple-element.505), channel_id=5, replica_groups=mesh['head'=2,'blk'=16] {'blk'}, use_global_device_ids=true, to_apply=%region_26.27.clone | all-reduce | flops 2097152 | bytes 12582912
  1416.3 9.4 all-to-all-done.7
  1426.1 6.9 fusion.100
  1440.1 7.7 fusion.144
  1462.4 58.2 %reduce-scatter.31.cloned.1.call-done = f32[48,16]{1,0:T(8,128)} async-done(((f32[1536,16]{1,0:T(8,128)}), f32[48,16]{1,0:T(8,128)}) %reduce-scatter.31.cloned.1.call-update) | async-done | bytes 3088
  1522.1 98.7 %reduce-scatter.33.cloned.1.call-done = f32[48,2]{1,0:T(8,128)} async-done(((f32[1536,2]{1,0:T(8,128)}), f32[48,2]{1,0:T(8,128)}) %reduce-scatter.33.cloned.1.call-update) | async-done | bytes 400
  1622.2 139.6 %reduce-scatter.21.cloned.1.call-done = f32[48,1536]{1,0:T(8,128)} async-done(((f32[1536,1536]{1,0:T(8,128)}), f32[48,1536]{1,0:T(8,128)}) %reduce-scatter.21.cloned.1.call-update) | async-done | bytes 294928 | tf_op jit(solution)/shard_map/reduce_scatter | solution.py:391
  1763.5 175.4 %reduce-scatter.19.cloned.1.call-done = f32[48,2560]{1,0:T(8,128)} async-done(((f32[1536,2560]{1,0:T(8,128)}), f32[48,2560]{1,0:T(8,128)}) %reduce-scatter.19.cloned.1.call-update) | async-done | bytes 491536 | tf_op jit(solution)/shard_map/reduce_scatter | solution.py:390
  1948.1 39.8 %all-reduce.2 = (f32[]{:T(128)}, f32[3]{0:T(128)S(1)}) all-reduce(f32[]{:T(128)S(6)} %add.676, f32[3]{0:T(128)S(1)} %pad_maximum_fusion.8), channel_id=1, replica_groups=mesh['head'=2,'blk'=16] {'head','blk'}, use_global_device_ids=true, to_apply=%region_46.47 | all-reduce | flops 4 | bytes 32 | tf_op jit(solution)/shard_map/psum | solution.py:422
  (581 shorter events, 362.0 us)
Async XLA Ops:
  7.2 82.3 %all-gather.13.cloned.1.call-start = ((), (), s32[]{:S(2)}) async-start(), calls=%async_computation.16 | async-start | bytes 8110080 | tf_op jit(solution)/shard_map/all_gather | solution.py:124
  9.0 144.9 %all-gather.27.cloned.1.call-start = ((), (), s32[]{:S(2)}) async-start(), calls=%async_computation.29 | async-start | bytes 2228224 | tf_op jit(solution)/shard_map/all_gather | solution.py:172
  113.9 89.0 %all-gather.25.cloned.1.call-start = ((), (), s32[]{:S(2)}) async-start(), calls=%async_computation.28 | async-start | bytes 2228224 | tf_op jit(solution)/shard_map/all_gather | solution.py:173
  115.6 147.0 %all-gather.15.cloned.1.call-start = ((), (), s32[]{:S(2)}) async-start(), calls=%async_computation.17 | async-start | bytes 4866048 | tf_op jit(solution)/shard_map/all_gather | solution.py:125
  116.3 584.0 %all-gather.17.cloned.1.call-start = ((), (), s32[]{:S(2)}) async-start(), calls=%async_computation.18 | async-start | bytes 4718592 | tf_op jit(solution)/shard_map/all_gather | solution.py:133
  227.0 11.0 all-to-all-start.1
  267.9 828.4 %copy-start.3 = (bf16[128,1536]{1,0:T(8,128)(2,1)}, bf16[128,1536]{1,0:T(8,128)(2,1)S(1)}, u32[]{:S(2)}) copy-start(bf16[128,1536]{1,0:T(8,128)(2,1)S(1)} %multiply_convert_fusion.4) | copy-start | bytes 1179652
  393.4 301.2 %all-to-all-start.2 = ((bf16[16,96,1536]{2,1,0:T(8,128)(2,1)}), bf16[16,96,1536]{2,1,0:T(8,128)(2,1)}, u32[]{:S(2)}, u32[]{:S(2)}) async-start(bf16[16,96,1536]{2,1,0:T(8,128)(2,1)} %scatter_fusion), calls=%async_computation.2 | async-start | bytes 9437184 | tf_op jit(solution)/shard_map/all_to_all | solution.py:28
  398.2 312.0 %all-gather.19.cloned.1.call-start = ((), (), s32[]{:S(2)}) async-start(), calls=%async_computation.19 | async-start | bytes 2359296 | tf_op jit(solution)/shard_map/all_gather | solution.py:134
  399.2 438.2 %all-gather.21.cloned.1.call-start = ((), (), s32[]{:S(2)}) async-start(), calls=%async_computation.20 | async-start | bytes 6488064 | tf_op jit(solution)/shard_map/all_gather | solution.py:126
  694.6 97.7 %all-to-all-start.4 = ((bf16[16,96,1536]{2,1,0:T(8,128)(2,1)}), bf16[16,96,1536]{2,1,0:T(8,128)(2,1)}, u32[]{:S(2)}, u32[]{:S(2)}) async-start(bf16[16,96,1536]{2,1,0:T(8,128)(2,1)} %scatter_fusion.1), calls=%async_computation.4 | async-start | bytes 9437184 | tf_op jit(solution)/shard_map/all_to_all | solution.py:28
  699.3 141.9 %all-gather.23.cloned.1.call-start = ((), (), s32[]{:S(2)}) async-start(), calls=%async_computation.21 | async-start | bytes 3244032 | tf_op jit(solution)/shard_map/all_gather | solution.py:127
  806.7 133.8 %all-to-all-start.3 = ((bf16[16,96,1536]{2,1,0:T(8,128)(2,1)}), bf16[16,96,1536]{2,1,0:T(8,128)(2,1)}, u32[]{:S(2)}, u32[]{:S(2)}) async-start(bf16[16,96,1536]{2,1,0:T(8,128)(2,1)} %bitcast.369), calls=%async_computation.3 | async-start | bytes 9437184 | tf_op jit(solution)/shard_map/all_to_all | solution.py:32
  836.9 612.3 %reduce-scatter.25.cloned.1.call-start = ((), (), s32[]{:S(2)}) async-start(), calls=%async_computation.25 | async-start | bytes 6488064 | tf_op jit(solution)/shard_map/reduce_scatter | solution.py:393
  940.5 121.3 %all-to-all-start.5 = ((bf16[16,96,1536]{2,1,0:T(8,128)(2,1)}), bf16[16,96,1536]{2,1,0:T(8,128)(2,1)}, u32[]{:S(2)}, u32[]{:S(2)}) async-start(bf16[16,96,1536]{2,1,0:T(8,128)(2,1)} %bitcast.368), calls=%async_computation.5 | async-start | bytes 9437184 | tf_op jit(solution)/shard_map/all_to_all | solution.py:32
  970.9 479.9 %reduce-scatter.29.cloned.1.call-start = ((), (), s32[]{:S(2)}) async-start(), calls=%async_computation.27 | async-start | bytes 2359296 | tf_op jit(solution)/shard_map/reduce_scatter | solution.py:407
  977.1 477.0 %reduce-scatter.27.cloned.1.call-start = ((), (), s32[]{:S(2)}) async-start(), calls=%async_computation.26 | async-start | bytes 4718592 | tf_op jit(solution)/shard_map/reduce_scatter | solution.py:404
  1092.7 10.5 all-to-all-start.6
  1096.2 362.4 %reduce-scatter.23.cloned.1.call-start = ((), (), s32[]{:S(2)}) async-start(), calls=%async_computation.24 | async-start | bytes 12976128 | tf_op jit(solution)/shard_map/reduce_scatter | solution.py:392
  1410.5 15.2 all-to-all-start.7
  1414.9 105.8 %reduce-scatter.31.cloned.1.call-start = ((), (), s32[]{:S(2)}) async-start(), calls=%async_computation.30 | async-start | bytes 811008
  1416.1 204.6 %reduce-scatter.33.cloned.1.call-start = ((), (), s32[]{:S(2)}) async-start(), calls=%async_computation.31 | async-start | bytes 811008
  1434.2 327.6 %reduce-scatter.21.cloned.1.call-start = ((), (), s32[]{:S(2)}) async-start(), calls=%async_computation.23 | async-start | bytes 9732096 | tf_op jit(solution)/shard_map/reduce_scatter | solution.py:391
  1439.3 499.5 %reduce-scatter.19.cloned.1.call-start = ((), (), s32[]{:S(2)}) async-start(), calls=%async_computation.22 | async-start | bytes 16220160 | tf_op jit(solution)/shard_map/reduce_scatter | solution.py:390
  1458.5 530.1 %copy-start.89 = (f32[2,48]{1,0:T(2,128)S(1)}, f32[2,48]{1,0:T(2,128)}, u32[]{:S(2)}) copy-start(f32[2,48]{1,0:T(2,128)} %param.53) | copy-start | bytes 1156
  1458.5 530.1 %copy-start.90 = (f32[2,48]{1,0:T(2,128)S(1)}, f32[2,48]{1,0:T(2,128)}, u32[]{:S(2)}) copy-start(f32[2,48]{1,0:T(2,128)} %param.55) | copy-start | bytes 1156
  1458.5 530.1 %copy-start.91 = (f32[2,48]{1,0:T(2,128)S(1)}, f32[2,48]{1,0:T(2,128)}, u32[]{:S(2)}) copy-start(f32[2,48]{1,0:T(2,128)} %param.54) | copy-start | bytes 1156
  1458.5 530.7 %copy-start.72 = (f32[48,16]{0,1:T(8,128)S(1)}, f32[48,16]{0,1:T(8,128)}, u32[]{:S(2)}) copy-start(f32[48,16]{0,1:T(8,128)} %param.50) | copy-start | bytes 9220
  1458.5 530.7 %copy-start.77 = (f32[48,16]{0,1:T(8,128)S(1)}, f32[48,16]{0,1:T(8,128)}, u32[]{:S(2)}) copy-start(f32[48,16]{0,1:T(8,128)} %param.52) | copy-start | bytes 9220
  1458.5 530.7 %copy-start.78 = (f32[48,16]{0,1:T(8,128)S(1)}, f32[48,16]{0,1:T(8,128)}, u32[]{:S(2)}) copy-start(f32[48,16]{0,1:T(8,128)} %param.51) | copy-start | bytes 9220
  1458.5 531.8 %copy-start.17 = (f32[1,256,1536]{2,1,0:T(8,128)S(1)}, f32[1,256,1536]{2,1,0:T(8,128)}, u32[]{:S(2)}) copy-start(f32[1,256,1536]{2,1,0:T(8,128)} %param.59) | copy-start | bytes 4718596
  1521.5 474.4 %copy-start.65 = (f32[48,16]{0,1:T(8,128)}, f32[48,16]{0,1:T(8,128)S(1)}, u32[]{:S(2)}) copy-start(f32[48,16]{0,1:T(8,128)S(1)} %copy.289) | copy-start | bytes 9220
  (98 other events, 1772.5 us)
Sparse Core Ops, SparseCore 0:
  11.5 77.9 all-gather.12
  114.0 39.9 all-gather.26
  156.7 40.1 all-gather.24
  200.2 62.3 all-gather.14
  264.6 43.7 all-gather.16
  400.8 28.1 all-gather.18
  432.5 102.5 all-gather.20
  703.6 108.1 all-gather.22
  848.2 160.1 reduce-scatter.24
  1011.2 28.1 reduce-scatter.28
  1042.2 43.3 reduce-scatter.26
  1104.4 212.6 reduce-scatter.22
  1421.4 99.2 reduce-scatter.30
  1526.2 94.5 reduce-scatter.32
  1627.1 134.6 reduce-scatter.20
  1769.3 169.5 reduce-scatter.18
where the time goes:
time: 2030 us; the launch traced here: 2020 us
  waiting for transfers between devices  793 us (39%)
  blocking collectives  463 us (23%)
  local copies, waits for them, and re-layouts  335 us (17%)
  matrix products  215 us (11%)
  other arithmetic  102 us (5%)
  starting transfers between devices  83.3 us (4%)
  between operations  23.3 us (1%)
    unnamed x1, blocking collectives  211 us
    reduce_scatter x1, waiting for transfers between devices, local(): lax.psum_scatter(grad_qkv, ('head', 'blk'), scatter_dimension=0, tiled=True)  175 us
    unnamed x18, waiting for transfers between devices  157 us
    all_gather x1, blocking collectives, local(): lax.all_gather(w_router.astype(low_type), ('head', 'blk'), axis=0, tiled=...  156 us
    reduce_scatter x1, waiting for transfers between devices, local(): lax.psum_scatter(grad_out_w, ('head', 'blk'), scatter_dimension=0, tiled=...  140 us
    all_to_all x2, waiting for transfers between devices, from_experts(): lax.all_to_all(buffer, 'blk', split_axis=0, concat_axis=0, tiled=True)  131 us
    scatter x1, local copies, waits for them, and re-layouts, local(): outgoing = jnp.zeros((experts, capacity, width), low_type).at[flat_route,...  120 us
    scatter x1, local copies, waits for them, and re-layouts, local(): jnp.zeros((experts, capacity, width), low_type).at[flat_route, flat_slot]  120 us
  transfers between devices with their start and end apart: 23, of which 13 were waited for; matrix products, arithmetic and copies ran while one was open for 30% of the time, Pallas kernels for 0%

commit v1 on v0

--- a/solution.py
+++ b/solution.py
@@ -1,6 +1,10 @@
+import functools
+
 import jax
 import jax.numpy as jnp
 from jax import lax
+from jax.experimental import pallas as pl
+from jax.experimental.pallas import tpu as pltpu
 from jax.sharding import PartitionSpec as P
 
 HEADS = 12
@@ -74,6 +78,232 @@
         + weight_decay * weight
     )
     return (first_new, second_new, change)
+
+
+WIDTH_ROWS = 512
+
+
+def axis_bits(name):
+    size = lax.axis_size(name)
+    return [(name, 1 << k) for k in reversed(range(size.bit_length() - 1))]
+
+
+def swap(values, step):
+    name, bit = step
+    size = lax.axis_size(name)
+    return lax.ppermute(values, name, [(i, i ^ bit) for i in range(size)])
+
+
+def own_bit(step):
+    return (lax.axis_index(step[0]) // step[1]) % 2
+
+
+def both_orders():
+    head_bits, blk_bits = axis_bits("head"), axis_bits("blk")
+    first = blk_bits[:-1] + head_bits + blk_bits[-1:]
+    second = blk_bits[:-2] + head_bits + blk_bits[-2:]
+    return (first, second)
+
+
+def blk_orders():
+    blk_bits = axis_bits("blk")
+    return (blk_bits, blk_bits[-2:-1] + blk_bits[:-2] + blk_bits[-1:])
+
+
+def lockstep(pieces, orders, act, backwards=False):
+    count = len(orders[0])
+    for turn in reversed(range(count)) if backwards else range(count):
+        pieces = [act(piece, order[turn]) for piece, order in zip(pieces, orders)]
+    return pieces
+
+
+def gather_relative(pieces, orders):
+    def act(piece, step):
+        return jnp.concatenate([piece, swap(piece, step)], axis=0)
+
+    return lockstep([piece[None] for piece in pieces], orders, act)
+
+
+def scatter_relative(pieces, orders):
+    def act(piece, step):
+        half = piece.shape[0] // 2
+        return piece[:half] + swap(piece[half:], step)
+
+    return [piece[0] for piece in lockstep(pieces, orders, act, backwards=True)]
+
+
+def gather_rows(pieces, orders):
+    places = axis_bits("head") + axis_bits("blk")
+
+    def act(piece, step):
+        place = places.index(step)
+        shape = [1] * piece.ndim
+        shape[place] = 2
+        mine = lax.broadcasted_iota(jnp.int32, shape, place) == own_bit(step)
+        return jnp.where(mine, piece, swap(piece, step))
+
+    wide = [piece.reshape((1,) * len(places) + piece.shape) for piece in pieces]
+    return [
+        full.reshape(-1, full.shape[-1]) for full in lockstep(wide, orders, act)
+    ]
+
+
+def scatter_rows(pieces, orders):
+    places = axis_bits("head") + axis_bits("blk")
+    devices = 1 << len(places)
+
+    def act(piece, step):
+        place = places.index(step)
+        bit = own_bit(step)
+        mine = lax.dynamic_slice_in_dim(piece, bit, 1, place)
+        theirs = lax.dynamic_slice_in_dim(piece, 1 - bit, 1, place)
+        return mine + swap(theirs, step)
+
+    wide = [
+        piece.reshape((2,) * len(places) + (piece.shape[0] // devices, piece.shape[1]))
+        for piece in pieces
+    ]
+    return [
+        own.reshape(own.shape[-2:]) for own in lockstep(wide, orders, act, backwards=True)
+    ]
+
+
+def sum_everywhere(values):
+    for step in axis_bits("blk") + axis_bits("head"):
+        values = values + swap(values, step)
+    return values
+
+
+def block_devices(order):
+    offsets = [(0, 0)]
+    for name, bit in order:
+        offsets = offsets + [
+            (h ^ bit, b) if name == "head" else (h, b ^ bit) for h, b in offsets
+        ]
+    head_index, blk_index = lax.axis_index("head"), lax.axis_index("blk")
+    heads = jnp.array([h for h, _ in offsets], jnp.int32)
+    blks = jnp.array([b for _, b in offsets], jnp.int32)
+    return (head_index ^ heads) * lax.axis_size("blk") + (blk_index ^ blks)
+
+
+def stack_heads(block):
+    return jnp.concatenate(
+        [block[:, i * HEAD_DIM : (i + 1) * HEAD_DIM] for i in range(GROUP)], axis=0
+    )
+
+
+def group_scores(query, keys, limit, key_pos):
+    scores = lax.dot_general(
+        query, keys, (((1,), (1,)), ((), ())), preferred_element_type=jnp.float32
+    ) * (HEAD_DIM ** (-0.5))
+    return jnp.where(key_pos <= limit, scores, masked_score)
+
+
+def attend_kernel(q_ref, kv_ref, pos_ref, limit_ref, out_ref, low_ref, log_ref):
+    stretch = q_ref.shape[0]
+    query = stack_heads(q_ref[...])
+    keys = kv_ref[:, :, :HEAD_DIM].reshape(-1, HEAD_DIM)
+    values = kv_ref[:, :, HEAD_DIM:].reshape(-1, HEAD_DIM)
+    limit = jnp.concatenate([limit_ref[...]] * GROUP, axis=0)
+    scores = group_scores(query, keys, limit, pos_ref[...])
+    top = jnp.max(scores, axis=1, keepdims=True)
+    weights = jnp.exp(scores - top)
+    total = jnp.sum(weights, axis=1, keepdims=True)
+    out = jnp.dot(weights.astype(jnp.bfloat16), values, preferred_element_type=jnp.float32)
+    out = out / total
+    log_ref[0] = top + jnp.log(total)
+    for i in range(GROUP):
+        part = out[i * stretch : (i + 1) * stretch]
+        columns = slice(i * HEAD_DIM, (i + 1) * HEAD_DIM)
+        out_ref[:, columns] = part
+        low_ref[:, columns] = part.astype(jnp.bfloat16)
+
+
+def attend_back_kernel(
+    q_ref, kv_ref, pos_ref, limit_ref, grad_ref, out_ref, log_ref, dq_ref, dkv_ref
+):
+    stretch = q_ref.shape[0]
+    scale = HEAD_DIM ** (-0.5)
+    low_type = jnp.bfloat16
+    query = stack_heads(q_ref[...])
+    keys = kv_ref[:, :, :HEAD_DIM].reshape(-1, HEAD_DIM)
+    values = kv_ref[:, :, HEAD_DIM:].reshape(-1, HEAD_DIM)
+    grad = stack_heads(grad_ref[...])
+    row_dot = jnp.sum(
+        grad.astype(jnp.float32) * stack_heads(out_ref[...]), axis=1, keepdims=True
+    )
+    limit = jnp.concatenate([limit_ref[...]] * GROUP, axis=0)
+    scores = group_scores(query, keys, limit, pos_ref[...])
+    weights = jnp.exp(scores - log_ref[0])
+    grad_weights = lax.dot_general(
+        grad, values, (((1,), (1,)), ((), ())), preferred_element_type=jnp.float32
+    )
+    grad_scores = (weights * (grad_weights - row_dot)).astype(low_type)
+    weights_low = weights.astype(low_type)
+    dq = jnp.dot(grad_scores, keys, preferred_element_type=jnp.float32) * scale
+    dk = outer_dot(grad_scores, query) * scale
+    dv = outer_dot(weights_low, grad)
+    block = dkv_ref.shape[:2] + (HEAD_DIM,)
+    dkv_ref[:, :, :HEAD_DIM] = dk.astype(low_type).reshape(block)
+    dkv_ref[:, :, HEAD_DIM:] = dv.astype(low_type).reshape(block)
+    for i in range(GROUP):
+        part = dq[i * stretch : (i + 1) * stretch]
+        dq_ref[:, i * HEAD_DIM : (i + 1) * HEAD_DIM] = part.astype(low_type)
+
+
+def attention_specs(stretch, devices):
+    wide = pl.BlockSpec((stretch, GROUP * HEAD_DIM), lambda s: (s, 0))
+    pair = pl.BlockSpec((devices, stretch, 2 * HEAD_DIM), lambda s: (0, s, 0))
+    pos = pl.BlockSpec((1, devices * stretch), lambda s: (0, 0))
+    limit = pl.BlockSpec((stretch, 1), lambda s: (s, 0))
+    log = pl.BlockSpec((1, GROUP * stretch, 1), lambda s: (s, 0, 0))
+    return wide, pair, pos, limit, log
+
+
+def attention_cost(seqs, stretch, devices, matmuls):
+    scores = seqs * GROUP * stretch * devices * stretch
+    return pl.CostEstimate(
+        flops=2 * matmuls * scores * HEAD_DIM,
+        bytes_accessed=devices * seqs * stretch * 2 * HEAD_DIM * 2,
+        transcendentals=scores,
+    )
+
+
+def attend(query, pair, key_pos, limit, seqs, stretch):
+    devices = pair.shape[0]
+    wide, kv, pos, lim, log = attention_specs(stretch, devices)
+    return pl.pallas_call(
+        attend_kernel,
+        grid=(seqs,),
+        in_specs=[wide, kv, pos, lim],
+        out_specs=[wide, wide, log],
+        out_shape=[
+            jax.ShapeDtypeStruct(query.shape, jnp.float32),
+            jax.ShapeDtypeStruct(query.shape, jnp.bfloat16),
+            jax.ShapeDtypeStruct((seqs, GROUP * stretch, 1), jnp.float32),
+        ],
+        compiler_params=pltpu.CompilerParams(vmem_limit_bytes=48 << 20),
+        cost_estimate=attention_cost(seqs, stretch, devices, 2),
+        name="attend",
+    )(query, pair, key_pos, limit)
+
+
+def attend_back(query, pair, key_pos, limit, grad, out, log_total, seqs, stretch):
+    devices = pair.shape[0]
+    wide, kv, pos, lim, log = attention_specs(stretch, devices)
+    return pl.pallas_call(
+        attend_back_kernel,
+        grid=(seqs,),
+        in_specs=[wide, kv, pos, lim, wide, wide, log],
+        out_specs=[wide, kv],
+        out_shape=[
+            jax.ShapeDtypeStruct(query.shape, jnp.bfloat16),
+            jax.ShapeDtypeStruct(pair.shape, jnp.bfloat16),
+        ],
+        compiler_params=pltpu.CompilerParams(vmem_limit_bytes=48 << 20),
+        cost_estimate=attention_cost(seqs, stretch, devices, 5),
+        name="attend_back",
+    )(query, pair, key_pos, limit, grad, out, log_total)
 
 
 def local(
@@ -474,6 +704,327 @@
     )
 
 
+def local_cube(
+    tokens,
+    cotangent,
+    lengths,
+    routes,
+    w_qkv,
+    m_qkv,
+    v_qkv,
+    w_out,
+    m_out,
+    v_out,
+    w_shgu,
+    m_shgu,
+    v_shgu,
+    w_shdown,
+    m_shdown,
+    v_shdown,
+    w_router,
+    m_router,
+    v_router,
+    w_gains,
+    m_gains,
+    v_gains,
+    w_expgu,
+    m_expgu,
+    v_expgu,
+    w_expdown,
+    m_expdown,
+    v_expdown,
+):
+    low_type = jnp.bfloat16
+    full_type = jnp.float32
+    heads_axis = lax.axis_size("head")
+    blocks_axis = lax.axis_size("blk")
+    head_index = lax.axis_index("head")
+    blk_index = lax.axis_index("blk")
+    devices = heads_axis * blocks_axis
+    me = head_index * blocks_axis + blk_index
+    seqs, stretch, width = tokens.shape
+    rows = seqs * stretch
+    experts = w_router.shape[1]
+    shard = w_qkv.shape[0]
+    group_cols = (GROUP + 2) * HEAD_DIM
+    query_cols = GROUP * HEAD_DIM
+    extra = -(-(experts + 2) // 128) * 128
+    tail = -(-2 * experts // 128) * 128
+    all_orders = both_orders()
+    row_orders = blk_orders()
+    head_bits = axis_bits("head")
+
+    small = jnp.concatenate([w_router, w_gains.T], axis=1)
+    small = jnp.pad(small, ((0, 0), (0, extra - experts - 2)))
+    half_cols = w_qkv.shape[1] // 2
+    first_half, second_half = gather_rows(
+        [
+            w_qkv[:, :half_cols].astype(low_type),
+            jnp.concatenate([w_qkv[:, half_cols:], small], axis=1).astype(low_type),
+        ],
+        all_orders,
+    )
+    router_full = second_half[:, half_cols : half_cols + experts]
+    gains_full = second_half[:, half_cols + experts : half_cols + experts + 2].astype(full_type)
+    second_half = second_half[:, :half_cols]
+    gain_in = gains_full[:, 0][None]
+    gain_mid = gains_full[:, 1][None]
+    out_full = lax.all_gather(w_out.astype(low_type), ("head", "blk"), axis=0, tiled=True)
+    shgu_full = lax.all_gather(w_shgu.astype(low_type), ("head", "blk"), axis=0, tiled=True)
+    shdown_full = lax.all_gather(w_shdown.astype(low_type), ("head", "blk"), axis=0, tiled=True)
+
+    own_pos = me * stretch + jnp.arange(stretch, dtype=jnp.int32)
+    valid = (own_pos[None, :] < lengths[:, None]).astype(full_type).reshape(rows, 1)
+    limit = jnp.minimum(own_pos[None, :], lengths[:, None] - 1).reshape(rows, 1)
+    grad_final = cotangent.astype(full_type).reshape(rows, width) * valid
+    grad_low = grad_final.astype(low_type)
+
+    inputs = tokens.astype(full_type).reshape(rows, width)
+    inverse_in = lax.rsqrt(jnp.mean(inputs * inputs, axis=1, keepdims=True) + norm_eps)
+    normed_in = (inputs * inverse_in * gain_in).astype(low_type)
+    projected = [
+        jnp.dot(normed_in, half, preferred_element_type=full_type).astype(low_type)
+        for half in (first_half, second_half)
+    ]
+    per_half = KV_HEADS // 2
+    group_parts = [
+        projected[g // per_half][:, (g % per_half) * group_cols : (g % per_half + 1) * group_cols]
+        for g in range(KV_HEADS)
+    ]
+    queries = [part[:, :query_cols] for part in group_parts]
+    kv_orders = [all_orders[g % 2] for g in range(KV_HEADS)]
+    pairs = gather_relative([part[:, query_cols:] for part in group_parts], kv_orders)
+    key_pos = [
+        (block_devices(order)[:, None] * stretch + jnp.arange(stretch, dtype=jnp.int32)).reshape(
+            1, -1
+        )
+        for order in all_orders
+    ]
+
+    route_rows = jnp.transpose(routes, (1, 0, 2)).reshape(rows, TOP)
+    hits = route_rows[:, :, None] == jnp.arange(experts, dtype=jnp.int32)
+    named = jnp.sum(hits.astype(full_type), axis=1)
+    early = jnp.concatenate(
+        [grad_low, jnp.pad(named, ((0, 0), (0, tail - experts))).astype(low_type)], axis=1
+    )
+    early, projected[0] = lax.optimization_barrier((early, projected[0]))
+
+    def to_columns(values):
+        pieces = gather_relative(list(values.reshape(seqs, stretch, -1)), row_orders)
+        return jnp.concatenate([piece.reshape(-1, values.shape[1]) for piece in pieces], axis=0)
+
+    def from_columns(values):
+        pieces = values.reshape(seqs, blocks_axis, stretch, -1)
+        return jnp.concatenate(scatter_relative(list(pieces), row_orders), axis=0)
+
+    early_all = to_columns(early)
+    grads_all = early_all[:, :width]
+    named_all = early_all[:, width : width + experts] > 0
+
+    def gather_head(values):
+        own = values.astype(low_type)[None]
+        for step in reversed(head_bits):
+            mine = jnp.arange(2).reshape(2, 1, 1, 1) == own_bit(step)
+            own = jnp.where(mine, own[None], swap(own, step)[None])
+            own = own.reshape((-1,) + own.shape[2:])
+        return own.reshape(-1, values.shape[1])
+
+    def scatter_head(values):
+        for step in head_bits:
+            half = values.shape[0] // 2
+            bit = own_bit(step)
+            mine = lax.dynamic_slice_in_dim(values, bit * half, half, 0)
+            theirs = lax.dynamic_slice_in_dim(values, (1 - bit) * half, half, 0)
+            values = mine + swap(theirs.astype(low_type), step).astype(full_type)
+        return values
+
+    expgu_full = gather_head(w_expgu[0])
+    expdown_full = gather_head(w_expdown[0])
+
+    attended = [
+        attend(queries[g], pairs[g], key_pos[g % 2], limit, seqs, stretch)
+        for g in range(KV_HEADS)
+    ]
+    attended_tok = jnp.concatenate([item[1] for item in attended], axis=1)
+    branch = jnp.dot(attended_tok, out_full, preferred_element_type=full_type)
+    middle = inputs + branch
+    inverse_mid = lax.rsqrt(jnp.mean(middle * middle, axis=1, keepdims=True) + norm_eps)
+    normed_mid = (middle * inverse_mid * gain_mid).astype(low_type)
+
+    def all_gates(values, chosen):
+        logits = jnp.dot(values, router_full, preferred_element_type=full_type)
+        logits = jnp.where(chosen, logits, masked_score)
+        raised = jnp.where(chosen, jnp.exp(logits - jnp.max(logits, axis=1, keepdims=True)), 0.0)
+        return raised / jnp.sum(raised, axis=1, keepdims=True)
+
+    own_expert = jnp.arange(experts, dtype=jnp.int32)[None] == blk_index
+    mid_all = to_columns(normed_mid)
+    gate = jnp.sum(
+        jnp.where(own_expert, all_gates(mid_all, named_all), 0.0), axis=1, keepdims=True
+    )
+    hidden = jnp.dot(mid_all, expgu_full, preferred_element_type=full_type)
+    gate_part = hidden[:, :EXPERT_FF]
+    up_part = hidden[:, EXPERT_FF:]
+    middle_act = (jax.nn.silu(gate_part) * up_part).astype(low_type).astype(full_type)
+    weighed_act = (gate * middle_act).astype(low_type)
+    pulled = back_dot(grads_all, expdown_full)
+    routed_terms = jnp.dot(weighed_act, expdown_full, preferred_element_type=full_type)
+    grad_gate = jnp.sum(pulled * middle_act, axis=1, keepdims=True)
+    grad_middle_act = gate * pulled
+    grad_hidden = jnp.concatenate(
+        [
+            grad_middle_act * up_part * silu_grad(gate_part),
+            grad_middle_act * jax.nn.silu(gate_part),
+        ],
+        axis=1,
+    ).astype(low_type)
+    gate_high = grad_gate.astype(low_type).astype(full_type)
+    lanes = jnp.arange(tail, dtype=jnp.int32)[None]
+    gate_lanes = jnp.where(lanes == blk_index, gate_high, 0.0) + jnp.where(
+        lanes == experts + blk_index, grad_gate - gate_high, 0.0
+    )
+    in_terms = jnp.concatenate([back_dot(grad_hidden, expgu_full), gate_lanes], axis=1)
+    back_sums = from_columns(in_terms.astype(low_type)).astype(full_type)
+    routed = from_columns(routed_terms.astype(low_type)).astype(full_type)
+    grad_expdown = outer_dot(weighed_act, grads_all)
+    grad_expgu = outer_dot(mid_all, grad_hidden)
+    g_expgu = scatter_head(grad_expgu)[None]
+    g_expdown = scatter_head(grad_expdown)[None]
+
+    shared_hidden = jnp.dot(normed_mid, shgu_full, preferred_element_type=full_type)
+    shared_gate = shared_hidden[:, :SHARED]
+    shared_up = shared_hidden[:, SHARED:]
+    shared_mid = (jax.nn.silu(shared_gate) * shared_up).astype(low_type)
+    shared_out = jnp.dot(shared_mid, shdown_full, preferred_element_type=full_type)
+    final = middle + routed + shared_out
+    block_out = final.astype(low_type).reshape(seqs, stretch, width)
+    stat_sums = jnp.stack(
+        [
+            jnp.sum(branch * branch * valid),
+            jnp.sum(middle * middle * valid),
+            jnp.sum(final * final * valid),
+        ]
+    )
+
+    def sum_rows(values):
+        return lax.psum_scatter(
+            values.astype(low_type), ("head", "blk"), scatter_dimension=0, tiled=True
+        ).astype(full_type)
+
+    grad_shdown = outer_dot(shared_mid, grad_low)
+    grad_shared_mid = back_dot(grad_low, shdown_full)
+    grad_shared_hidden = jnp.concatenate(
+        [
+            grad_shared_mid * shared_up * silu_grad(shared_gate),
+            grad_shared_mid * jax.nn.silu(shared_gate),
+        ],
+        axis=1,
+    ).astype(low_type)
+    grad_shgu = outer_dot(normed_mid, grad_shared_hidden)
+    g_shdown = sum_rows(grad_shdown)
+    g_shgu = sum_rows(grad_shgu)
+    grad_normed = back_dot(grad_shared_hidden, shgu_full)
+
+    chosen = named > 0
+    gates = all_gates(normed_mid, chosen)
+    grad_gates = back_sums[:, width : width + experts] + (
+        back_sums[:, width + experts : width + 2 * experts]
+    )
+    grad_logits = gates * (grad_gates - jnp.sum(gates * grad_gates, axis=1, keepdims=True))
+    grad_logits = jnp.where(chosen, grad_logits, 0.0).astype(low_type)
+    grad_router = outer_dot(normed_mid, grad_logits)
+    grad_normed = grad_normed + back_dot(grad_logits, router_full) + back_sums[:, :width]
+    scaled_mid = grad_normed * gain_mid
+    grad_gain_mid = jnp.sum(grad_normed * middle * inverse_mid, axis=0)
+    grad_mid_total = (
+        grad_final
+        + inverse_mid * scaled_mid
+        - middle * inverse_mid**3 * jnp.mean(scaled_mid * middle, axis=1, keepdims=True)
+    )
+    grad_branch = grad_mid_total.astype(low_type)
+    grad_attended = back_dot(grad_branch, out_full).astype(low_type)
+    g_out = sum_rows(outer_dot(attended_tok, grad_branch))
+
+    back = [
+        attend_back(
+            queries[g],
+            pairs[g],
+            key_pos[g % 2],
+            limit,
+            grad_attended[:, g * query_cols : (g + 1) * query_cols],
+            attended[g][0],
+            attended[g][2],
+            seqs,
+            stretch,
+        )
+        for g in range(KV_HEADS)
+    ]
+    pair_sums = scatter_relative([item[1] for item in back], kv_orders)
+    grad_groups = [
+        jnp.concatenate([item[0], pair], axis=1) for item, pair in zip(back, pair_sums)
+    ]
+    grad_halves = [
+        jnp.concatenate(grad_groups[:per_half], axis=1),
+        jnp.concatenate(grad_groups[per_half:], axis=1),
+    ]
+    grad_normed_in = back_dot(grad_halves[0], first_half) + back_dot(grad_halves[1], second_half)
+    scaled_in = grad_normed_in * gain_in
+    grad_gain_in = jnp.sum(grad_normed_in * inputs * inverse_in, axis=0)
+    grad_inputs = (
+        grad_mid_total
+        + inverse_in * scaled_in
+        - inputs * inverse_in**3 * jnp.mean(scaled_in * inputs, axis=1, keepdims=True)
+    )
+    token_grad = grad_inputs.reshape(seqs, stretch, width)
+    grad_small = jnp.concatenate(
+        [grad_router, jnp.stack([grad_gain_in, grad_gain_mid], axis=1)], axis=1
+    )
+    grad_small = jnp.pad(grad_small, ((0, 0), (0, extra - experts - 2)))
+    sums = scatter_rows(
+        [
+            outer_dot(normed_in, grad_halves[0]).astype(low_type),
+            jnp.concatenate([outer_dot(normed_in, grad_halves[1]), grad_small], axis=1).astype(
+                low_type
+            ),
+        ],
+        all_orders,
+    )
+    g_qkv = jnp.concatenate([sums[0], sums[1][:, :half_cols]], axis=1).astype(full_type)
+    g_router = sums[1][:, half_cols : half_cols + experts].astype(full_type)
+    g_gains = sums[1][:, half_cols + experts : half_cols + experts + 2].astype(full_type).T
+
+    local_squares = (
+        jnp.sum(g_qkv * g_qkv)
+        + jnp.sum(g_out * g_out)
+        + jnp.sum(g_shgu * g_shgu)
+        + jnp.sum(g_shdown * g_shdown)
+        + jnp.sum(g_router * g_router)
+        + jnp.sum(g_gains * g_gains)
+        + jnp.sum(g_expgu * g_expgu)
+        + jnp.sum(g_expdown * g_expdown)
+    )
+    scalars = jnp.concatenate([local_squares[None], stat_sums])
+    totals = sum_everywhere(jnp.pad(scalars, (0, 124)).reshape(1, 128))[0]
+    count = jnp.sum(lengths).astype(full_type) * width
+    stats = jnp.sqrt(totals[1:4] / count)
+    grad_norm = jnp.sqrt(totals[0])
+    factor = clip_norm / jnp.maximum(grad_norm, clip_norm)
+    outputs = [block_out, token_grad]
+    for weight, first, second, grad in (
+        (w_qkv, m_qkv, v_qkv, g_qkv),
+        (w_out, m_out, v_out, g_out),
+        (w_shgu, m_shgu, v_shgu, g_shgu),
+        (w_shdown, m_shdown, v_shdown, g_shdown),
+        (w_router, m_router, v_router, g_router),
+        (w_gains, m_gains, v_gains, g_gains),
+        (w_expgu, m_expgu, v_expgu, g_expgu),
+        (w_expdown, m_expdown, v_expdown, g_expdown),
+    ):
+        outputs.append(grad)
+        outputs.extend(adam_update(weight, first, second, grad, factor))
+    return (*outputs, grad_norm, stats)
+
+
 def solution(mesh):
     in_specs = (
         P(None, ("head", "blk"), None),
@@ -543,4 +1094,7 @@
         P(),
         P(),
     )
-    return jax.shard_map(local, mesh=mesh, in_specs=in_specs, out_specs=out_specs, check_vma=False)
+    shards = mesh.size
+    cubes = all(size & (size - 1) == 0 for size in mesh.shape.values())
+    step = local_cube if cubes and WIDTH_ROWS % (16 * shards) == 0 else local
+    return jax.shard_map(step, mesh=mesh, in_specs=in_specs, out_specs=out_specs, check_vma=False)

time: 2030 us -> 953 us (0.47)
  blocking collectives: 463 us -> 0 us
  waiting for transfers between devices: 793 us -> 427 us
  local copies, waits for them, and re-layouts: 335 us -> 128 us
  matrix products: 215 us -> 113 us
  other arithmetic: 102 us -> 134 us
  Pallas kernels: 0 us -> 22.7 us
    ppermute x0 -> x101, waiting for transfers between devices: none -> 393 us  [swap(): return lax.ppermute(values, name, [(i, i ^ bit) for i in range(size)])]
    reduce_scatter x6 -> x3, waiting for transfers between devices: 315 us -> 33.8 us  [sum_rows(): lax.psum_scatter(values.astype(low_type), ('head', 'blk'), scatter_dimens...]
    scatter x2 -> x0, local copies, waits for them, and re-layouts: 240 us -> none  [the longest x1 120 us: local(): outgoing = jnp.zeros((experts, capacity, width), low_type).at[flat_route,...]
    all_to_all x7 -> x0, waiting for transfers between devices: 230 us -> none  [the longest x2 131 us: from_experts(): lax.all_to_all(buffer, 'blk', split_axis=0, concat_axis=0, tiled=True)]
    unnamed x1 -> x0, blocking collectives: 211 us -> none
    all_gather x2 -> x0, blocking collectives: 199 us -> none  [the longest x1 156 us: local(): lax.all_gather(w_router.astype(low_type), ('head', 'blk'), axis=0, tiled=...]
    unnamed x18 -> x6, waiting for transfers between devices: 157 us -> 0.1 us
    dot_general x35 -> x9, matrix products: 136 us -> 33.5 us  [the longest x1 12.3 us: local_cube(): hidden = jnp.dot(mid_all, expgu_full, preferred_element_type=full_type)]
  transfers between devices with their start and end apart: 23 -> 107, of which waited for: 13 -> 49; matrix products, arithmetic and copies ran while one was open for 30% -> 34% of each run, Pallas kernels for 0% -> 2%
where the time goes in v1:
time: 953 us; the launch traced here: 941 us
  waiting for transfers between devices  427 us (45%)
  other arithmetic  134 us (14%)
  local copies, waits for them, and re-layouts  128 us (13%)
  matrix products  113 us (12%)
  starting transfers between devices  91.6 us (10%)
  between operations  24.8 us (3%)
  Pallas kernels  22.7 us (2%)
    ppermute x101, waiting for transfers between devices, swap(): return lax.ppermute(values, name, [(i, i ^ bit) for i in range(size)])  393 us
    ppermute x101, starting transfers between devices, swap(): return lax.ppermute(values, name, [(i, i ^ bit) for i in range(size)])  91.1 us
    dot_general x8, matrix products, back_dot(): lax.dot_general(left, right, (((1,), (1,)), ((), ())), preferred_element_...  50.8 us
    unnamed x342, local copies, waits for them, and re-layouts  44.3 us
    reduce_scatter x3, waiting for transfers between devices, sum_rows(): lax.psum_scatter(values.astype(low_type), ('head', 'blk'), scatter_dimens...  33.8 us
    dot_general x8, matrix products, outer_dot(): lax.dot_general(left, right, (((0,), (0,)), ((), ())), preferred_element_...  28.9 us
    slice x37, local copies, waits for them, and re-layouts, act(): return piece[:half] + swap(piece[half:], step)  22.4 us
    mul x8, other arithmetic, adam_update(): -learn_rate  21.7 us
  transfers between devices with their start and end apart: 107, of which 49 were waited for; matrix products, arithmetic and copies ran while one was open for 34% of the time, Pallas kernels for 2%

profile of v1, /device:TPU:0, one launch (start us, length us, event | category | flops | bytes accessed | tf_op | source)
XLA Modules:
  0.0 941.0 jit_solution(6825142314244976702)
XLA Ops:
  40.6 7.1 collective-permute-done.6
  58.7 42.7 %collective-permute-done.2 = bf16[1,2,2,1,1,48,1408]{6,5,2,1,4,3,0:T(8,128)(2,1)S(1)} collective-permute-done((bf16[1,2,2,1,1,48,1408]{6,5,2,1,4,3,0:T(8,128)(2,1)S(1)}, bf16[1,2,2,1,1,48,1408]{6,5,2,1,4,3,0:T(8,128)(2,1)S(1)}, u32[]{:S(2)}, u32[]{:S(2)}) %collective-permute-start.2) | collective-permute-done | bytes 540704 | tf_op jit(solution)/shard_map/ppermute | solution.py:94
  103.4 19.8 %collective-permute-done.8 = bf16[1,2,2,2,1,48,1280]{6,5,3,2,1,4,0:T(8,128)(2,1)S(1)} collective-permute-done((bf16[1,2,2,2,1,48,1280]{6,5,3,2,1,4,0:T(8,128)(2,1)S(1)}, bf16[1,2,2,2,1,48,1280]{6,5,3,2,1,4,0:T(8,128)(2,1)S(1)}, u32[]{:S(2)}, u32[]{:S(2)}) %collective-permute-start.8) | collective-permute-done | bytes 983072 | tf_op jit(solution)/shard_map/ppermute | solution.py:94
  123.6 6.0 collective-permute-done.3
  159.9 19.2 %collective-permute-done.20 = bf16[1,128,256]{2,1,0:T(8,128)(2,1)S(1)} collective-permute-done((bf16[1,128,256]{2,1,0:T(8,128)(2,1)S(1)}, bf16[1,128,256]{2,1,0:T(8,128)(2,1)S(1)}, u32[]{:S(2)}, u32[]{:S(2)}) %collective-permute-start.20) | collective-permute-done | bytes 65568 | tf_op jit(solution)/shard_map/ppermute | solution.py:94
  209.8 10.8 %collective-permute-done.31 = bf16[2,64,1664]{2,1,0:T(8,128)(2,1)S(1)} collective-permute-done((bf16[2,64,1664]{2,1,0:T(8,128)(2,1)S(1)}, bf16[2,64,1664]{2,1,0:T(8,128)(2,1)S(1)}, u32[]{:S(2)}, u32[]{:S(2)}) %collective-permute-start.31) | collective-permute-done | bytes 426016 | tf_op jit(solution)/shard_map/ppermute | solution.py:94
  233.6 18.9 %collective-permute-done.32 = bf16[4,64,1664]{2,1,0:T(8,128)(2,1)S(1)} collective-permute-done((bf16[4,64,1664]{2,1,0:T(8,128)(2,1)S(1)}, bf16[4,64,1664]{2,1,0:T(8,128)(2,1)S(1)}, u32[]{:S(2)}, u32[]{:S(2)}) %collective-permute-start.32) | collective-permute-done | bytes 852000 | tf_op jit(solution)/shard_map/ppermute | solution.py:94
  296.9 10.2 %collective-permute-done.38 = bf16[1,64,1536]{2,1,0:T(8,128)(2,1)S(1)} collective-permute-done((bf16[1,64,1536]{2,1,0:T(8,128)(2,1)S(1)}, bf16[1,64,1536]{2,1,0:T(8,128)(2,1)S(1)}, u32[]{:S(2)}, u32[]{:S(2)}) %collective-permute-start.38) | collective-permute-done | bytes 196640 | tf_op jit(solution)/shard_map/ppermute | solution.py:94
  311.7 14.7 %collective-permute-done.39 = bf16[2,64,1536]{2,1,0:T(8,128)(2,1)S(1)} collective-permute-done((bf16[2,64,1536]{2,1,0:T(8,128)(2,1)S(1)}, bf16[2,64,1536]{2,1,0:T(8,128)(2,1)S(1)}, u32[]{:S(2)}, u32[]{:S(2)}) %collective-permute-start.39) | collective-permute-done | bytes 393248 | tf_op jit(solution)/shard_map/ppermute | solution.py:94
  329.0 16.3 %collective-permute-done.40 = bf16[4,64,1536]{2,1,0:T(8,128)(2,1)S(1)} collective-permute-done((bf16[4,64,1536]{2,1,0:T(8,128)(2,1)S(1)}, bf16[4,64,1536]{2,1,0:T(8,128)(2,1)S(1)}, u32[]{:S(2)}, u32[]{:S(2)}) %collective-permute-start.40) | collective-permute-done | bytes 786464 | tf_op jit(solution)/shard_map/ppermute | solution.py:94
  355.9 12.3 %fusion.20 = f32[2048,1024]{0,1:T(8,128)} fusion(bf16[1536,1024]{1,0:T(8,128)(2,1)S(1)} %copy-done.65, bf16[1024,1536]{1,0:T(8,128)(2,1)} %bitcast.256, bf16[1024,1536]{1,0:T(8,128)(2,1)} %bitcast.259), kind=kOutput, calls=%fused_computation.66 | convolution fusion | flops 6455033856 | bytes 17825792 | tf_op jit(solution)/shard_map/dot_general | solution.py:865
  368.3 27.4 %multiply_convert_fusion.1 = (bf16[2048,512]{0,1:T(8,128)(2,1)S(1)}, bf16[2048,512]{0,1:T(8,128)(2,1)S(1)}, f32[2048]{0:T(1024)S(1)}, bf16[2048,512]{0,1:T(8,128)(2,1)S(1)}) fusion(f32[2048,1024]{0,1:T(8,128)} %fusion.20, f32[2048]{0:T(1024)S(1)} %select_reduce_fusion, bf16[512,1536]{1,0:T(8,128)(2,1)S(1)} %copy-done.73, ...), kind=kOutput, calls=%fused_computation.24 | convolution fusion | flops 3253729280 | bytes 23085056 | tf_op jit(solution)/shard_map/dot_general | solution.py:46
  403.3 7.1 convolution_convert_fusion
  421.2 8.6 fusion.4
  471.5 6.0 collective-permute-done.53
  478.3 6.9 collective-permute-done.57
  487.2 18.2 %collective-permute-done.61 = bf16[4,64,1664]{2,1,0:T(8,128)(2,1)S(1)} collective-permute-done((bf16[4,64,1664]{2,1,0:T(8,128)(2,1)S(1)}, bf16[4,64,1664]{2,1,0:T(8,128)(2,1)S(1)}, u32[]{:S(2)}, u32[]{:S(2)}) %collective-permute-start.61) | collective-permute-done | bytes 852000 | tf_op jit(solution)/shard_map/ppermute | solution.py:94
  505.6 24.8 %collective-permute-done.50 = bf16[2,64,1536]{2,1,0:T(8,128)(2,1)S(1)} collective-permute-done((bf16[2,64,1536]{2,1,0:T(8,128)(2,1)S(1)}, bf16[2,64,1536]{2,1,0:T(8,128)(2,1)S(1)}, u32[]{:S(2)}, u32[]{:S(2)}) %collective-permute-start.50) | collective-permute-done | bytes 393248 | tf_op jit(solution)/shard_map/ppermute | solution.py:94
  532.1 18.0 %collective-permute-done.51 = bf16[1,64,1536]{2,1,0:T(8,128)(2,1)S(1)} collective-permute-done((bf16[1,64,1536]{2,1,0:T(8,128)(2,1)S(1)}, bf16[1,64,1536]{2,1,0:T(8,128)(2,1)S(1)}, u32[]{:S(2)}, u32[]{:S(2)}) %collective-permute-start.51) | collective-permute-done | bytes 196640 | tf_op jit(solution)/shard_map/ppermute | solution.py:94
  551.3 9.9 %collective-permute-done.59 = bf16[1,64,1664]{2,1,0:T(8,128)(2,1)S(1)} collective-permute-done((bf16[1,64,1664]{2,1,0:T(8,128)(2,1)S(1)}, bf16[1,64,1664]{2,1,0:T(8,128)(2,1)S(1)}, u32[]{:S(2)}, u32[]{:S(2)}) %collective-permute-start.59) | collective-permute-done | bytes 213024 | tf_op jit(solution)/shard_map/ppermute | solution.py:94
  608.2 7.4 collective-permute-done.65
  619.3 7.5 collective-permute-done.75
  645.2 6.1 collective-permute-done.77
  678.1 7.0 fusion.11
  698.1 30.1 %collective-permute-done.94 = bf16[768,1024]{1,0:T(8,128)(2,1)} collective-permute-done((bf16[768,1024]{1,0:T(8,128)(2,1)}, bf16[768,1024]{1,0:T(8,128)(2,1)}, u32[]{:S(2)}, u32[]{:S(2)}) %collective-permute-start.94) | collective-permute-done | bytes 1572896 | tf_op jit(solution)/shard_map/ppermute | solution.py:94
  737.4 6.3 copy.311
  743.7 5.8 add.639
  769.8 14.7 %collective-permute-done.90 = bf16[2,2,2,1,1,48,1408]{6,5,4,3,2,1,0:T(8,128)(2,1)} collective-permute-done((bf16[2,2,2,1,1,48,1408]{6,5,4,3,2,1,0:T(8,128)(2,1)}, bf16[2,2,2,1,1,48,1408]{6,5,4,3,2,1,0:T(8,128)(2,1)}, u32[]{:S(2)}, u32[]{:S(2)}) %collective-permute-start.90) | collective-permute-done | bytes 1081376 | tf_op jit(solution)/shard_map/ppermute | solution.py:94
  813.7 8.3 collective-permute-done.92
  828.2 12.1 %collective-permute-done.93 = bf16[1,1,1,1,1,48,1408]{5,6,4,3,2,1,0:T(8,128)(2,1)S(1)} collective-permute-done((bf16[1,1,1,1,1,48,1408]{5,6,4,3,2,1,0:T(8,128)(2,1)S(1)}, bf16[1,1,1,1,1,48,1408]{5,6,4,3,2,1,0:T(8,128)(2,1)S(1)}, u32[]{:S(2)}, u32[]{:S(2)}) %collective-permute-start.93) | collective-permute-done | bytes 135200 | tf_op jit(solution)/shard_map/ppermute | solution.py:94
  845.6 33.8 %reduce-scatter.4.cloned.1.call-done = bf16[48,1536]{1,0:T(8,128)(2,1)} async-done(((bf16[1536,1536]{1,0:T(8,128)(2,1)}), bf16[48,1536]{1,0:T(8,128)(2,1)}) %reduce-scatter.4.cloned.1.call-update) | async-done | bytes 147472 | tf_op jit(solution)/shard_map/reduce_scatter | solution.py:910
  927.0 5.7 add_multiply_fusion
  (831 shorter events, 466.4 us)
Async XLA Ops:
  7.2 282.5 %all-gather.4.cloned.1.call-start = ((), (), s32[]{:S(2)}) async-start(), calls=%async_computation.3 | async-start | bytes 4866048 | tf_op jit(solution)/shard_map/all_gather | solution.py:772
  8.9 428.2 %all-gather.6.cloned.1.call-start = ((), (), s32[]{:S(2)}) async-start(), calls=%async_computation.4 | async-start | bytes 6488064 | tf_op jit(solution)/shard_map/all_gather | solution.py:773
  10.7 435.9 %all-gather.8.cloned.1.call-start = ((), (), s32[]{:S(2)}) async-start(), calls=%async_computation.5 | async-start | bytes 3244032 | tf_op jit(solution)/shard_map/all_gather | solution.py:774
  22.1 110.4 %collective-permute-start.46 = (bf16[1,768,1024]{2,1,0:T(8,128)(2,1)}, bf16[1,768,1024]{2,1,0:T(8,128)(2,1)}, u32[]{:S(2)}, u32[]{:S(2)}) collective-permute-start(bf16[1,768,1024]{2,1,0:T(8,128)(2,1)} %convert_element_type.206), channel_id=1, source_target_pairs={{0,16},{16,0},{1,17},{17,1},{2,18},{18,2},{3,19},{19,3},{4,20},{20... | collective-permute-start | bytes 4718600 | tf_op jit(solution)/shard_map/ppermute | solution.py:94
  26.3 103.6 %collective-permute-start.47 = (bf16[1,256,1536]{2,1,0:T(8,128)(2,1)}, bf16[1,256,1536]{2,1,0:T(8,128)(2,1)}, u32[]{:S(2)}, u32[]{:S(2)}) collective-permute-start(bf16[1,256,1536]{2,1,0:T(8,128)(2,1)} %convert_element_type.211), channel_id=1, source_target_pairs={{0,16},{16,0},{1,17},{17,1},{2,18},{18,2},{3,19},{19,3},{4,20},{20... | collective-permute-start | bytes 2359304 | tf_op jit(solution)/shard_map/ppermute | solution.py:94
  27.2 737.1 %reduce-scatter.8.cloned.1.call-start = ((), (), s32[]{:S(2)}) async-start(), calls=%async_computation.8 | async-start | bytes 3244032 | tf_op jit(solution)/shard_map/reduce_scatter | solution.py:910
  53.0 48.5 %collective-permute-start.2 = (bf16[1,2,2,1,1,48,1408]{6,5,2,1,4,3,0:T(8,128)(2,1)S(1)}, bf16[1,2,2,1,1,48,1408]{6,5,2,1,4,3,0:T(8,128)(2,1)S(1)}, u32[]{:S(2)}, u32[]{:S(2)}) collective-permute-start(bf16[1,2,2,1,1,48,1408]{6,5,2,1,4,3,0:T(8,128)(2,1)S(1)} %broadcast_select_fusion.9), channel_id=1, source_target_pairs={{0,16},{16,0},{1,17},{17,1},{2,18},{18,2},{3,19},{19,3},{4,20},{20... | collective-permute-start | bytes 1622024 | tf_op jit(solution)/shard_map/ppermute | solution.py:94
  56.9 66.4 %collective-permute-start.8 = (bf16[1,2,2,2,1,48,1280]{6,5,3,2,1,4,0:T(8,128)(2,1)S(1)}, bf16[1,2,2,2,1,48,1280]{6,5,3,2,1,4,0:T(8,128)(2,1)S(1)}, u32[]{:S(2)}, u32[]{:S(2)}) collective-permute-start(bf16[1,2,2,2,1,48,1280]{6,5,3,2,1,4,0:T(8,128)(2,1)S(1)} %broadcast_select_fusion.7), channel_id=1, source_target_pairs={{0,16},{16,0},{1,17},{17,1},{2,18},{18,2},{3,19},{19,3},{4,20},{20... | collective-permute-start | bytes 2949128 | tf_op jit(solution)/shard_map/ppermute | solution.py:94
  101.7 27.9 %collective-permute-start.3 = (bf16[2,2,2,1,1,48,1408]{6,5,2,1,0,4,3:T(8,128)(2,1)S(1)}, bf16[2,2,2,1,1,48,1408]{6,5,2,1,0,4,3:T(8,128)(2,1)S(1)}, u32[]{:S(2)}, u32[]{:S(2)}) collective-permute-start(bf16[2,2,2,1,1,48,1408]{6,5,2,1,0,4,3:T(8,128)(2,1)S(1)} %broadcast_select_fusion.5), channel_id=1, source_target_pairs={{0,2},{1,3},{2,0},{3,1},{4,6},{5,7},{6,4},{7,5},{8,10},{9,11},{10,... | collective-permute-start | bytes 3244040 | tf_op jit(solution)/shard_map/ppermute | solution.py:94
  148.7 49.1 %collective-permute-start.30 = (bf16[1,64,1664]{2,1,0:T(8,128)(2,1)}, bf16[1,64,1664]{2,1,0:T(8,128)(2,1)S(1)}, u32[]{:S(2)}, u32[]{:S(2)}) collective-permute-start(bf16[1,64,1664]{2,1,0:T(8,128)(2,1)} %get-tuple-element.378), channel_id=1, source_target_pairs={{0,8},{1,9},{2,10},{3,11},{4,12},{5,13},{6,14},{7,15},{8,0},{9,1},... | collective-permute-start | bytes 638984 | tf_op jit(solution)/shard_map/ppermute | solution.py:94
  149.1 51.1 %collective-permute-start.34 = (bf16[1,64,1664]{2,1,0:T(8,128)(2,1)}, bf16[1,64,1664]{2,1,0:T(8,128)(2,1)S(1)}, u32[]{:S(2)}, u32[]{:S(2)}) collective-permute-start(bf16[1,64,1664]{2,1,0:T(8,128)(2,1)} %get-tuple-element.379), channel_id=1, source_target_pairs={{0,2},{1,3},{2,0},{3,1},{4,6},{5,7},{6,4},{7,5},{8,10},{9,11},{10,... | collective-permute-start | bytes 638984 | tf_op jit(solution)/shard_map/ppermute | solution.py:94
  150.7 28.4 %collective-permute-start.20 = (bf16[1,128,256]{2,1,0:T(8,128)(2,1)S(1)}, bf16[1,128,256]{2,1,0:T(8,128)(2,1)S(1)}, u32[]{:S(2)}, u32[]{:S(2)}) collective-permute-start(bf16[1,128,256]{2,1,0:T(8,128)(2,1)S(1)} %get-tuple-element.395), channel_id=1, source_target_pairs={{0,8},{1,9},{2,10},{3,11},{4,12},{5,13},{6,14},{7,15},{8,0},{9,1},... | collective-permute-start | bytes 196616 | tf_op jit(solution)/shard_map/ppermute | solution.py:94
  153.2 27.3 %collective-permute-start.15 = (bf16[1,128,256]{2,1,0:T(8,128)(2,1)}, bf16[1,128,256]{2,1,0:T(8,128)(2,1)S(1)}, u32[]{:S(2)}, u32[]{:S(2)}) collective-permute-start(bf16[1,128,256]{2,1,0:T(8,128)(2,1)} %get-tuple-element.402), channel_id=1, source_target_pairs={{0,8},{1,9},{2,10},{3,11},{4,12},{5,13},{6,14},{7,15},{8,0},{9,1},... | collective-permute-start | bytes 196616 | tf_op jit(solution)/shard_map/ppermute | solution.py:94
  228.7 29.2 %collective-permute-start.29 = (bf16[16,128,256]{2,1,0:T(8,128)(2,1)S(1)}, bf16[16,128,256]{2,1,0:T(8,128)(2,1)S(1)}, u32[]{:S(2)}, u32[]{:S(2)}) collective-permute-start(bf16[16,128,256]{2,1,0:T(8,128)(2,1)S(1)} %get-tuple-element.368), channel_id=1, source_target_pairs={{0,1},{1,0},{2,3},{3,2},{4,5},{5,4},{6,7},{7,6},{8,9},{9,8},{10,11... | collective-permute-start | bytes 3145736 | tf_op jit(solution)/shard_map/ppermute | solution.py:94
  231.3 33.3 %collective-permute-start.24 = (bf16[16,128,256]{2,1,0:T(8,128)(2,1)}, bf16[16,128,256]{2,1,0:T(8,128)(2,1)}, u32[]{:S(2)}, u32[]{:S(2)}) collective-permute-start(bf16[16,128,256]{2,1,0:T(8,128)(2,1)} %get-tuple-element.370), channel_id=1, source_target_pairs={{0,1},{1,0},{2,3},{3,2},{4,5},{5,4},{6,7},{7,6},{8,9},{9,8},{10,11... | collective-permute-start | bytes 3145736 | tf_op jit(solution)/shard_map/ppermute | solution.py:94
  232.2 28.9 %collective-permute-start.19 = (bf16[16,128,256]{2,1,0:T(8,128)(2,1)}, bf16[16,128,256]{2,1,0:T(8,128)(2,1)}, u32[]{:S(2)}, u32[]{:S(2)}) collective-permute-start(bf16[16,128,256]{2,1,0:T(8,128)(2,1)} %get-tuple-element.372), channel_id=1, source_target_pairs={{0,1},{1,0},{2,3},{3,2},{4,5},{5,4},{6,7},{7,6},{8,9},{9,8},{10,11... | collective-permute-start | bytes 3145736 | tf_op jit(solution)/shard_map/ppermute | solution.py:94
  402.5 39.6 %collective-permute-start.48 = (bf16[8,64,1536]{2,1,0:T(8,128)(2,1)}, bf16[8,64,1536]{2,1,0:T(8,128)(2,1)}, u32[]{:S(2)}, u32[]{:S(2)}) collective-permute-start(bf16[8,64,1536]{2,1,0:T(8,128)(2,1)} %bitcast.42), channel_id=1, source_target_pairs={{0,1},{1,0},{2,3},{3,2},{4,5},{5,4},{6,7},{7,6},{8,9},{9,8},{10,11... | collective-permute-start | bytes 4718600 | tf_op jit(solution)/shard_map/ppermute | solution.py:94
  402.7 51.9 %collective-permute-start.52 = (bf16[8,64,1536]{2,1,0:T(8,128)(2,1)}, bf16[8,64,1536]{2,1,0:T(8,128)(2,1)}, u32[]{:S(2)}, u32[]{:S(2)}) collective-permute-start(bf16[8,64,1536]{2,1,0:T(8,128)(2,1)} %bitcast.45), channel_id=1, source_target_pairs={{0,1},{1,0},{2,3},{3,2},{4,5},{5,4},{6,7},{7,6},{8,9},{9,8},{10,11... | collective-permute-start | bytes 4718600 | tf_op jit(solution)/shard_map/ppermute | solution.py:94
  417.1 45.4 %collective-permute-start.56 = (bf16[8,64,1664]{2,1,0:T(8,128)(2,1)}, bf16[8,64,1664]{2,1,0:T(8,128)(2,1)}, u32[]{:S(2)}, u32[]{:S(2)}) collective-permute-start(bf16[8,64,1664]{2,1,0:T(8,128)(2,1)} %bitcast.246), channel_id=1, source_target_pairs={{0,1},{1,0},{2,3},{3,2},{4,5},{5,4},{6,7},{7,6},{8,9},{9,8},{10,11... | collective-permute-start | bytes 5111816 | tf_op jit(solution)/shard_map/ppermute | solution.py:94
  420.9 45.1 %collective-permute-start.60 = (bf16[8,64,1664]{2,1,0:T(8,128)(2,1)}, bf16[8,64,1664]{2,1,0:T(8,128)(2,1)}, u32[]{:S(2)}, u32[]{:S(2)}) collective-permute-start(bf16[8,64,1664]{2,1,0:T(8,128)(2,1)} %bitcast.245), channel_id=1, source_target_pairs={{0,1},{1,0},{2,3},{3,2},{4,5},{5,4},{6,7},{7,6},{8,9},{9,8},{10,11... | collective-permute-start | bytes 5111816 | tf_op jit(solution)/shard_map/ppermute | solution.py:94
  454.3 340.0 %reduce-scatter.6.cloned.1.call-start = ((), (), s32[]{:S(2)}) async-start(), calls=%async_computation.7 | async-start | bytes 6488064 | tf_op jit(solution)/shard_map/reduce_scatter | solution.py:910
  468.1 37.3 %collective-permute-start.61 = (bf16[4,64,1664]{2,1,0:T(8,128)(2,1)S(1)}, bf16[4,64,1664]{2,1,0:T(8,128)(2,1)S(1)}, u32[]{:S(2)}, u32[]{:S(2)}) collective-permute-start(bf16[4,64,1664]{2,1,0:T(8,128)(2,1)S(1)} %slice.530), channel_id=1, source_target_pairs={{0,4},{1,5},{2,6},{3,7},{4,0},{5,1},{6,2},{7,3},{8,12},{9,13},{10,... | collective-permute-start | bytes 2555912 | tf_op jit(solution)/shard_map/ppermute | solution.py:94
  471.5 59.0 %collective-permute-start.50 = (bf16[2,64,1536]{2,1,0:T(8,128)(2,1)S(1)}, bf16[2,64,1536]{2,1,0:T(8,128)(2,1)S(1)}, u32[]{:S(2)}, u32[]{:S(2)}) collective-permute-start(bf16[2,64,1536]{2,1,0:T(8,128)(2,1)S(1)} %slice.504), channel_id=1, source_target_pairs={{0,4},{1,5},{2,6},{3,7},{4,0},{5,1},{6,2},{7,3},{8,12},{9,13},{10,... | collective-permute-start | bytes 1179656 | tf_op jit(solution)/shard_map/ppermute | solution.py:94
  477.7 53.2 %collective-permute-start.54 = (bf16[2,64,1536]{2,1,0:T(8,128)(2,1)S(1)}, bf16[2,64,1536]{2,1,0:T(8,128)(2,1)S(1)}, u32[]{:S(2)}, u32[]{:S(2)}) collective-permute-start(bf16[2,64,1536]{2,1,0:T(8,128)(2,1)S(1)} %slice.512), channel_id=1, source_target_pairs={{0,8},{1,9},{2,10},{3,11},{4,12},{5,13},{6,14},{7,15},{8,0},{9,1},... | collective-permute-start | bytes 1179656 | tf_op jit(solution)/shard_map/ppermute | solution.py:94
  485.4 64.7 %collective-permute-start.58 = (bf16[2,64,1664]{2,1,0:T(8,128)(2,1)S(1)}, bf16[2,64,1664]{2,1,0:T(8,128)(2,1)S(1)}, u32[]{:S(2)}, u32[]{:S(2)}) collective-permute-start(bf16[2,64,1664]{2,1,0:T(8,128)(2,1)S(1)} %slice.524), channel_id=1, source_target_pairs={{0,4},{1,5},{2,6},{3,7},{4,0},{5,1},{6,2},{7,3},{8,12},{9,13},{10,... | collective-permute-start | bytes 1277960 | tf_op jit(solution)/shard_map/ppermute | solution.py:94
  505.5 44.9 %collective-permute-start.62 = (bf16[2,64,1664]{2,1,0:T(8,128)(2,1)S(1)}, bf16[2,64,1664]{2,1,0:T(8,128)(2,1)S(1)}, u32[]{:S(2)}, u32[]{:S(2)}) collective-permute-start(bf16[2,64,1664]{2,1,0:T(8,128)(2,1)S(1)} %slice.532), channel_id=1, source_target_pairs={{0,8},{1,9},{2,10},{3,11},{4,12},{5,13},{6,14},{7,15},{8,0},{9,1},... | collective-permute-start | bytes 1277960 | tf_op jit(solution)/shard_map/ppermute | solution.py:94
  575.6 113.6 %collective-permute-start.95 = (bf16[256,1536]{1,0:T(8,128)(2,1)}, bf16[256,1536]{1,0:T(8,128)(2,1)}, u32[]{:S(2)}, u32[]{:S(2)}) collective-permute-start(bf16[256,1536]{1,0:T(8,128)(2,1)} %dynamic-slice_convert_fusion.1), channel_id=1, source_target_pairs={{0,16},{16,0},{1,17},{17,1},{2,18},{18,2},{3,19},{19,3},{4,20},{20... | collective-permute-start | bytes 2359304 | tf_op jit(solution)/shard_map/ppermute | solution.py:94
  593.5 285.9 %reduce-scatter.4.cloned.1.call-start = ((), (), s32[]{:S(2)}) async-start(), calls=%async_computation.6 | async-start | bytes 4866048 | tf_op jit(solution)/shard_map/reduce_scatter | solution.py:910
  664.3 28.8 %collective-permute-start.84 = (bf16[2,2,2,2,1,48,1280]{6,5,4,3,2,1,0:T(8,128)(2,1)}, bf16[2,2,2,2,1,48,1280]{6,5,4,3,2,1,0:T(8,128)(2,1)}, u32[]{:S(2)}, u32[]{:S(2)}) collective-permute-start(bf16[2,2,2,2,1,48,1280]{6,5,4,3,2,1,0:T(8,128)(2,1)} %constant_dynamic-slice_fusion.8), channel_id=1, source_target_pairs={{0,1},{1,0},{2,3},{3,2},{4,5},{5,4},{6,7},{7,6},{8,9},{9,8},{10,11... | collective-permute-start | bytes 5898248 | tf_op jit(solution)/shard_map/ppermute | solution.py:94
  675.6 61.7 %collective-permute-start.89 = (bf16[2,2,2,2,1,48,1408]{6,5,4,3,2,1,0:T(8,128)(2,1)}, bf16[2,2,2,2,1,48,1408]{6,5,4,3,2,1,0:T(8,128)(2,1)}, u32[]{:S(2)}, u32[]{:S(2)}) collective-permute-start(bf16[2,2,2,2,1,48,1408]{6,5,4,3,2,1,0:T(8,128)(2,1)} %get-tuple-element.360), channel_id=1, source_target_pairs={{0,1},{1,0},{2,3},{3,2},{4,5},{5,4},{6,7},{7,6},{8,9},{9,8},{10,11... | collective-permute-start | bytes 6488072 | tf_op jit(solution)/shard_map/ppermute | solution.py:94
  689.1 39.1 %collective-permute-start.94 = (bf16[768,1024]{1,0:T(8,128)(2,1)}, bf16[768,1024]{1,0:T(8,128)(2,1)}, u32[]{:S(2)}, u32[]{:S(2)}) collective-permute-start(bf16[768,1024]{1,0:T(8,128)(2,1)} %dynamic-slice_convert_fusion), channel_id=1, source_target_pairs={{0,16},{16,0},{1,17},{17,1},{2,18},{18,2},{3,19},{19,3},{4,20},{20... | collective-permute-start | bytes 4718600 | tf_op jit(solution)/shard_map/ppermute | solution.py:94
  696.1 70.5 %collective-permute-start.85 = (bf16[1,2,2,2,1,48,1280]{6,5,4,3,2,1,0:T(8,128)(2,1)}, bf16[1,2,2,2,1,48,1280]{6,5,4,3,2,1,0:T(8,128)(2,1)}, u32[]{:S(2)}, u32[]{:S(2)}) collective-permute-start(bf16[1,2,2,2,1,48,1280]{6,5,4,3,2,1,0:T(8,128)(2,1)} %constant_dynamic-slice_fusion.7), channel_id=1, source_target_pairs={{0,16},{16,0},{1,17},{17,1},{2,18},{18,2},{3,19},{19,3},{4,20},{20... | collective-permute-start | bytes 2949128 | tf_op jit(solution)/shard_map/ppermute | solution.py:94
  (229 other events, 3830.1 us)
Sparse Core Ops, SparseCore 0:
  11.5 80.0 all-gather.3
  95.1 84.3 all-gather.5
  182.9 68.5 all-gather.7
  454.5 120.5 reduce-scatter.7
  593.5 120.8 reduce-scatter.5
  764.4 114.9 reduce-scatter.3

commit v2 on v1

--- a/solution.py
+++ b/solution.py
@@ -1,3 +1,5 @@
+import functools
+
 import functools
 
 import jax
@@ -80,6 +82,8 @@
     return (first_new, second_new, change)
 
 
+WAVES_KV = (0, 0, 1, 1)
+WAVES_COL = None
 WIDTH_ROWS = 512
 
 
@@ -92,6 +96,10 @@
     name, bit = step
     size = lax.axis_size(name)
     return lax.ppermute(values, name, [(i, i ^ bit) for i in range(size)])
+
+
+def after(values, *earlier):
+    return lax.optimization_barrier((values, earlier))[0]
 
 
 def own_bit(step):
@@ -110,26 +118,59 @@
     return (blk_bits, blk_bits[-2:-1] + blk_bits[:-2] + blk_bits[-1:])
 
 
-def lockstep(pieces, orders, act, backwards=False):
+def lockstep(pieces, orders, act, backwards=False, waves=None, beside=None):
     count = len(orders[0])
-    for turn in reversed(range(count)) if backwards else range(count):
-        pieces = [act(piece, order[turn]) for piece, order in zip(pieces, orders)]
+    pieces = list(pieces)
+    for turn, at in enumerate(reversed(range(count)) if backwards else range(count)):
+        before = list(pieces)
+        for place, order in enumerate(orders):
+            piece = pieces[place]
+            if waves is not None and waves[place] > 0:
+                ahead = [p for p, wave in zip(pieces, waves) if wave == waves[place] - 1]
+                piece = after(piece, ahead)
+            pieces[place] = act(piece, order[at])
+        if beside is not None:
+            work, results = beside
+            if work is None:
+                pieces = lax.optimization_barrier(pieces)
+            elif turn in work:
+                found = work[turn](before)
+                pieces, found = lax.optimization_barrier((pieces, found))
+                results.append(found)
     return pieces
 
 
-def gather_relative(pieces, orders):
+def gather_relative(pieces, orders, waves=None, beside=None):
     def act(piece, step):
-        return jnp.concatenate([piece, swap(piece, step)], axis=0)
-
-    return lockstep([piece[None] for piece in pieces], orders, act)
-
-
-def scatter_relative(pieces, orders):
+        piece = piece[0] if len(piece) == 1 else jnp.concatenate(piece, axis=0)
+        return (piece, swap(piece, step))
+
+    return lockstep([(piece[None],) for piece in pieces], orders, act, False, waves, beside)
+
+
+def scatter_relative(pieces, orders, waves=None, beside=None):
     def act(piece, step):
-        half = piece.shape[0] // 2
-        return piece[:half] + swap(piece[half:], step)
-
-    return [piece[0] for piece in lockstep(pieces, orders, act, backwards=True)]
+        kept, sent = piece
+        total = kept + swap(sent, step)
+        half = total.shape[0] // 2
+        return (total[:half], total[half:]) if half else total
+
+    return [piece[0] for piece in lockstep(pieces, orders, act, True, waves, beside)]
+
+
+def transpose_blk(values):
+    places = axis_bits("blk")
+    shape = values.shape
+    values = values.reshape((2,) * len(places) + shape[1:])
+    for place, step in enumerate(places):
+        bit = own_bit(step)
+        mine = lax.dynamic_slice_in_dim(values, bit, 1, place)
+        theirs = lax.dynamic_slice_in_dim(values, 1 - bit, 1, place)
+        index = [1] * values.ndim
+        index[place] = 2
+        here = lax.broadcasted_iota(jnp.int32, index, place) == bit
+        values = jnp.where(here, mine, swap(theirs, step))
+    return values.reshape(shape)
 
 
 def gather_rows(pieces, orders):
@@ -144,7 +185,8 @@
 
     wide = [piece.reshape((1,) * len(places) + piece.shape) for piece in pieces]
     return [
-        full.reshape(-1, full.shape[-1]) for full in lockstep(wide, orders, act)
+        full.reshape(-1, full.shape[-1])
+        for full in lockstep(wide, orders, act, beside=(None, []))
     ]
 
 
@@ -164,14 +206,42 @@
         for piece in pieces
     ]
     return [
-        own.reshape(own.shape[-2:]) for own in lockstep(wide, orders, act, backwards=True)
+        own.reshape(own.shape[-2:])
+        for own in lockstep(wide, orders, act, True)
     ]
 
 
+def swap_both(values, first, second):
+    sizes = {name: lax.axis_size(name) for name in ("head", "blk")}
+    flip = {"head": 0, "blk": 0}
+    for name, bit in (first, second):
+        flip[name] ^= bit
+    pairs = [
+        (h * sizes["blk"] + b, (h ^ flip["head"]) * sizes["blk"] + (b ^ flip["blk"]))
+        for h in range(sizes["head"])
+        for b in range(sizes["blk"])
+    ]
+    return lax.ppermute(values, ("head", "blk"), pairs)
+
+
 def sum_everywhere(values):
-    for step in axis_bits("blk") + axis_bits("head"):
+    blk_bits = axis_bits("blk")
+    steps = blk_bits[:-1] + axis_bits("head")
+    while len(steps) > 1:
+        first, second, steps = steps[0], steps[1], steps[2:]
+        values = (values + swap(values, first)) + (
+            swap(values, second) + swap_both(values, first, second)
+        )
+    for step in steps + blk_bits[-1:]:
         values = values + swap(values, step)
     return values
+
+
+def blk_blocks(order):
+    offsets = [0]
+    for _, bit in order:
+        offsets = offsets + [offset ^ bit for offset in offsets]
+    return lax.axis_index("blk") ^ jnp.array(offsets, jnp.int32)
 
 
 def block_devices(order):
@@ -199,11 +269,16 @@
     return jnp.where(key_pos <= limit, scores, masked_score)
 
 
-def attend_kernel(q_ref, kv_ref, pos_ref, limit_ref, out_ref, low_ref, log_ref):
+def join(low_ref, high_ref, start):
+    parts = [ref[:, :, start : start + HEAD_DIM].reshape(-1, HEAD_DIM) for ref in (low_ref, high_ref)]
+    return jnp.concatenate(parts, axis=0)
+
+
+def attend_kernel(q_ref, kv0_ref, kv1_ref, pos_ref, limit_ref, out_ref, low_ref, log_ref):
     stretch = q_ref.shape[0]
     query = stack_heads(q_ref[...])
-    keys = kv_ref[:, :, :HEAD_DIM].reshape(-1, HEAD_DIM)
-    values = kv_ref[:, :, HEAD_DIM:].reshape(-1, HEAD_DIM)
+    keys = join(kv0_ref, kv1_ref, 0)
+    values = join(kv0_ref, kv1_ref, HEAD_DIM)
     limit = jnp.concatenate([limit_ref[...]] * GROUP, axis=0)
     scores = group_scores(query, keys, limit, pos_ref[...])
     top = jnp.max(scores, axis=1, keepdims=True)
@@ -220,14 +295,24 @@
 
 
 def attend_back_kernel(
-    q_ref, kv_ref, pos_ref, limit_ref, grad_ref, out_ref, log_ref, dq_ref, dkv_ref
+    q_ref,
+    kv0_ref,
+    kv1_ref,
+    pos_ref,
+    limit_ref,
+    grad_ref,
+    out_ref,
+    log_ref,
+    dq_ref,
+    dkv0_ref,
+    dkv1_ref,
 ):
     stretch = q_ref.shape[0]
     scale = HEAD_DIM ** (-0.5)
     low_type = jnp.bfloat16
     query = stack_heads(q_ref[...])
-    keys = kv_ref[:, :, :HEAD_DIM].reshape(-1, HEAD_DIM)
-    values = kv_ref[:, :, HEAD_DIM:].reshape(-1, HEAD_DIM)
+    keys = join(kv0_ref, kv1_ref, 0)
+    values = join(kv0_ref, kv1_ref, HEAD_DIM)
     grad = stack_heads(grad_ref[...])
     row_dot = jnp.sum(
         grad.astype(jnp.float32) * stack_heads(out_ref[...]), axis=1, keepdims=True
@@ -243,67 +328,269 @@
     dq = jnp.dot(grad_scores, keys, preferred_element_type=jnp.float32) * scale
     dk = outer_dot(grad_scores, query) * scale
     dv = outer_dot(weights_low, grad)
-    block = dkv_ref.shape[:2] + (HEAD_DIM,)
-    dkv_ref[:, :, :HEAD_DIM] = dk.astype(low_type).reshape(block)
-    dkv_ref[:, :, HEAD_DIM:] = dv.astype(low_type).reshape(block)
+    block = dkv0_ref.shape[:2] + (HEAD_DIM,)
+    half = dk.shape[0] // 2
+    for start, ref in ((0, dkv0_ref), (half, dkv1_ref)):
+        ref[:, :, :HEAD_DIM] = dk[start : start + half].astype(low_type).reshape(block)
+        ref[:, :, HEAD_DIM:] = dv[start : start + half].astype(low_type).reshape(block)
     for i in range(GROUP):
         part = dq[i * stretch : (i + 1) * stretch]
         dq_ref[:, i * HEAD_DIM : (i + 1) * HEAD_DIM] = part.astype(low_type)
 
 
 def attention_specs(stretch, devices):
-    wide = pl.BlockSpec((stretch, GROUP * HEAD_DIM), lambda s: (s, 0))
-    pair = pl.BlockSpec((devices, stretch, 2 * HEAD_DIM), lambda s: (0, s, 0))
-    pos = pl.BlockSpec((1, devices * stretch), lambda s: (0, 0))
-    limit = pl.BlockSpec((stretch, 1), lambda s: (s, 0))
-    log = pl.BlockSpec((1, GROUP * stretch, 1), lambda s: (s, 0, 0))
+    wide = pl.BlockSpec((stretch, GROUP * HEAD_DIM), lambda g: (0, g))
+    pair = pl.BlockSpec((devices // 2, stretch, 2 * HEAD_DIM), lambda g: (0, 0, g))
+    pos = pl.BlockSpec((1, devices * stretch), lambda g: (0, 0))
+    limit = pl.BlockSpec((stretch, 1), lambda g: (0, 0))
+    log = pl.BlockSpec((1, GROUP * stretch, 1), lambda g: (g, 0, 0))
     return wide, pair, pos, limit, log
 
 
-def attention_cost(seqs, stretch, devices, matmuls):
-    scores = seqs * GROUP * stretch * devices * stretch
+def attention_cost(groups, stretch, devices, matmuls):
+    scores = groups * GROUP * stretch * devices * stretch
     return pl.CostEstimate(
         flops=2 * matmuls * scores * HEAD_DIM,
-        bytes_accessed=devices * seqs * stretch * 2 * HEAD_DIM * 2,
+        bytes_accessed=devices * groups * stretch * 2 * HEAD_DIM * 2,
         transcendentals=scores,
     )
 
 
-def attend(query, pair, key_pos, limit, seqs, stretch):
-    devices = pair.shape[0]
+def attend(query, pair, key_pos, limit):
+    stretch = query.shape[0]
+    groups = query.shape[1] // (GROUP * HEAD_DIM)
+    devices = 2 * pair[0].shape[0]
     wide, kv, pos, lim, log = attention_specs(stretch, devices)
     return pl.pallas_call(
         attend_kernel,
-        grid=(seqs,),
-        in_specs=[wide, kv, pos, lim],
+        grid=(groups,),
+        in_specs=[wide, kv, kv, pos, lim],
         out_specs=[wide, wide, log],
         out_shape=[
             jax.ShapeDtypeStruct(query.shape, jnp.float32),
             jax.ShapeDtypeStruct(query.shape, jnp.bfloat16),
-            jax.ShapeDtypeStruct((seqs, GROUP * stretch, 1), jnp.float32),
+            jax.ShapeDtypeStruct((groups, GROUP * stretch, 1), jnp.float32),
         ],
         compiler_params=pltpu.CompilerParams(vmem_limit_bytes=48 << 20),
-        cost_estimate=attention_cost(seqs, stretch, devices, 2),
+        cost_estimate=attention_cost(groups, stretch, devices, 2),
         name="attend",
-    )(query, pair, key_pos, limit)
-
-
-def attend_back(query, pair, key_pos, limit, grad, out, log_total, seqs, stretch):
-    devices = pair.shape[0]
+    )(query, *pair, key_pos, limit)
+
+
+def attend_back(query, pair, key_pos, limit, grad, out, log_total):
+    stretch = query.shape[0]
+    groups = query.shape[1] // (GROUP * HEAD_DIM)
+    devices = 2 * pair[0].shape[0]
     wide, kv, pos, lim, log = attention_specs(stretch, devices)
     return pl.pallas_call(
         attend_back_kernel,
-        grid=(seqs,),
-        in_specs=[wide, kv, pos, lim, wide, wide, log],
-        out_specs=[wide, kv],
+        grid=(groups,),
+        in_specs=[wide, kv, kv, pos, lim, wide, wide, log],
+        out_specs=[wide, kv, kv],
         out_shape=[
             jax.ShapeDtypeStruct(query.shape, jnp.bfloat16),
-            jax.ShapeDtypeStruct(pair.shape, jnp.bfloat16),
+            jax.ShapeDtypeStruct(pair[0].shape, jnp.bfloat16),
+            jax.ShapeDtypeStruct(pair[1].shape, jnp.bfloat16),
         ],
         compiler_params=pltpu.CompilerParams(vmem_limit_bytes=48 << 20),
-        cost_estimate=attention_cost(seqs, stretch, devices, 5),
+        cost_estimate=attention_cost(groups, stretch, devices, 5),
         name="attend_back",
-    )(query, pair, key_pos, limit, grad, out, log_total)
+    )(query, *pair, key_pos, limit, grad, out, log_total)
+
+
+def expert_kernel(blocks, place_ref, low_ref, high_ref, router_ref, own_ref, gu_ref, *refs):
+    pulled_refs, named_refs = refs[:blocks], refs[blocks : 2 * blocks]
+    out_low_ref, out_high_ref, act_ref, hid_ref = refs[2 * blocks :]
+    low_type = jnp.bfloat16
+    turn = pl.program_id(0)
+    half = pl.num_programs(0) // 2
+    first = jnp.where(turn < half, half + turn, turn - half) * blocks
+    values = jnp.where(turn < half, high_ref[...], low_ref[...])
+    width = values.shape[1]
+    stretch = values.shape[0] // blocks
+    chosen = jnp.concatenate([ref[...].reshape(stretch, -1) for ref in named_refs], axis=0) > 0
+    pulled = jnp.concatenate([ref[...].reshape(stretch, -1) for ref in pulled_refs], axis=0)
+    logits = jnp.dot(values, router_ref[...], preferred_element_type=jnp.float32)
+    logits = jnp.where(chosen, logits, masked_score)
+    raised = jnp.where(chosen, jnp.exp(logits - jnp.max(logits, axis=1, keepdims=True)), 0.0)
+    own = own_ref[...]
+    gate = jnp.sum(raised * own[:1], axis=1, keepdims=True) / jnp.sum(
+        raised, axis=1, keepdims=True
+    )
+    hidden = jnp.dot(values, gu_ref[...], preferred_element_type=jnp.float32)
+    shared = (hidden.shape[1] - 2 * EXPERT_FF) // 2
+
+    def mixed(gate_part, up_part, grad_act, start):
+        logistic = 1.0 / (1.0 + jnp.exp(-gate_part))
+        smooth = gate_part * logistic
+        slope = logistic * (1.0 + gate_part * (1.0 - logistic))
+        size = gate_part.shape[1]
+        hid_ref[:, start : start + size] = (grad_act * up_part * slope).astype(low_type)
+        hid_ref[:, start + size : start + 2 * size] = (grad_act * smooth).astype(low_type)
+        return (smooth * up_part).astype(low_type)
+
+    start = 2 * EXPERT_FF
+    act = mixed(
+        hidden[:, :EXPERT_FF], hidden[:, EXPERT_FF:start], gate * pulled[:, :EXPERT_FF], 0
+    ).astype(jnp.float32)
+    grad_gate = jnp.sum(pulled[:, :EXPERT_FF] * act, axis=1, keepdims=True)
+    shared_act = mixed(
+        hidden[:, start : start + shared],
+        hidden[:, start + shared :],
+        pulled[:, EXPERT_FF : EXPERT_FF + shared],
+        start,
+    )
+    rest = act_ref.shape[2] - EXPERT_FF - shared
+    acts = jnp.concatenate(
+        [
+            (gate * act).astype(low_type),
+            shared_act,
+            jnp.zeros((values.shape[0], rest), low_type),
+        ],
+        axis=1,
+    )
+    for block in range(blocks):
+        act_ref[place_ref[first + block]] = acts[block * stretch : (block + 1) * stretch]
+    out = back_dot(hid_ref[...], gu_ref[...]).astype(low_type)
+    high = grad_gate.astype(low_type).astype(jnp.float32)
+    lanes = (high * own[:1] + (grad_gate - high) * own[1:]).astype(low_type)
+
+    @pl.when(turn < half)
+    def _():
+        out_high_ref[:, :width] = out
+        out_high_ref[:, width:] = lanes
+
+    @pl.when(turn >= half)
+    def _():
+        out_low_ref[:, :width] = out
+        out_low_ref[:, width:] = lanes
+
+
+def run_expert(mid, pulled, early, router, own, gate_up, places, seq):
+    rows, width = mid[0].shape
+    devices, _, stretch, acts = pulled.shape
+    block = min(rows, 256)
+    blocks = block // stretch
+    half = rows // block
+    lanes = own.shape[1]
+    hid = gate_up.shape[1]
+    low_type = jnp.bfloat16
+
+    def fixed(shape):
+        return pl.BlockSpec(shape, lambda i, _: (0,) * len(shape))
+
+    def first(i):
+        return jnp.where(i < half, half + i, i - half) * blocks
+
+    def scattered(piece, size, column):
+        return pl.BlockSpec(
+            (1, 1, stretch, size), lambda i, place: (place[first(i) + piece], seq, 0, column)
+        )
+
+    def low_rows(size):
+        return pl.BlockSpec((block, size), lambda i, _: (jnp.maximum(i - half, 0), 0))
+
+    def high_rows(size):
+        return pl.BlockSpec((block, size), lambda i, _: (jnp.minimum(i, half - 1), 0))
+
+    return pl.pallas_call(
+        functools.partial(expert_kernel, blocks),
+        grid_spec=pltpu.PrefetchScalarGridSpec(
+            num_scalar_prefetch=1,
+            grid=(2 * half,),
+            in_specs=[
+                low_rows(width),
+                high_rows(width),
+                fixed(router.shape),
+                fixed(own.shape),
+                fixed(gate_up.shape),
+            ]
+            + [scattered(piece, acts, 0) for piece in range(blocks)]
+            + [scattered(piece, lanes, width // lanes) for piece in range(blocks)],
+            out_specs=[
+                low_rows(width + lanes),
+                high_rows(width + lanes),
+                fixed((devices, stretch, acts)),
+                pl.BlockSpec((block, hid), lambda i, _: (first(i) // blocks, 0)),
+            ],
+        ),
+        out_shape=[
+            jax.ShapeDtypeStruct((rows, width + lanes), low_type),
+            jax.ShapeDtypeStruct((rows, width + lanes), low_type),
+            jax.ShapeDtypeStruct((devices, stretch, acts), low_type),
+            jax.ShapeDtypeStruct((2 * rows, hid), low_type),
+        ],
+        compiler_params=pltpu.CompilerParams(vmem_limit_bytes=48 << 20),
+        cost_estimate=pl.CostEstimate(
+            flops=8 * rows * width * hid,
+            bytes_accessed=4 * rows * (2 * width + 3 * acts + hid),
+            transcendentals=2 * rows * acts,
+        ),
+        name="expert",
+    )(places, mid[0], mid[1], router, own, gate_up, *[pulled] * blocks, *[early] * blocks)
+
+
+def outer_experts_kernel(low0_ref, high0_ref, low1_ref, high1_ref, right0_ref, right1_ref, out_ref):
+    total = None
+    rows = low0_ref.shape[0]
+    for refs, right in (((low0_ref, high0_ref), right0_ref), ((low1_ref, high1_ref), right1_ref)):
+        for part, ref in enumerate(refs):
+            term = outer_dot(ref[...], right[part * rows : (part + 1) * rows])
+            total = term if total is None else total + term
+    out_ref[...] = total.astype(out_ref.dtype)
+
+
+def outer_experts(mid, hids):
+    rows, width = mid[0][0].shape
+    columns = hids[0].shape[1]
+    block = 256
+    lefts = pl.BlockSpec((rows, block), lambda i: (0, i))
+    rights = pl.BlockSpec((2 * rows, columns), lambda i: (0, 0))
+    return pl.pallas_call(
+        outer_experts_kernel,
+        grid=(width // block,),
+        in_specs=[lefts] * 4 + [rights] * 2,
+        out_specs=pl.BlockSpec((block, columns), lambda i: (i, 0)),
+        out_shape=jax.ShapeDtypeStruct((width, columns), jnp.bfloat16),
+        compiler_params=pltpu.CompilerParams(vmem_limit_bytes=48 << 20),
+        cost_estimate=pl.CostEstimate(
+            flops=8 * rows * width * columns,
+            bytes_accessed=8 * rows * (width + columns) + 2 * width * columns,
+            transcendentals=0,
+        ),
+        name="outer_experts",
+    )(*mid[0], *mid[1], *hids)
+
+
+def outer_acts_kernel(left0_ref, left1_ref, right_ref, out_ref):
+    total = None
+    for seq, ref in enumerate((left0_ref, left1_ref)):
+        left = ref[...].reshape(-1, ref.shape[2])
+        right = right_ref[:, seq].reshape(-1, right_ref.shape[3])
+        term = outer_dot(left, right)
+        total = term if total is None else total + term
+    out_ref[...] = total.astype(out_ref.dtype)
+
+
+def outer_acts(acts, early, width):
+    devices, stretch, size = acts[0].shape
+    block = 128
+    lefts = pl.BlockSpec((devices, stretch, block), lambda i: (0, 0, i))
+    rights = pl.BlockSpec((devices, 2, stretch, width), lambda i: (0, 0, 0, 0))
+    return pl.pallas_call(
+        outer_acts_kernel,
+        grid=(size // block,),
+        in_specs=[lefts] * 2 + [rights],
+        out_specs=pl.BlockSpec((block, width), lambda i: (i, 0)),
+        out_shape=jax.ShapeDtypeStruct((size, width), jnp.bfloat16),
+        compiler_params=pltpu.CompilerParams(vmem_limit_bytes=48 << 20),
+        cost_estimate=pl.CostEstimate(
+            flops=4 * devices * stretch * size * width,
+            bytes_accessed=4 * devices * stretch * (width + size) + 2 * size * width,
+            transcendentals=0,
+        ),
+        name="outer_acts",
+    )(*acts, early)
 
 
 def local(
@@ -757,22 +1044,20 @@
     small = jnp.concatenate([w_router, w_gains.T], axis=1)
     small = jnp.pad(small, ((0, 0), (0, extra - experts - 2)))
     half_cols = w_qkv.shape[1] // 2
-    first_half, second_half = gather_rows(
+    first_half, second_half, small_full = gather_rows(
         [
             w_qkv[:, :half_cols].astype(low_type),
-            jnp.concatenate([w_qkv[:, half_cols:], small], axis=1).astype(low_type),
+            w_qkv[:, half_cols:].astype(low_type),
+            small.astype(low_type),
         ],
-        all_orders,
-    )
-    router_full = second_half[:, half_cols : half_cols + experts]
-    gains_full = second_half[:, half_cols + experts : half_cols + experts + 2].astype(full_type)
-    second_half = second_half[:, :half_cols]
+        (all_orders[0], all_orders[1], all_orders[0]),
+    )
+    router_full = small_full[:, :experts]
+    gains_full = small_full[:, experts : experts + 2].astype(full_type)
     gain_in = gains_full[:, 0][None]
     gain_mid = gains_full[:, 1][None]
-    out_full = lax.all_gather(w_out.astype(low_type), ("head", "blk"), axis=0, tiled=True)
-    shgu_full = lax.all_gather(w_shgu.astype(low_type), ("head", "blk"), axis=0, tiled=True)
-    shdown_full = lax.all_gather(w_shdown.astype(low_type), ("head", "blk"), axis=0, tiled=True)
-
+    out_low = w_out.astype(low_type)
+    out_full = lax.all_gather(out_low, ("head", "blk"), axis=0, tiled=True)
     own_pos = me * stretch + jnp.arange(stretch, dtype=jnp.int32)
     valid = (own_pos[None, :] < lengths[:, None]).astype(full_type).reshape(rows, 1)
     limit = jnp.minimum(own_pos[None, :], lengths[:, None] - 1).reshape(rows, 1)
@@ -787,13 +1072,22 @@
         for half in (first_half, second_half)
     ]
     per_half = KV_HEADS // 2
-    group_parts = [
-        projected[g // per_half][:, (g % per_half) * group_cols : (g % per_half + 1) * group_cols]
-        for g in range(KV_HEADS)
+    by_group = [half.reshape(seqs, stretch, per_half, group_cols) for half in projected]
+    queries = [
+        [half[s, :, :, :query_cols].reshape(stretch, -1) for half in by_group]
+        for s in range(seqs)
     ]
-    queries = [part[:, :query_cols] for part in group_parts]
-    kv_orders = [all_orders[g % 2] for g in range(KV_HEADS)]
-    pairs = gather_relative([part[:, query_cols:] for part in group_parts], kv_orders)
+    pairs = gather_relative(
+        [
+            half[s, :, :, query_cols:].reshape(stretch, -1)
+            for s in range(seqs)
+            for half in by_group
+        ],
+        [order for s in range(seqs) for order in all_orders],
+        WAVES_KV,
+    )
+    pairs = [pairs[2 * s : 2 * s + 2] for s in range(seqs)]
+    limits = limit.reshape(seqs, stretch, 1)
     key_pos = [
         (block_devices(order)[:, None] * stretch + jnp.arange(stretch, dtype=jnp.int32)).reshape(
             1, -1
@@ -807,49 +1101,120 @@
     early = jnp.concatenate(
         [grad_low, jnp.pad(named, ((0, 0), (0, tail - experts))).astype(low_type)], axis=1
     )
-    early, projected[0] = lax.optimization_barrier((early, projected[0]))
-
-    def to_columns(values):
-        pieces = gather_relative(list(values.reshape(seqs, stretch, -1)), row_orders)
-        return jnp.concatenate([piece.reshape(-1, values.shape[1]) for piece in pieces], axis=0)
-
-    def from_columns(values):
-        pieces = values.reshape(seqs, blocks_axis, stretch, -1)
-        return jnp.concatenate(scatter_relative(list(pieces), row_orders), axis=0)
-
-    early_all = to_columns(early)
-    grads_all = early_all[:, :width]
-    named_all = early_all[:, width : width + experts] > 0
-
-    def gather_head(values):
+    early_all = lax.all_gather(early, "blk", axis=0, tiled=True).reshape(
+        blocks_axis, seqs, stretch, -1
+    )
+
+    def to_columns(values, beside):
+        spread = gather_relative(values, row_orders, WAVES_COL, beside)
+        return [[half.reshape(-1, half.shape[-1]) for half in pair] for pair in spread]
+
+    def rows_of(values):
+        return list(values.reshape(seqs, stretch, -1))
+
+
+    def gather_head(values, *earlier):
         own = values.astype(low_type)[None]
         for step in reversed(head_bits):
             mine = jnp.arange(2).reshape(2, 1, 1, 1) == own_bit(step)
-            own = jnp.where(mine, own[None], swap(own, step)[None])
+            own = jnp.where(mine, own[None], after(swap(own, step), *earlier)[None])
             own = own.reshape((-1,) + own.shape[2:])
         return own.reshape(-1, values.shape[1])
 
-    def scatter_head(values):
+    def scatter_head(values, *earlier):
         for step in head_bits:
             half = values.shape[0] // 2
             bit = own_bit(step)
             mine = lax.dynamic_slice_in_dim(values, bit * half, half, 0)
             theirs = lax.dynamic_slice_in_dim(values, (1 - bit) * half, half, 0)
-            values = mine + swap(theirs.astype(low_type), step).astype(full_type)
+            others = after(swap(theirs.astype(low_type), step), *earlier)
+            values = mine.astype(full_type) + others.astype(full_type)
         return values
 
-    expgu_full = gather_head(w_expgu[0])
-    expdown_full = gather_head(w_expdown[0])
-
-    attended = [
-        attend(queries[g], pairs[g], key_pos[g % 2], limit, seqs, stretch)
-        for g in range(KV_HEADS)
-    ]
-    attended_tok = jnp.concatenate([item[1] for item in attended], axis=1)
-    branch = jnp.dot(attended_tok, out_full, preferred_element_type=full_type)
-    middle = inputs + branch
-    inverse_mid = lax.rsqrt(jnp.mean(middle * middle, axis=1, keepdims=True) + norm_eps)
-    normed_mid = (middle * inverse_mid * gain_mid).astype(low_type)
+    attended, attended_tok, branch, middle, inverse_mid, normed_mid = [], [], [], [], [], []
+    for s in range(seqs):
+        asked = queries[s] if s == 0 else after(queries[s], normed_mid[s - 1])
+        attended.append(
+            [
+                attend(query, pair, pos, limits[s])
+                for query, pair, pos in zip(asked, pairs[s], key_pos)
+            ]
+        )
+        attended_tok.append(jnp.concatenate([item[1] for item in attended[s]], axis=1))
+        branch.append(jnp.dot(attended_tok[s], out_full, preferred_element_type=full_type))
+        middle.append(rows_of(inputs)[s] + branch[s])
+        squares = jnp.mean(middle[s] * middle[s], axis=1, keepdims=True)
+        inverse_mid.append(lax.rsqrt(squares + norm_eps))
+        normed_mid.append((middle[s] * inverse_mid[s] * gain_mid).astype(low_type))
+
+    unit = SHARED // devices
+    w_shgu_late = after(w_shgu, projected)
+    w_expgu_late = after(w_expgu, projected)
+    units = 2 * heads_axis * unit
+    sliced = jnp.transpose(
+        w_shgu_late.astype(low_type).reshape(shard, 2 * heads_axis, blocks_axis, unit), (2, 0, 1, 3)
+    ).reshape(blocks_axis, shard, units)
+    sliced = gather_head(transpose_blk(sliced).reshape(blocks_axis * shard, units))
+    gate_up_full = jnp.concatenate([gather_head(w_expgu_late[0], normed_mid), sliced], axis=1)
+    down_full = jnp.concatenate([gather_head(w_expdown[0], projected), gather_head(w_shdown, projected)], axis=0)
+    act_rows = -(-down_full.shape[0] // 128) * 128
+    down_full = jnp.pad(down_full, ((0, act_rows - down_full.shape[0]), (0, 0)))
+
+    def pull(_):
+        flat = early_all.reshape(-1, early_all.shape[-1])[:, :width]
+        return back_dot(flat, down_full).reshape(blocks_axis, seqs, stretch, -1)
+
+    found = []
+    mid_all = to_columns(normed_mid, ({1: pull}, found))
+    pulled = found[0]
+
+    lanes = jnp.arange(tail, dtype=jnp.int32)[None]
+    own = jnp.concatenate([lanes == blk_index, lanes == experts + blk_index]).astype(full_type)
+    router_wide = jnp.pad(router_full, ((0, 0), (0, tail - experts)))
+    places = [blk_blocks(order) for order in row_orders]
+
+    done, back_sums = [], []
+    for s in range(seqs):
+        mid = mid_all[s] if s == 0 else after(mid_all[s], done[s - 1][0])
+        result = run_expert(
+            mid, pulled, early_all, router_wide, own, gate_up_full, places[s], s
+        )
+        done.append(result)
+        back_sums.append(
+            tuple(item.reshape(blocks_axis // 2, stretch, -1) for item in result[:2])
+        )
+    acts = [item[2] for item in done]
+    hids = [item[3] for item in done]
+
+    def outer_gate_up(before):
+        return outer_experts(mid_all, after(hids, before))
+
+    def outer_down(before):
+        return outer_acts(after(acts, before), early_all, width)
+
+    def routed(before):
+        terms = [
+            jnp.dot(act.reshape(-1, act.shape[2]), down_full, preferred_element_type=full_type)
+            .astype(low_type)
+            .reshape(blocks_axis, stretch, width)
+            for act in after(acts, before)
+        ]
+        return jnp.concatenate(terms, axis=1).reshape(-1, width)
+
+    found = []
+    back_sums = scatter_relative(
+        back_sums,
+        row_orders,
+        beside=({1: outer_gate_up, 2: outer_down, 3: routed}, found),
+    )
+    back_sums = [item.astype(full_type) for item in back_sums]
+    grad_gate_up, grad_down, routed_terms = found
+    added = lax.psum_scatter(routed_terms, "blk", scatter_dimension=0, tiled=True)
+
+    def sum_rows(values):
+        return lax.psum_scatter(
+            values.astype(low_type), ("head", "blk"), scatter_dimension=0, tiled=True
+        ).astype(full_type)
 
     def all_gates(values, chosen):
         logits = jnp.dot(values, router_full, preferred_element_type=full_type)
@@ -857,46 +1222,85 @@
         raised = jnp.where(chosen, jnp.exp(logits - jnp.max(logits, axis=1, keepdims=True)), 0.0)
         return raised / jnp.sum(raised, axis=1, keepdims=True)
 
-    own_expert = jnp.arange(experts, dtype=jnp.int32)[None] == blk_index
-    mid_all = to_columns(normed_mid)
-    gate = jnp.sum(
-        jnp.where(own_expert, all_gates(mid_all, named_all), 0.0), axis=1, keepdims=True
-    )
-    hidden = jnp.dot(mid_all, expgu_full, preferred_element_type=full_type)
-    gate_part = hidden[:, :EXPERT_FF]
-    up_part = hidden[:, EXPERT_FF:]
-    middle_act = (jax.nn.silu(gate_part) * up_part).astype(low_type).astype(full_type)
-    weighed_act = (gate * middle_act).astype(low_type)
-    pulled = back_dot(grads_all, expdown_full)
-    routed_terms = jnp.dot(weighed_act, expdown_full, preferred_element_type=full_type)
-    grad_gate = jnp.sum(pulled * middle_act, axis=1, keepdims=True)
-    grad_middle_act = gate * pulled
-    grad_hidden = jnp.concatenate(
-        [
-            grad_middle_act * up_part * silu_grad(gate_part),
-            grad_middle_act * jax.nn.silu(gate_part),
-        ],
-        axis=1,
-    ).astype(low_type)
-    gate_high = grad_gate.astype(low_type).astype(full_type)
-    lanes = jnp.arange(tail, dtype=jnp.int32)[None]
-    gate_lanes = jnp.where(lanes == blk_index, gate_high, 0.0) + jnp.where(
-        lanes == experts + blk_index, grad_gate - gate_high, 0.0
-    )
-    in_terms = jnp.concatenate([back_dot(grad_hidden, expgu_full), gate_lanes], axis=1)
-    back_sums = from_columns(in_terms.astype(low_type)).astype(full_type)
-    routed = from_columns(routed_terms.astype(low_type)).astype(full_type)
-    grad_expdown = outer_dot(weighed_act, grads_all)
-    grad_expgu = outer_dot(mid_all, grad_hidden)
-    g_expgu = scatter_head(grad_expgu)[None]
-    g_expdown = scatter_head(grad_expdown)[None]
-
-    shared_hidden = jnp.dot(normed_mid, shgu_full, preferred_element_type=full_type)
-    shared_gate = shared_hidden[:, :SHARED]
-    shared_up = shared_hidden[:, SHARED:]
-    shared_mid = (jax.nn.silu(shared_gate) * shared_up).astype(low_type)
-    shared_out = jnp.dot(shared_mid, shdown_full, preferred_element_type=full_type)
-    final = middle + routed + shared_out
+    chosen = rows_of(named > 0)
+    finals = rows_of(grad_final)
+    grad_router, grad_gain_mid, grad_mid_total, grad_branch, back = [], [], [], [], []
+    for s in range(seqs):
+        gates = all_gates(normed_mid[s], chosen[s])
+        sums = back_sums[s]
+        grad_gates = sums[:, width : width + experts] + (
+            sums[:, width + experts : width + 2 * experts]
+        )
+        grad_logits = gates * (grad_gates - jnp.sum(gates * grad_gates, axis=1, keepdims=True))
+        grad_logits = jnp.where(chosen[s], grad_logits, 0.0).astype(low_type)
+        grad_router.append(outer_dot(normed_mid[s], grad_logits))
+        grad_normed = back_dot(grad_logits, router_full) + sums[:, :width]
+        scaled_mid = grad_normed * gain_mid
+        grad_gain_mid.append(jnp.sum(grad_normed * middle[s] * inverse_mid[s], axis=0))
+        grad_mid_total.append(
+            finals[s]
+            + inverse_mid[s] * scaled_mid
+            - middle[s]
+            * inverse_mid[s] ** 3
+            * jnp.mean(scaled_mid * middle[s], axis=1, keepdims=True)
+        )
+        grad_branch.append(grad_mid_total[s].astype(low_type))
+        grad_attended = back_dot(grad_branch[s], out_full).astype(low_type)
+        cols = per_half * query_cols
+        back.append(
+            [
+                attend_back(
+                    queries[s][half],
+                    pairs[s][half],
+                    key_pos[half],
+                    limits[s],
+                    grad_attended[:, half * cols : (half + 1) * cols],
+                    attended[s][half][0],
+                    attended[s][half][2],
+                )
+                for half in range(2)
+            ]
+        )
+    grad_router = sum(grad_router)
+    grad_gain_mid = sum(grad_gain_mid)
+    grad_mid_total = jnp.concatenate(grad_mid_total, axis=0)
+    g_out = sum_rows(
+        outer_dot(jnp.concatenate(attended_tok, axis=0), jnp.concatenate(grad_branch, axis=0))
+    )
+    g_shgu = scatter_head(grad_gate_up[:, 2 * EXPERT_FF :], grad_branch).astype(low_type)
+    g_shgu = transpose_blk(g_shgu.reshape(blocks_axis, shard, units))
+    g_shgu = (
+        jnp.transpose(
+            g_shgu.reshape(blocks_axis, shard, 2 * heads_axis, unit), (1, 2, 0, 3)
+        )
+        .reshape(w_shgu.shape)
+        .astype(full_type)
+    )
+
+    pair_sums = scatter_relative(
+        [item[1:] for part in back for item in part],
+        [order for s in range(seqs) for order in all_orders],
+        WAVES_KV,
+    )
+    grad_halves = [
+        jnp.concatenate(
+            [
+                jnp.concatenate(
+                    [
+                        back[s][half][0].reshape(stretch, per_half, query_cols),
+                        pair_sums[2 * s + half].reshape(stretch, per_half, 2 * HEAD_DIM),
+                    ],
+                    axis=2,
+                ).reshape(stretch, -1)
+                for s in range(seqs)
+            ],
+            axis=0,
+        )
+        for half in range(2)
+    ]
+    branch = jnp.concatenate(branch, axis=0)
+    middle = jnp.concatenate(middle, axis=0)
+    final = middle + added.astype(full_type)
     block_out = final.astype(low_type).reshape(seqs, stretch, width)
     stat_sums = jnp.stack(
         [
@@ -905,68 +1309,10 @@
             jnp.sum(final * final * valid),
         ]
     )
-
-    def sum_rows(values):
-        return lax.psum_scatter(
-            values.astype(low_type), ("head", "blk"), scatter_dimension=0, tiled=True
-        ).astype(full_type)
-
-    grad_shdown = outer_dot(shared_mid, grad_low)
-    grad_shared_mid = back_dot(grad_low, shdown_full)
-    grad_shared_hidden = jnp.concatenate(
-        [
-            grad_shared_mid * shared_up * silu_grad(shared_gate),
-            grad_shared_mid * jax.nn.silu(shared_gate),
-        ],
-        axis=1,
-    ).astype(low_type)
-    grad_shgu = outer_dot(normed_mid, grad_shared_hidden)
-    g_shdown = sum_rows(grad_shdown)
-    g_shgu = sum_rows(grad_shgu)
-    grad_normed = back_dot(grad_shared_hidden, shgu_full)
-
-    chosen = named > 0
-    gates = all_gates(normed_mid, chosen)
-    grad_gates = back_sums[:, width : width + experts] + (
-        back_sums[:, width + experts : width + 2 * experts]
-    )
-    grad_logits = gates * (grad_gates - jnp.sum(gates * grad_gates, axis=1, keepdims=True))
-    grad_logits = jnp.where(chosen, grad_logits, 0.0).astype(low_type)
-    grad_router = outer_dot(normed_mid, grad_logits)
-    grad_normed = grad_normed + back_dot(grad_logits, router_full) + back_sums[:, :width]
-    scaled_mid = grad_normed * gain_mid
-    grad_gain_mid = jnp.sum(grad_normed * middle * inverse_mid, axis=0)
-    grad_mid_total = (
-        grad_final
-        + inverse_mid * scaled_mid
-        - middle * inverse_mid**3 * jnp.mean(scaled_mid * middle, axis=1, keepdims=True)
-    )
-    grad_branch = grad_mid_total.astype(low_type)
-    grad_attended = back_dot(grad_branch, out_full).astype(low_type)
-    g_out = sum_rows(outer_dot(attended_tok, grad_branch))
-
-    back = [
-        attend_back(
-            queries[g],
-            pairs[g],
-            key_pos[g % 2],
-            limit,
-            grad_attended[:, g * query_cols : (g + 1) * query_cols],
-            attended[g][0],
-            attended[g][2],
-            seqs,
-            stretch,
-        )
-        for g in range(KV_HEADS)
-    ]
-    pair_sums = scatter_relative([item[1] for item in back], kv_orders)
-    grad_groups = [
-        jnp.concatenate([item[0], pair], axis=1) for item, pair in zip(back, pair_sums)
-    ]
-    grad_halves = [
-        jnp.concatenate(grad_groups[:per_half], axis=1),
-        jnp.concatenate(grad_groups[per_half:], axis=1),
-    ]
+    grad_halves = after(grad_halves, g_shgu)
+    g_expgu = scatter_head(grad_gate_up[:, : 2 * EXPERT_FF], grad_halves)[None]
+    g_expdown = scatter_head(grad_down[:EXPERT_FF], grad_halves)[None]
+    g_shdown = scatter_head(grad_down[EXPERT_FF : EXPERT_FF + heads_axis * unit], grad_halves)
     grad_normed_in = back_dot(grad_halves[0], first_half) + back_dot(grad_halves[1], second_half)
     scaled_in = grad_normed_in * gain_in
     grad_gain_in = jnp.sum(grad_normed_in * inputs * inverse_in, axis=0)
@@ -981,17 +1327,13 @@
     )
     grad_small = jnp.pad(grad_small, ((0, 0), (0, extra - experts - 2)))
     sums = scatter_rows(
-        [
-            outer_dot(normed_in, grad_halves[0]).astype(low_type),
-            jnp.concatenate([outer_dot(normed_in, grad_halves[1]), grad_small], axis=1).astype(
-                low_type
-            ),
-        ],
-        all_orders,
-    )
-    g_qkv = jnp.concatenate([sums[0], sums[1][:, :half_cols]], axis=1).astype(full_type)
-    g_router = sums[1][:, half_cols : half_cols + experts].astype(full_type)
-    g_gains = sums[1][:, half_cols + experts : half_cols + experts + 2].astype(full_type).T
+        [outer_dot(normed_in, half).astype(low_type) for half in grad_halves]
+        + [grad_small.astype(low_type)],
+        (all_orders[0], all_orders[1], all_orders[0]),
+    )
+    g_qkv = jnp.concatenate(sums[:2], axis=1).astype(full_type)
+    g_router = sums[2][:, :experts].astype(full_type)
+    g_gains = sums[2][:, experts : experts + 2].astype(full_type).T
 
     local_squares = (
         jnp.sum(g_qkv * g_qkv)
@@ -1096,5 +1438,6 @@
     )
     shards = mesh.size
     cubes = all(size & (size - 1) == 0 for size in mesh.shape.values())
+    cubes = cubes and mesh.shape["head"] == 2
     step = local_cube if cubes and WIDTH_ROWS % (16 * shards) == 0 else local
     return jax.shard_map(step, mesh=mesh, in_specs=in_specs, out_specs=out_specs, check_vma=False)

time: 953 us -> 723 us (0.76)
  waiting for transfers between devices: 427 us -> 275 us
  matrix products: 113 us -> 43.4 us
  Pallas kernels: 22.7 us -> 80.9 us
  local copies, waits for them, and re-layouts: 128 us -> 81.3 us
  other arithmetic: 134 us -> 110 us
  starting transfers between devices: 91.6 us -> 103 us
    ppermute x101 -> x107, waiting for transfers between devices: 393 us -> 272 us  [swap(): return lax.ppermute(values, name, [(i, i ^ bit) for i in range(size)])]
    pallas_call x8 -> x12, Pallas kernels: 22.7 us -> 80.9 us  [the longest x2 31.8 us: run_expert(): pl.pallas_call(functools.partial(expert_kernel, blocks), grid_spec=pltpu....]
    reduce_scatter x3 -> x1, waiting for transfers between devices: 33.8 us -> 0.01 us  [sum_rows(): lax.psum_scatter(values.astype(low_type), ('head', 'blk'), scatter_dimens...]
    dot_general x8 -> x7, matrix products: 50.8 us -> 18.1 us  [back_dot(): lax.dot_general(left, right, (((1,), (1,)), ((), ())), preferred_element_...]
    dot_general x8 -> x5, matrix products: 28.9 us -> 7.3 us  [outer_dot(): lax.dot_general(left, right, (((0,), (0,)), ((), ())), preferred_element_...]
    slice x43 -> x33, local copies, waits for them, and re-layouts: 26.1 us -> 8.34 us  [the longest x22 3.67 us: act(): return (total[:half], total[half:]) if half else total]
    dot_general x5 -> x4, matrix products: 27.9 us -> 11.7 us  [the longest x2 6.06 us: local_cube(): jnp.dot(attended_tok[s], out_full, preferred_element_type=full_type)]
    unnamed x342 -> x440, local copies, waits for them, and re-layouts: 44.3 us -> 29.8 us
  transfers between devices with their start and end apart: 107 -> 113, of which waited for: 49 -> 54; matrix products, arithmetic and copies ran while one was open for 34% -> 26% of each run, Pallas kernels for 2% -> 11%
where the time goes in v2:
time: 723 us; the launch traced here: 719 us
  waiting for transfers between devices  275 us (38%)
  other arithmetic  110 us (15%)
  starting transfers between devices  103 us (14%)
  local copies, waits for them, and re-layouts  81.3 us (11%)
  Pallas kernels  80.9 us (11%)
  matrix products  43.4 us (6%)
  between operations  24.8 us (3%)
    ppermute x107, waiting for transfers between devices, swap(): return lax.ppermute(values, name, [(i, i ^ bit) for i in range(size)])  272 us
    ppermute x107, starting transfers between devices, swap(): return lax.ppermute(values, name, [(i, i ^ bit) for i in range(size)])  98.7 us
    pallas_call x2, Pallas kernels, run_expert(): pl.pallas_call(functools.partial(expert_kernel, blocks), grid_spec=pltpu....  31.8 us
    unnamed x440, local copies, waits for them, and re-layouts  29.8 us
    mul x8, other arithmetic, adam_update(): -learn_rate  19.2 us
    dot_general x7, matrix products, back_dot(): lax.dot_general(left, right, (((1,), (1,)), ((), ())), preferred_element_...  18.1 us
    pallas_call x4, Pallas kernels, attend_back(): pl.pallas_call(attend_back_kernel, grid=(groups,), in_specs=[wide, kv, kv...  17.4 us
    add x28, other arithmetic, act(): total = kept + swap(sent, step)  15 us
  transfers between devices with their start and end apart: 113, of which 54 were waited for; matrix products, arithmetic and copies ran while one was open for 26% of the time, Pallas kernels for 11%

profile of v2, /device:TPU:0, one launch (start us, length us, event | category | flops | bytes accessed | tf_op | source)
XLA Modules:
  0.0 718.7 jit_solution(882604496081523816)
XLA Ops:
  31.2 11.8 %collective-permute-done.5 = bf16[1,2,1,1,1,48,128]{6,5,1,4,3,2,0:T(8,128)(2,1)S(1)} collective-permute-done((bf16[1,2,1,1,1,48,128]{6,5,1,4,3,2,0:T(8,128)(2,1)S(1)}, bf16[1,2,1,1,1,48,128]{6,5,1,4,3,2,0:T(8,128)(2,1)S(1)}, u32[]{:S(2)}, u32[]{:S(2)}) %collective-permute-start.5) | collective-permute-done | bytes 24608 | tf_op jit(solution)/shard_map/ppermute | solution.py:98
  46.9 10.1 %collective-permute-done.8 = bf16[1,2,2,1,1,48,128]{6,5,2,1,4,3,0:T(8,128)(2,1)S(1)} collective-permute-done((bf16[1,2,2,1,1,48,128]{6,5,2,1,4,3,0:T(8,128)(2,1)S(1)}, bf16[1,2,2,1,1,48,128]{6,5,2,1,4,3,0:T(8,128)(2,1)S(1)}, u32[]{:S(2)}, u32[]{:S(2)}) %collective-permute-start.8) | collective-permute-done | bytes 49184 | tf_op jit(solution)/shard_map/ppermute | solution.py:98
  62.6 28.3 %collective-permute-done.11 = bf16[1,2,2,2,1,48,128]{6,5,3,2,1,4,0:T(8,128)(2,1)S(1)} collective-permute-done((bf16[1,2,2,2,1,48,128]{6,5,3,2,1,4,0:T(8,128)(2,1)S(1)}, bf16[1,2,2,2,1,48,128]{6,5,3,2,1,4,0:T(8,128)(2,1)S(1)}, u32[]{:S(2)}, u32[]{:S(2)}) %collective-permute-start.11) | collective-permute-done | bytes 98336 | tf_op jit(solution)/shard_map/ppermute | solution.py:98
  104.1 5.2 broadcast_select_fusion
  153.7 6.8 collective-permute-done.44
  183.4 10.3 %collective-permute-done.18 = bf16[8,64,512]{2,1,0:T(8,128)(2,1)S(1)} collective-permute-done((bf16[8,64,512]{2,1,0:T(8,128)(2,1)S(1)}, bf16[8,64,512]{2,1,0:T(8,128)(2,1)S(1)}, u32[]{:S(2)}, u32[]{:S(2)}) %collective-permute-start.18) | collective-permute-done | bytes 524320 | tf_op jit(solution)/shard_map/ppermute | solution.py:98
  206.0 8.8 %collective-permute-done.28 = bf16[8,64,512]{2,1,0:T(8,128)(2,1)S(1)} collective-permute-done((bf16[8,64,512]{2,1,0:T(8,128)(2,1)S(1)}, bf16[8,64,512]{2,1,0:T(8,128)(2,1)S(1)}, u32[]{:S(2)}, u32[]{:S(2)}) %collective-permute-start.28) | collective-permute-done | bytes 524320 | tf_op jit(solution)/shard_map/ppermute | solution.py:98
  242.6 5.1 collective-permute-done.37
  248.3 9.1 %fusion = f32[2048,640]{1,0:T(8,128)} fusion(bf16[2048,1664]{1,0:T(8,128)(2,1)} %all-gather.5.cloned.1.call-done, bf16[64,1536]{1,0:T(8,128)(2,1)S(1)} %copy-done.144, bf16[512,1536]{1,0:T(8,128)(2,1)} %bitcast_select_fusion.1), kind=kOutput, calls=%fused_computation.3 | convolution fusion | flops 4033413120 | bytes 13303808 | tf_op jit(solution)/shard_map/dot_general | solution.py:48
  257.5 9.6 %collective-permute-done.38 = bf16[2,64,1536]{2,1,0:T(8,128)(2,1)S(1)} collective-permute-done((bf16[2,64,1536]{2,1,0:T(8,128)(2,1)S(1)}, bf16[2,64,1536]{2,1,0:T(8,128)(2,1)S(1)}, u32[]{:S(2)}, u32[]{:S(2)}) %collective-permute-start.38) | collective-permute-done | bytes 393248 | tf_op jit(solution)/shard_map/ppermute | solution.py:98
  270.2 14.9 %collective-permute-done.41 = bf16[4,64,1536]{2,1,0:T(8,128)(2,1)S(1)} collective-permute-done((bf16[4,64,1536]{2,1,0:T(8,128)(2,1)S(1)}, bf16[4,64,1536]{2,1,0:T(8,128)(2,1)S(1)}, u32[]{:S(2)}, u32[]{:S(2)}) %collective-permute-start.41) | collective-permute-done | bytes 786464 | tf_op jit(solution)/shard_map/ppermute | solution.py:98
  290.9 15.7 %expert.2 = (bf16[512,1664]{1,0:T(8,128)(2,1)}, bf16[512,1664]{1,0:T(8,128)(2,1)}, bf16[16,64,640]{2,1,0:T(8,128)(2,1)S(1)}, bf16[1024,1152]{1,0:T(8,128)(2,1)}) custom-call(s32[16]{0:T(128)S(1)} %copy-done.33, bf16[512,1536]{1,0:T(8,128)(2,1)S(1)} %bitcast.274, bf16[512,1536]{1,0:T(8,128)(2,1)S(1)} %bitcast.276, ...), custom_call_target="tpu_custom_call" | custom-call | flops 7247757312 | bytes 12582912 | tf_op jit(solution)/shard_map/expert/pallas_call | solution.py:496
  307.2 16.1 %expert.3 = (bf16[512,1664]{1,0:T(8,128)(2,1)}, bf16[512,1664]{1,0:T(8,128)(2,1)}, bf16[16,64,640]{2,1,0:T(8,128)(2,1)S(1)}, bf16[1024,1152]{1,0:T(8,128)(2,1)}) custom-call(s32[16]{0:T(128)S(1)} %copy-done.32, bf16[512,1536]{1,0:T(8,128)(2,1)S(1)} %bitcast.272, bf16[512,1536]{1,0:T(8,128)(2,1)S(1)} %bitcast.278, ...), custom_call_target="tpu_custom_call" | custom-call | flops 7247757312 | bytes 12582912 | tf_op jit(solution)/shard_map/expert/pallas_call | solution.py:496
  334.6 13.0 %outer_experts.1 = bf16[1536,1152]{1,0:T(8,128)(2,1)} custom-call(bf16[512,1536]{1,0:T(8,128)(2,1)S(1)} %bitcast.275, bf16[512,1536]{1,0:T(8,128)(2,1)S(1)} %bitcast.277, bf16[512,1536]{1,0:T(8,128)(2,1)S(1)} %bitcast.273, bf16[512,1536]{1,0:T(8,128)(2,1)} %bitcast.279, bf16[1024,1152]{1,0:T(8,128)(2,1)} %get-tuple-element.217.right0_ref, ...), custom_call_target="tpu_custom_call" | custom-call | flops 7247757312 | bytes 14548992 | tf_op jit(solution)/shard_map/outer_experts/pallas_call | solution.py:549
  350.8 4.4 collective-permute-done.54
  356.5 8.3 %outer_acts.1 = bf16[640,1536]{1,0:T(8,128)(2,1)S(1)} custom-call(bf16[16,64,640]{2,1,0:T(8,128)(2,1)S(1)} %copy-done.35, bf16[16,64,640]{2,1,0:T(8,128)(2,1)S(1)} %copy-done.37, bf16[16,2,64,1664]{3,2,1,0:T(8,128)(2,1)} %bitcast.298), custom_call_target="tpu_custom_call" | custom-call | flops 4026531840 | bytes 10878976 | tf_op jit(solution)/shard_map/outer_acts/pallas_call | solution.py:580
  364.8 8.4 %collective-permute-done.55 = bf16[2,64,1664]{2,1,0:T(8,128)(2,1)S(1)} collective-permute-done((bf16[2,64,1664]{2,1,0:T(8,128)(2,1)S(1)}, bf16[2,64,1664]{2,1,0:T(8,128)(2,1)S(1)}, u32[]{:S(2)}, u32[]{:S(2)}) %collective-permute-start.55) | collective-permute-done | bytes 426016 | tf_op jit(solution)/shard_map/ppermute | solution.py:98
  373.4 5.6 collective-permute-done.56
  438.2 4.6 attend_back.5
  448.0 4.7 attend_back.7
  464.3 9.4 %collective-permute-done.66 = bf16[8,64,512]{2,1,0:T(8,128)(2,1)S(1)} collective-permute-done((bf16[8,64,512]{2,1,0:T(8,128)(2,1)S(1)}, bf16[8,64,512]{2,1,0:T(8,128)(2,1)S(1)}, u32[]{:S(2)}, u32[]{:S(2)}) %collective-permute-start.66) | collective-permute-done | bytes 524320 | tf_op jit(solution)/shard_map/ppermute | solution.py:98
  486.2 5.3 collective-permute-done.62
  498.4 4.9 collective-permute-done.63
  514.1 17.9 %collective-permute-done.67 = bf16[8,64,512]{2,1,0:T(8,128)(2,1)S(1)} collective-permute-done((bf16[8,64,512]{2,1,0:T(8,128)(2,1)S(1)}, bf16[8,64,512]{2,1,0:T(8,128)(2,1)S(1)}, u32[]{:S(2)}, u32[]{:S(2)}) %collective-permute-start.67) | collective-permute-done | bytes 524320 | tf_op jit(solution)/shard_map/ppermute | solution.py:98
  548.6 5.5 collective-permute-done.73
  554.4 4.5 collective-permute-done.78
  577.6 8.0 %collective-permute-done.96 = bf16[1,2,2,2,1,48,128]{5,6,4,3,2,1,0:T(8,128)(2,1)S(1)} collective-permute-done((bf16[1,2,2,2,1,48,128]{5,6,4,3,2,1,0:T(8,128)(2,1)S(1)}, bf16[1,2,2,2,1,48,128]{5,6,4,3,2,1,0:T(8,128)(2,1)S(1)}, u32[]{:S(2)}, u32[]{:S(2)}) %collective-permute-start.96) | collective-permute-done | bytes 98336 | tf_op jit(solution)/shard_map/ppermute | solution.py:98
  587.8 4.5 fusion.6
  612.4 17.4 %collective-permute-done.90 = bf16[2,2,2,1,1,48,1280]{6,5,4,3,2,1,0:T(8,128)(2,1)S(1)} collective-permute-done((bf16[2,2,2,1,1,48,1280]{6,5,4,3,2,1,0:T(8,128)(2,1)}, bf16[2,2,2,1,1,48,1280]{6,5,4,3,2,1,0:T(8,128)(2,1)S(1)}, u32[]{:S(2)}, u32[]{:S(2)}) %collective-permute-start.90) | collective-permute-done | bytes 983072 | tf_op jit(solution)/shard_map/ppermute | solution.py:98
  635.2 7.2 %collective-permute-done.91 = bf16[1,2,2,1,1,48,1280]{6,5,4,3,2,1,0:T(8,128)(2,1)S(1)} collective-permute-done((bf16[1,2,2,1,1,48,1280]{6,5,4,3,2,1,0:T(8,128)(2,1)S(1)}, bf16[1,2,2,1,1,48,1280]{6,5,4,3,2,1,0:T(8,128)(2,1)S(1)}, u32[]{:S(2)}, u32[]{:S(2)}) %collective-permute-start.91) | collective-permute-done | bytes 491552 | tf_op jit(solution)/shard_map/ppermute | solution.py:98
  645.3 6.2 collective-permute-done.92
  692.8 7.8 %add_multiply_fusion = (f32[1,768,1024]{2,1,0:T(8,128)}, f32[1,768,1024]{2,1,0:T(8,128)}, f32[1,768,1024]{2,1,0:T(8,128)}) fusion(f32[1,768,1024]{2,1,0:T(8,128)S(1)} %copy-done.62, f32[]{:T(128)S(6)} %div.248, bf16[768,1024]{1,0:T(8,128)(2,1)} %collective-permute-done.100, bf16[1536,1024]{1,0:T(8,128)(2,1)} %copy-done.63, s32[]{:T(128)S(6)} %select_n.532, ...), kind=kLoop, calls=%fused_computation.19 | loop fusion | flops 14155776 | bytes 22020104 | tf_op jit(solution)/shard_map/mul | solution.py:78
  (960 shorter events, 394.5 us)
Async XLA Ops:
  7.3 214.4 %all-gather.3.cloned.1.call-start = ((), (), s32[]{:S(2)}) async-start(), calls=%async_computation.2 | async-start | bytes 4866048 | tf_op jit(solution)/shard_map/all_gather | solution.py:1060
  9.1 239.2 %all-gather.5.cloned.1.call-start = ((), (), s32[]{:S(2)}) async-start(), calls=%async_computation.3 | async-start | bytes 7241728 | tf_op jit(solution)/shard_map/all_gather | solution.py:1104
  18.1 106.0 %collective-permute-start.40 = (bf16[1,32,1536]{2,1,0:T(8,128)(2,1)}, bf16[1,32,1536]{2,1,0:T(8,128)(2,1)}, u32[]{:S(2)}, u32[]{:S(2)}) collective-permute-start(bf16[1,32,1536]{2,1,0:T(8,128)(2,1)} %convert_bitcast_fusion.6), channel_id=1, source_target_pairs={{0,16},{16,0},{1,17},{17,1},{2,18},{18,2},{3,19},{19,3},{4,20},{20... | collective-permute-start | bytes 294920 | tf_op jit(solution)/shard_map/ppermute | solution.py:98
  20.5 103.5 %collective-permute-start.39 = (bf16[1,256,1536]{2,1,0:T(8,128)(2,1)}, bf16[1,256,1536]{2,1,0:T(8,128)(2,1)}, u32[]{:S(2)}, u32[]{:S(2)}) collective-permute-start(bf16[1,256,1536]{2,1,0:T(8,128)(2,1)} %convert_element_type.212), channel_id=1, source_target_pairs={{0,16},{16,0},{1,17},{17,1},{2,18},{18,2},{3,19},{19,3},{4,20},{20... | collective-permute-start | bytes 2359304 | tf_op jit(solution)/shard_map/ppermute | solution.py:98
  23.9 586.3 %reduce-scatter.5.cloned.1.call-start = ((), (), s32[]{:S(2)}) async-start(), calls=%async_computation.5 | async-start | bytes 4866048 | tf_op jit(solution)/shard_map/reduce_scatter | solution.py:1215
  58.2 32.8 %collective-permute-start.9 = (bf16[1,2,2,2,1,48,1280]{6,5,3,2,1,4,0:T(8,128)(2,1)S(1)}, bf16[1,2,2,2,1,48,1280]{6,5,3,2,1,4,0:T(8,128)(2,1)S(1)}, u32[]{:S(2)}, u32[]{:S(2)}) collective-permute-start(bf16[1,2,2,2,1,48,1280]{6,5,3,2,1,4,0:T(8,128)(2,1)S(1)} %broadcast_select_fusion.5), channel_id=1, source_target_pairs={{0,16},{16,0},{1,17},{17,1},{2,18},{18,2},{3,19},{19,3},{4,20},{20... | collective-permute-start | bytes 2949128 | tf_op jit(solution)/shard_map/ppermute | solution.py:98
  59.8 32.7 %collective-permute-start.10 = (bf16[2,2,2,1,1,48,1280]{6,5,2,1,0,4,3:T(8,128)(2,1)S(1)}, bf16[2,2,2,1,1,48,1280]{6,5,2,1,0,4,3:T(8,128)(2,1)S(1)}, u32[]{:S(2)}, u32[]{:S(2)}) collective-permute-start(bf16[2,2,2,1,1,48,1280]{6,5,2,1,0,4,3:T(8,128)(2,1)S(1)} %broadcast_select_fusion.4), channel_id=1, source_target_pairs={{0,2},{1,3},{2,0},{3,1},{4,6},{5,7},{6,4},{7,5},{8,10},{9,11},{10,... | collective-permute-start | bytes 2949128 | tf_op jit(solution)/shard_map/ppermute | solution.py:98
  61.4 29.5 %collective-permute-start.11 = (bf16[1,2,2,2,1,48,128]{6,5,3,2,1,4,0:T(8,128)(2,1)S(1)}, bf16[1,2,2,2,1,48,128]{6,5,3,2,1,4,0:T(8,128)(2,1)S(1)}, u32[]{:S(2)}, u32[]{:S(2)}) collective-permute-start(bf16[1,2,2,2,1,48,128]{6,5,3,2,1,4,0:T(8,128)(2,1)S(1)} %broadcast_select_fusion.21), channel_id=1, source_target_pairs={{0,16},{16,0},{1,17},{17,1},{2,18},{18,2},{3,19},{19,3},{4,20},{20... | collective-permute-start | bytes 294920 | tf_op jit(solution)/shard_map/ppermute | solution.py:98
  118.5 26.6 %collective-permute-start.15 = (bf16[1,64,512]{2,1,0:T(8,128)(2,1)}, bf16[1,64,512]{2,1,0:T(8,128)(2,1)}, u32[]{:S(2)}, u32[]{:S(2)}) collective-permute-start(bf16[1,64,512]{2,1,0:T(8,128)(2,1)} %broadcast_in_dim_reshape_squeeze.12), channel_id=1, source_target_pairs={{0,8},{1,9},{2,10},{3,11},{4,12},{5,13},{6,14},{7,15},{8,0},{9,1},... | collective-permute-start | bytes 196616 | tf_op jit(solution)/shard_map/ppermute | solution.py:98
  122.4 25.8 %collective-permute-start.20 = (bf16[1,64,512]{2,1,0:T(8,128)(2,1)}, bf16[1,64,512]{2,1,0:T(8,128)(2,1)}, u32[]{:S(2)}, u32[]{:S(2)}) collective-permute-start(bf16[1,64,512]{2,1,0:T(8,128)(2,1)} %broadcast_in_dim_reshape_squeeze.13), channel_id=1, source_target_pairs={{0,8},{1,9},{2,10},{3,11},{4,12},{5,13},{6,14},{7,15},{8,0},{9,1},... | collective-permute-start | bytes 196616 | tf_op jit(solution)/shard_map/ppermute | solution.py:98
  132.0 28.6 %collective-permute-start.44 = (bf16[1,2,2,2,48,128]{4,5,3,2,1,0:T(8,128)(2,1)}, bf16[1,2,2,2,48,128]{4,5,3,2,1,0:T(8,128)(2,1)}, u32[]{:S(2)}, u32[]{:S(2)}) collective-permute-start(bf16[1,2,2,2,48,128]{4,5,3,2,1,0:T(8,128)(2,1)} %get-tuple-element.511), channel_id=1, source_target_pairs={{0,8},{1,9},{2,10},{3,11},{4,12},{5,13},{6,14},{7,15},{8,0},{9,1},... | collective-permute-start | bytes 294920 | tf_op jit(solution)/shard_map/ppermute | solution.py:98
  193.8 21.0 %collective-permute-start.19 = (bf16[16,64,512]{2,1,0:T(8,128)(2,1)S(1)}, bf16[16,64,512]{2,1,0:T(8,128)(2,1)S(1)}, u32[]{:S(2)}, u32[]{:S(2)}) collective-permute-start(bf16[16,64,512]{2,1,0:T(8,128)(2,1)S(1)} %constant_dynamic-update-slice_fusion.9.kv0_ref), channel_id=1, source_target_pairs={{0,1},{1,0},{2,3},{3,2},{4,5},{5,4},{6,7},{7,6},{8,9},{9,8},{10,11... | collective-permute-start | bytes 3145736 | tf_op jit(solution)/shard_map/ppermute | solution.py:98
  204.2 82.5 %collective-permute-start.43 = (bf16[1,768,1024]{2,1,0:T(8,128)(2,1)}, bf16[1,768,1024]{2,1,0:T(8,128)(2,1)}, u32[]{:S(2)}, u32[]{:S(2)}) collective-permute-start(bf16[1,768,1024]{2,1,0:T(8,128)(2,1)} %convert_element_type.216), channel_id=1, source_target_pairs={{0,16},{16,0},{1,17},{17,1},{2,18},{18,2},{3,19},{19,3},{4,20},{20... | collective-permute-start | bytes 4718600 | tf_op jit(solution)/shard_map/ppermute | solution.py:98
  285.8 21.4 %collective-permute-start.52 = (bf16[8,64,1536]{2,1,0:T(8,128)(2,1)S(1)}, bf16[8,64,1536]{2,1,0:T(8,128)(2,1)S(1)}, u32[]{:S(2)}, u32[]{:S(2)}) collective-permute-start(bf16[8,64,1536]{2,1,0:T(8,128)(2,1)S(1)} %constant_dynamic-update-slice_fusion.51), channel_id=1, source_target_pairs={{0,1},{1,0},{2,3},{3,2},{4,5},{5,4},{6,7},{7,6},{8,9},{9,8},{10,11... | collective-permute-start | bytes 4718600 | tf_op jit(solution)/shard_map/ppermute | solution.py:98
  329.4 21.2 %collective-permute-start.50 = (bf16[4,64,1664]{2,1,0:T(8,128)(2,1)S(1)}, bf16[4,64,1664]{2,1,0:T(8,128)(2,1)S(1)}, u32[]{:S(2)}, u32[]{:S(2)}) collective-permute-start(bf16[4,64,1664]{2,1,0:T(8,128)(2,1)S(1)} %slice.348), channel_id=1, source_target_pairs={{0,2},{1,3},{2,0},{3,1},{4,6},{5,7},{6,4},{7,5},{8,10},{9,11},{10,... | collective-permute-start | bytes 2555912 | tf_op jit(solution)/shard_map/ppermute | solution.py:98
  334.3 20.9 %collective-permute-start.54 = (bf16[4,64,1664]{2,1,0:T(8,128)(2,1)S(1)}, bf16[4,64,1664]{2,1,0:T(8,128)(2,1)S(1)}, u32[]{:S(2)}, u32[]{:S(2)}) collective-permute-start(bf16[4,64,1664]{2,1,0:T(8,128)(2,1)S(1)} %slice.352), channel_id=1, source_target_pairs={{0,4},{1,5},{2,6},{3,7},{4,0},{5,1},{6,2},{7,3},{8,12},{9,13},{10,... | collective-permute-start | bytes 2555912 | tf_op jit(solution)/shard_map/ppermute | solution.py:98
  355.9 23.1 %collective-permute-start.56 = (bf16[2,64,1664]{2,1,0:T(8,128)(2,1)S(1)}, bf16[2,64,1664]{2,1,0:T(8,128)(2,1)S(1)}, u32[]{:S(2)}, u32[]{:S(2)}) collective-permute-start(bf16[2,64,1664]{2,1,0:T(8,128)(2,1)S(1)} %get-tuple-element.222), channel_id=1, source_target_pairs={{0,8},{1,9},{2,10},{3,11},{4,12},{5,13},{6,14},{7,15},{8,0},{9,1},... | collective-permute-start | bytes 1277960 | tf_op jit(solution)/shard_map/ppermute | solution.py:98
  397.2 271.1 %reduce-scatter.3.cloned.1.call-start = ((), (), s32[]{:S(2)}) async-start(), calls=%async_computation.4 | async-start | bytes 6684672 | tf_op jit(solution)/shard_map/reduce_scatter | solution.py:1212
  404.0 173.3 %collective-permute-start.100 = (bf16[768,1024]{1,0:T(8,128)(2,1)}, bf16[768,1024]{1,0:T(8,128)(2,1)}, u32[]{:S(2)}, u32[]{:S(2)}) collective-permute-start(bf16[768,1024]{1,0:T(8,128)(2,1)} %constant_dynamic-slice_fusion.1), channel_id=1, source_target_pairs={{0,16},{16,0},{1,17},{17,1},{2,18},{18,2},{3,19},{19,3},{4,20},{20... | collective-permute-start | bytes 4718600 | tf_op jit(solution)/shard_map/ppermute | solution.py:98
  405.7 190.4 %collective-permute-start.94 = (bf16[32,1536]{1,0:T(8,128)(2,1)}, bf16[32,1536]{1,0:T(8,128)(2,1)}, u32[]{:S(2)}, u32[]{:S(2)}) collective-permute-start(bf16[32,1536]{1,0:T(8,128)(2,1)} %constant_dynamic-slice_fusion.8), channel_id=1, source_target_pairs={{0,16},{16,0},{1,17},{17,1},{2,18},{18,2},{3,19},{19,3},{4,20},{20... | collective-permute-start | bytes 294920 | tf_op jit(solution)/shard_map/ppermute | solution.py:98
  413.4 22.0 %collective-permute-start.59 = (bf16[16,64,512]{2,1,0:T(8,128)(2,1)S(1)}, bf16[16,64,512]{2,1,0:T(8,128)(2,1)S(1)}, u32[]{:S(2)}, u32[]{:S(2)}) collective-permute-start(bf16[16,64,512]{2,1,0:T(8,128)(2,1)S(1)} %get-tuple-element.240), channel_id=1, source_target_pairs={{0,1},{1,0},{2,3},{3,2},{4,5},{5,4},{6,7},{7,6},{8,9},{9,8},{10,11... | collective-permute-start | bytes 3145736 | tf_op jit(solution)/shard_map/ppermute | solution.py:98
  417.8 39.5 %collective-permute-start.64 = (bf16[16,64,512]{2,1,0:T(8,128)(2,1)}, bf16[16,64,512]{2,1,0:T(8,128)(2,1)}, u32[]{:S(2)}, u32[]{:S(2)}) collective-permute-start(bf16[16,64,512]{2,1,0:T(8,128)(2,1)} %get-tuple-element.249), channel_id=1, source_target_pairs={{0,1},{1,0},{2,3},{3,2},{4,5},{5,4},{6,7},{7,6},{8,9},{9,8},{10,11... | collective-permute-start | bytes 3145736 | tf_op jit(solution)/shard_map/ppermute | solution.py:98
  436.6 25.0 %collective-permute-start.60 = (bf16[8,64,512]{2,1,0:T(8,128)(2,1)}, bf16[8,64,512]{2,1,0:T(8,128)(2,1)}, u32[]{:S(2)}, u32[]{:S(2)}) collective-permute-start(bf16[8,64,512]{2,1,0:T(8,128)(2,1)} %slice.368), channel_id=1, source_target_pairs={{0,16},{16,0},{1,17},{17,1},{2,18},{18,2},{3,19},{19,3},{4,20},{20... | collective-permute-start | bytes 1572872 | tf_op jit(solution)/shard_map/ppermute | solution.py:98
  483.4 21.1 %collective-permute-start.65 = (bf16[16,64,512]{2,1,0:T(8,128)(2,1)S(1)}, bf16[16,64,512]{2,1,0:T(8,128)(2,1)}, u32[]{:S(2)}, u32[]{:S(2)}) collective-permute-start(bf16[16,64,512]{2,1,0:T(8,128)(2,1)S(1)} %copy-done.39), channel_id=1, source_target_pairs={{0,1},{1,0},{2,3},{3,2},{4,5},{5,4},{6,7},{7,6},{8,9},{9,8},{10,11... | collective-permute-start | bytes 3145736 | tf_op jit(solution)/shard_map/ppermute | solution.py:98
  483.4 22.8 %collective-permute-start.74 = (bf16[16,64,512]{2,1,0:T(8,128)(2,1)}, bf16[16,64,512]{2,1,0:T(8,128)(2,1)}, u32[]{:S(2)}, u32[]{:S(2)}) collective-permute-start(bf16[16,64,512]{2,1,0:T(8,128)(2,1)} %copy-done.40), channel_id=1, source_target_pairs={{0,1},{1,0},{2,3},{3,2},{4,5},{5,4},{6,7},{7,6},{8,9},{9,8},{10,11... | collective-permute-start | bytes 3145736 | tf_op jit(solution)/shard_map/ppermute | solution.py:98
  503.2 89.0 %collective-permute-start.101 = (bf16[256,1536]{1,0:T(8,128)(2,1)}, bf16[256,1536]{1,0:T(8,128)(2,1)}, u32[]{:S(2)}, u32[]{:S(2)}) collective-permute-start(bf16[256,1536]{1,0:T(8,128)(2,1)} %constant_dynamic-slice_fusion), channel_id=1, source_target_pairs={{0,16},{16,0},{1,17},{17,1},{2,18},{18,2},{3,19},{19,3},{4,20},{20... | collective-permute-start | bytes 2359304 | tf_op jit(solution)/shard_map/ppermute | solution.py:98
  506.2 25.8 %collective-permute-start.67 = (bf16[8,64,512]{2,1,0:T(8,128)(2,1)S(1)}, bf16[8,64,512]{2,1,0:T(8,128)(2,1)S(1)}, u32[]{:S(2)}, u32[]{:S(2)}) collective-permute-start(bf16[8,64,512]{2,1,0:T(8,128)(2,1)S(1)} %get-tuple-element.253), channel_id=1, source_target_pairs={{0,16},{16,0},{1,17},{17,1},{2,18},{18,2},{3,19},{19,3},{4,20},{20... | collective-permute-start | bytes 1572872 | tf_op jit(solution)/shard_map/ppermute | solution.py:98
  510.2 23.9 %collective-permute-start.75 = (bf16[8,64,512]{2,1,0:T(8,128)(2,1)S(1)}, bf16[8,64,512]{2,1,0:T(8,128)(2,1)S(1)}, u32[]{:S(2)}, u32[]{:S(2)}) collective-permute-start(bf16[8,64,512]{2,1,0:T(8,128)(2,1)S(1)} %get-tuple-element.269), channel_id=1, source_target_pairs={{0,2},{1,3},{2,0},{3,1},{4,6},{5,7},{6,4},{7,5},{8,10},{9,11},{10,... | collective-permute-start | bytes 1572872 | tf_op jit(solution)/shard_map/ppermute | solution.py:98
  569.4 36.3 %collective-permute-start.89 = (bf16[2,2,2,2,1,48,1280]{6,5,4,3,2,1,0:T(8,128)(2,1)}, bf16[2,2,2,2,1,48,1280]{6,5,4,3,2,1,0:T(8,128)(2,1)S(1)}, u32[]{:S(2)}, u32[]{:S(2)}) collective-permute-start(bf16[2,2,2,2,1,48,1280]{6,5,4,3,2,1,0:T(8,128)(2,1)} %constant_dynamic-slice_fusion.13), channel_id=1, source_target_pairs={{0,1},{1,0},{2,3},{3,2},{4,5},{5,4},{6,7},{7,6},{8,9},{9,8},{10,11... | collective-permute-start | bytes 5898248 | tf_op jit(solution)/shard_map/ppermute | solution.py:98
  577.4 30.2 %collective-permute-start.84 = (bf16[2,2,2,2,1,48,1280]{6,5,4,3,2,1,0:T(8,128)(2,1)S(1)}, bf16[2,2,2,2,1,48,1280]{6,5,4,3,2,1,0:T(8,128)(2,1)S(1)}, u32[]{:S(2)}, u32[]{:S(2)}) collective-permute-start(bf16[2,2,2,2,1,48,1280]{6,5,4,3,2,1,0:T(8,128)(2,1)S(1)} %constant_dynamic-slice_fusion.18), channel_id=1, source_target_pairs={{0,1},{1,0},{2,3},{3,2},{4,5},{5,4},{6,7},{7,6},{8,9},{9,8},{10,11... | collective-permute-start | bytes 5898248 | tf_op jit(solution)/shard_map/ppermute | solution.py:98
  607.1 22.7 %collective-permute-start.90 = (bf16[2,2,2,1,1,48,1280]{6,5,4,3,2,1,0:T(8,128)(2,1)}, bf16[2,2,2,1,1,48,1280]{6,5,4,3,2,1,0:T(8,128)(2,1)S(1)}, u32[]{:S(2)}, u32[]{:S(2)}) collective-permute-start(bf16[2,2,2,1,1,48,1280]{6,5,4,3,2,1,0:T(8,128)(2,1)} %constant_dynamic-slice_fusion.12), channel_id=1, source_target_pairs={{0,2},{1,3},{2,0},{3,1},{4,6},{5,7},{6,4},{7,5},{8,10},{9,11},{10,... | collective-permute-start | bytes 2949128 | tf_op jit(solution)/shard_map/ppermute | solution.py:98
  608.8 23.1 %collective-permute-start.85 = (bf16[1,2,2,2,1,48,1280]{6,5,4,3,2,1,0:T(8,128)(2,1)}, bf16[1,2,2,2,1,48,1280]{6,5,4,3,2,1,0:T(8,128)(2,1)}, u32[]{:S(2)}, u32[]{:S(2)}) collective-permute-start(bf16[1,2,2,2,1,48,1280]{6,5,4,3,2,1,0:T(8,128)(2,1)} %constant_dynamic-slice_fusion.17), channel_id=1, source_target_pairs={{0,16},{16,0},{1,17},{17,1},{2,18},{18,2},{3,19},{19,3},{4,20},{20... | collective-permute-start | bytes 2949128 | tf_op jit(solution)/shard_map/ppermute | solution.py:98
  (285 other events, 2637.2 us)
Sparse Core Ops, SparseCore 0:
  11.6 76.6 all-gather.2
  91.1 83.0 all-gather.4
  397.3 112.2 reduce-scatter.4
  513.9 87.0 reduce-scatter.2

commit v3 on v2

--- a/solution.py
+++ b/solution.py
@@ -159,18 +159,7 @@
 
 
 def transpose_blk(values):
-    places = axis_bits("blk")
-    shape = values.shape
-    values = values.reshape((2,) * len(places) + shape[1:])
-    for place, step in enumerate(places):
-        bit = own_bit(step)
-        mine = lax.dynamic_slice_in_dim(values, bit, 1, place)
-        theirs = lax.dynamic_slice_in_dim(values, 1 - bit, 1, place)
-        index = [1] * values.ndim
-        index[place] = 2
-        here = lax.broadcasted_iota(jnp.int32, index, place) == bit
-        values = jnp.where(here, mine, swap(theirs, step))
-    return values.reshape(shape)
+    return lax.all_to_all(values, "blk", split_axis=0, concat_axis=0, tiled=True)
 
 
 def gather_rows(pieces, orders):
@@ -1280,7 +1269,7 @@
     pair_sums = scatter_relative(
         [item[1:] for part in back for item in part],
         [order for s in range(seqs) for order in all_orders],
-        WAVES_KV,
+        None,
     )
     grad_halves = [
         jnp.concatenate(

time: 723 us -> 716 us (level)
  waiting for transfers between devices: 275 us -> 251 us
  starting transfers between devices: 103 us -> 111 us
    ppermute x107 -> x99, waiting for transfers between devices: 272 us -> 245 us  [swap(): return lax.ppermute(values, name, [(i, i ^ bit) for i in range(size)])]
    all_to_all x0 -> x2, starting transfers between devices: none -> 9.14 us  [transpose_blk(): lax.all_to_all(values, 'blk', split_axis=0, concat_axis=0, tiled=True)]
    unnamed x440 -> x448, local copies, waits for them, and re-layouts: 29.8 us -> 36.2 us
    ppermute x107 -> x99, starting transfers between devices: 98.7 us -> 97 us  [swap(): return lax.ppermute(values, name, [(i, i ^ bit) for i in range(size)])]
  transfers between devices with their start and end apart: 113 -> 107, of which waited for: 54 -> 56; matrix products, arithmetic and copies ran while one was open for 26% -> 25% of each run, Pallas kernels for 11% -> 12%
where the time goes in v3:
time: 716 us; the launch traced here: 707 us
  waiting for transfers between devices  251 us (35%)
  other arithmetic  112 us (16%)
  starting transfers between devices  111 us (16%)
  Pallas kernels  84.2 us (12%)
  local copies, waits for them, and re-layouts  79.3 us (11%)
  matrix products  44.9 us (6%)
  between operations  24.7 us (3%)
    ppermute x99, waiting for transfers between devices, swap(): return lax.ppermute(values, name, [(i, i ^ bit) for i in range(size)])  245 us
    ppermute x99, starting transfers between devices, swap(): return lax.ppermute(values, name, [(i, i ^ bit) for i in range(size)])  97 us
    unnamed x448, local copies, waits for them, and re-layouts  36.2 us
    pallas_call x2, Pallas kernels, run_expert(): pl.pallas_call(functools.partial(expert_kernel, blocks), grid_spec=pltpu....  32.1 us
    pallas_call x4, Pallas kernels, attend_back(): pl.pallas_call(attend_back_kernel, grid=(groups,), in_specs=[wide, kv, kv...  19.4 us
    dot_general x7, matrix products, back_dot(): lax.dot_general(left, right, (((1,), (1,)), ((), ())), preferred_element_...  19.2 us
    mul x8, other arithmetic, adam_update(): -learn_rate  17.9 us
    add x28, other arithmetic, act(): total = kept + swap(sent, step)  14.6 us
  transfers between devices with their start and end apart: 107, of which 56 were waited for; matrix products, arithmetic and copies ran while one was open for 25% of the time, Pallas kernels for 12%

profile of v3, /device:TPU:0, one launch (start us, length us, event | category | flops | bytes accessed | tf_op | source)
XLA Modules:
  0.0 707.4 jit_solution(4146003587607671148)
XLA Ops:
  31.2 11.8 %collective-permute-done.5 = bf16[1,2,1,1,1,48,128]{6,5,1,4,3,2,0:T(8,128)(2,1)S(1)} collective-permute-done((bf16[1,2,1,1,1,48,128]{6,5,1,4,3,2,0:T(8,128)(2,1)S(1)}, bf16[1,2,1,1,1,48,128]{6,5,1,4,3,2,0:T(8,128)(2,1)S(1)}, u32[]{:S(2)}, u32[]{:S(2)}) %collective-permute-start.5) | collective-permute-done | bytes 24608 | tf_op jit(solution)/shard_map/ppermute | solution.py:98
  46.9 10.3 %collective-permute-done.8 = bf16[1,2,2,1,1,48,128]{6,5,2,1,4,3,0:T(8,128)(2,1)S(1)} collective-permute-done((bf16[1,2,2,1,1,48,128]{6,5,2,1,4,3,0:T(8,128)(2,1)S(1)}, bf16[1,2,2,1,1,48,128]{6,5,2,1,4,3,0:T(8,128)(2,1)S(1)}, u32[]{:S(2)}, u32[]{:S(2)}) %collective-permute-start.8) | collective-permute-done | bytes 49184 | tf_op jit(solution)/shard_map/ppermute | solution.py:98
  62.8 29.0 %collective-permute-done.11 = bf16[1,2,2,2,1,48,128]{6,5,3,2,1,4,0:T(8,128)(2,1)S(1)} collective-permute-done((bf16[1,2,2,2,1,48,128]{6,5,3,2,1,4,0:T(8,128)(2,1)S(1)}, bf16[1,2,2,2,1,48,128]{6,5,3,2,1,4,0:T(8,128)(2,1)S(1)}, u32[]{:S(2)}, u32[]{:S(2)}) %collective-permute-start.11) | collective-permute-done | bytes 98336 | tf_op jit(solution)/shard_map/ppermute | solution.py:98
  106.6 5.1 broadcast_select_fusion
  123.9 8.1 %collective-permute-done.15 = bf16[1,64,512]{2,1,0:T(8,128)(2,1)} collective-permute-done((bf16[1,64,512]{2,1,0:T(8,128)(2,1)S(1)}, bf16[1,64,512]{2,1,0:T(8,128)(2,1)}, u32[]{:S(2)}, u32[]{:S(2)}) %collective-permute-start.15) | collective-permute-done | bytes 65568 | tf_op jit(solution)/shard_map/ppermute | solution.py:98
  144.8 4.9 all-to-all-start
  154.7 6.3 collective-permute-done.21
  178.2 4.6 collective-permute-done.18
  210.0 5.7 collective-permute-done.28
  225.2 4.3 multiply_reduce_fusion.11
  250.9 9.1 %fusion = f32[2048,640]{1,0:T(8,128)} fusion(bf16[2048,1664]{1,0:T(8,128)(2,1)} %all-gather.5.cloned.1.call-done, bf16[64,1536]{1,0:T(8,128)(2,1)S(1)} %copy-done.151, bf16[512,1536]{1,0:T(8,128)(2,1)} %bitcast_select_fusion.1), kind=kOutput, calls=%fused_computation.3 | convolution fusion | flops 4033413120 | bytes 13303808 | tf_op jit(solution)/shard_map/dot_general | solution.py:48
  260.0 9.7 %collective-permute-done.38 = bf16[2,64,1536]{2,1,0:T(8,128)(2,1)S(1)} collective-permute-done((bf16[2,64,1536]{2,1,0:T(8,128)(2,1)S(1)}, bf16[2,64,1536]{2,1,0:T(8,128)(2,1)S(1)}, u32[]{:S(2)}, u32[]{:S(2)}) %collective-permute-start.38) | collective-permute-done | bytes 393248 | tf_op jit(solution)/shard_map/ppermute | solution.py:98
  273.7 13.5 %collective-permute-done.41 = bf16[4,64,1536]{2,1,0:T(8,128)(2,1)S(1)} collective-permute-done((bf16[4,64,1536]{2,1,0:T(8,128)(2,1)S(1)}, bf16[4,64,1536]{2,1,0:T(8,128)(2,1)S(1)}, u32[]{:S(2)}, u32[]{:S(2)}) %collective-permute-start.41) | collective-permute-done | bytes 786464 | tf_op jit(solution)/shard_map/ppermute | solution.py:98
  293.8 15.8 %expert.2 = (bf16[512,1664]{1,0:T(8,128)(2,1)}, bf16[512,1664]{1,0:T(8,128)(2,1)}, bf16[16,64,640]{2,1,0:T(8,128)(2,1)S(1)}, bf16[1024,1152]{1,0:T(8,128)(2,1)}) custom-call(s32[16]{0:T(128)S(1)} %copy-done.34, bf16[512,1536]{1,0:T(8,128)(2,1)S(1)} %bitcast.246, bf16[512,1536]{1,0:T(8,128)(2,1)S(1)} %bitcast.248, ...), custom_call_target="tpu_custom_call" | custom-call | flops 7247757312 | bytes 12582912 | tf_op jit(solution)/shard_map/expert/pallas_call | solution.py:485
  310.2 16.3 %expert.3 = (bf16[512,1664]{1,0:T(8,128)(2,1)}, bf16[512,1664]{1,0:T(8,128)(2,1)}, bf16[16,64,640]{2,1,0:T(8,128)(2,1)S(1)}, bf16[1024,1152]{1,0:T(8,128)(2,1)}) custom-call(s32[16]{0:T(128)S(1)} %copy-done.35, bf16[512,1536]{1,0:T(8,128)(2,1)S(1)} %bitcast.244, bf16[512,1536]{1,0:T(8,128)(2,1)S(1)} %bitcast.250, ...), custom_call_target="tpu_custom_call" | custom-call | flops 7247757312 | bytes 12582912 | tf_op jit(solution)/shard_map/expert/pallas_call | solution.py:485
  336.8 13.0 %outer_experts.1 = bf16[1536,1152]{1,0:T(8,128)(2,1)} custom-call(bf16[512,1536]{1,0:T(8,128)(2,1)S(1)} %bitcast.247, bf16[512,1536]{1,0:T(8,128)(2,1)S(1)} %bitcast.249, bf16[512,1536]{1,0:T(8,128)(2,1)S(1)} %bitcast.245, bf16[512,1536]{1,0:T(8,128)(2,1)} %bitcast.251, bf16[1024,1152]{1,0:T(8,128)(2,1)} %get-tuple-element.197.right0_ref, ...), custom_call_target="tpu_custom_call" | custom-call | flops 7247757312 | bytes 14548992 | tf_op jit(solution)/shard_map/outer_experts/pallas_call | solution.py:538
  360.9 8.3 %outer_acts.1 = bf16[640,1536]{1,0:T(8,128)(2,1)S(1)} custom-call(bf16[16,64,640]{2,1,0:T(8,128)(2,1)S(1)} %copy-done.37, bf16[16,64,640]{2,1,0:T(8,128)(2,1)S(1)} %copy-done.39, bf16[16,2,64,1664]{3,2,1,0:T(8,128)(2,1)} %bitcast.270), custom_call_target="tpu_custom_call" | custom-call | flops 4026531840 | bytes 10878976 | tf_op jit(solution)/shard_map/outer_acts/pallas_call | solution.py:569
  369.2 7.9 %collective-permute-done.51 = bf16[2,64,1664]{2,1,0:T(8,128)(2,1)S(1)} collective-permute-done((bf16[2,64,1664]{2,1,0:T(8,128)(2,1)S(1)}, bf16[2,64,1664]{2,1,0:T(8,128)(2,1)S(1)}, u32[]{:S(2)}, u32[]{:S(2)}) %collective-permute-start.51) | collective-permute-done | bytes 426016 | tf_op jit(solution)/shard_map/ppermute | solution.py:98
  413.8 5.2 attend_back.5
  421.4 5.3 attend_back.4
  432.9 5.3 attend_back.7
  480.6 5.7 collective-permute-done.56
  489.4 5.8 collective-permute-done.71
  495.3 12.2 %collective-permute-done.66 = bf16[8,64,512]{2,1,0:T(8,128)(2,1)S(1)} collective-permute-done((bf16[8,64,512]{2,1,0:T(8,128)(2,1)S(1)}, bf16[8,64,512]{2,1,0:T(8,128)(2,1)S(1)}, u32[]{:S(2)}, u32[]{:S(2)}) %collective-permute-start.66) | collective-permute-done | bytes 524320 | tf_op jit(solution)/shard_map/ppermute | solution.py:98
  507.7 5.5 collective-permute-done.62
  568.0 7.8 %collective-permute-done.88 = bf16[1,2,2,2,1,48,128]{5,6,4,3,2,1,0:T(8,128)(2,1)S(1)} collective-permute-done((bf16[1,2,2,2,1,48,128]{5,6,4,3,2,1,0:T(8,128)(2,1)S(1)}, bf16[1,2,2,2,1,48,128]{5,6,4,3,2,1,0:T(8,128)(2,1)S(1)}, u32[]{:S(2)}, u32[]{:S(2)}) %collective-permute-start.88) | collective-permute-done | bytes 98336 | tf_op jit(solution)/shard_map/ppermute | solution.py:98
  576.0 4.6 fusion.6
  597.1 18.3 %collective-permute-done.82 = bf16[2,2,2,1,1,48,1280]{6,5,4,3,2,1,0:T(8,128)(2,1)S(1)} collective-permute-done((bf16[2,2,2,1,1,48,1280]{6,5,4,3,2,1,0:T(8,128)(2,1)S(1)}, bf16[2,2,2,1,1,48,1280]{6,5,4,3,2,1,0:T(8,128)(2,1)S(1)}, u32[]{:S(2)}, u32[]{:S(2)}) %collective-permute-start.82) | collective-permute-done | bytes 983072 | tf_op jit(solution)/shard_map/ppermute | solution.py:98
  620.2 7.6 %collective-permute-done.83 = bf16[1,2,2,1,1,48,1280]{6,5,4,3,2,1,0:T(8,128)(2,1)S(1)} collective-permute-done((bf16[1,2,2,1,1,48,1280]{6,5,4,3,2,1,0:T(8,128)(2,1)S(1)}, bf16[1,2,2,1,1,48,1280]{6,5,4,3,2,1,0:T(8,128)(2,1)S(1)}, u32[]{:S(2)}, u32[]{:S(2)}) %collective-permute-start.83) | collective-permute-done | bytes 491552 | tf_op jit(solution)/shard_map/ppermute | solution.py:98
  630.6 6.5 collective-permute-done.84
  640.0 4.4 collective-permute-start.80
  682.4 7.8 %add_multiply_fusion = (f32[1,768,1024]{2,1,0:T(8,128)}, f32[1,768,1024]{2,1,0:T(8,128)}, f32[1,768,1024]{2,1,0:T(8,128)}) fusion(f32[1,768,1024]{2,1,0:T(8,128)S(1)} %copy-done.61, f32[]{:T(128)S(6)} %div.240, bf16[768,1024]{1,0:T(8,128)(2,1)} %collective-permute-done.92, bf16[1536,1024]{1,0:T(8,128)(2,1)} %copy-done.62, s32[]{:T(128)S(6)} %select_n.437, ...), kind=kLoop, calls=%fused_computation.19 | loop fusion | flops 14155776 | bytes 22020104 | tf_op jit(solution)/shard_map/mul | solution.py:78
  (930 shorter events, 397.1 us)
Async XLA Ops:
  7.3 217.9 %all-gather.3.cloned.1.call-start = ((), (), s32[]{:S(2)}) async-start(), calls=%async_computation.4 | async-start | bytes 4866048 | tf_op jit(solution)/shard_map/all_gather | solution.py:1049
  9.1 241.7 %all-gather.5.cloned.1.call-start = ((), (), s32[]{:S(2)}) async-start(), calls=%async_computation.5 | async-start | bytes 7241728 | tf_op jit(solution)/shard_map/all_gather | solution.py:1093
  18.1 169.4 %collective-permute-start.40 = (bf16[1,32,1536]{2,1,0:T(8,128)(2,1)}, bf16[1,32,1536]{2,1,0:T(8,128)(2,1)}, u32[]{:S(2)}, u32[]{:S(2)}) collective-permute-start(bf16[1,32,1536]{2,1,0:T(8,128)(2,1)} %convert_bitcast_fusion.5), channel_id=1, source_target_pairs={{0,16},{16,0},{1,17},{17,1},{2,18},{18,2},{3,19},{19,3},{4,20},{20... | collective-permute-start | bytes 294920 | tf_op jit(solution)/shard_map/ppermute | solution.py:98
  20.5 170.3 %collective-permute-start.39 = (bf16[1,256,1536]{2,1,0:T(8,128)(2,1)}, bf16[1,256,1536]{2,1,0:T(8,128)(2,1)}, u32[]{:S(2)}, u32[]{:S(2)}) collective-permute-start(bf16[1,256,1536]{2,1,0:T(8,128)(2,1)} %convert_element_type.216), channel_id=1, source_target_pairs={{0,16},{16,0},{1,17},{17,1},{2,18},{18,2},{3,19},{19,3},{4,20},{20... | collective-permute-start | bytes 2359304 | tf_op jit(solution)/shard_map/ppermute | solution.py:98
  58.6 33.3 %collective-permute-start.9 = (bf16[1,2,2,2,1,48,1280]{6,5,3,2,1,4,0:T(8,128)(2,1)}, bf16[1,2,2,2,1,48,1280]{6,5,3,2,1,4,0:T(8,128)(2,1)}, u32[]{:S(2)}, u32[]{:S(2)}) collective-permute-start(bf16[1,2,2,2,1,48,1280]{6,5,3,2,1,4,0:T(8,128)(2,1)} %broadcast_select_fusion.5), channel_id=1, source_target_pairs={{0,16},{16,0},{1,17},{17,1},{2,18},{18,2},{3,19},{19,3},{4,20},{20... | collective-permute-start | bytes 2949128 | tf_op jit(solution)/shard_map/ppermute | solution.py:98
  60.2 34.8 %collective-permute-start.10 = (bf16[2,2,2,1,1,48,1280]{6,5,2,1,0,4,3:T(8,128)(2,1)S(1)}, bf16[2,2,2,1,1,48,1280]{6,5,2,1,0,4,3:T(8,128)(2,1)}, u32[]{:S(2)}, u32[]{:S(2)}) collective-permute-start(bf16[2,2,2,1,1,48,1280]{6,5,2,1,0,4,3:T(8,128)(2,1)S(1)} %broadcast_select_fusion.4), channel_id=1, source_target_pairs={{0,2},{1,3},{2,0},{3,1},{4,6},{5,7},{6,4},{7,5},{8,10},{9,11},{10,... | collective-permute-start | bytes 2949128 | tf_op jit(solution)/shard_map/ppermute | solution.py:98
  61.9 29.9 %collective-permute-start.11 = (bf16[1,2,2,2,1,48,128]{6,5,3,2,1,4,0:T(8,128)(2,1)S(1)}, bf16[1,2,2,2,1,48,128]{6,5,3,2,1,4,0:T(8,128)(2,1)S(1)}, u32[]{:S(2)}, u32[]{:S(2)}) collective-permute-start(bf16[1,2,2,2,1,48,128]{6,5,3,2,1,4,0:T(8,128)(2,1)S(1)} %broadcast_select_fusion.13), channel_id=1, source_target_pairs={{0,16},{16,0},{1,17},{17,1},{2,18},{18,2},{3,19},{19,3},{4,20},{20... | collective-permute-start | bytes 294920 | tf_op jit(solution)/shard_map/ppermute | solution.py:98
  137.2 23.7 %collective-permute-start.21 = (bf16[2,64,512]{2,1,0:T(8,128)(2,1)}, bf16[2,64,512]{2,1,0:T(8,128)(2,1)}, u32[]{:S(2)}, u32[]{:S(2)}) collective-permute-start(bf16[2,64,512]{2,1,0:T(8,128)(2,1)} %get-tuple-element.493), channel_id=1, source_target_pairs={{0,4},{1,5},{2,6},{3,7},{4,0},{5,1},{6,2},{7,3},{8,12},{9,13},{10,... | collective-permute-start | bytes 393224 | tf_op jit(solution)/shard_map/ppermute | solution.py:98
  144.8 51.6 %all-to-all-start = ((bf16[16,48,128]{2,1,0:T(8,128)(2,1)}), bf16[16,48,128]{2,1,0:T(8,128)(2,1)}, u32[]{:S(2)}, u32[]{:S(2)}) async-start(bf16[16,48,128]{2,1,0:T(8,128)(2,1)} %copy.243), calls=%async_computation | async-start | bytes 393216 | tf_op jit(solution)/shard_map/all_to_all | solution.py:162
  149.7 500.3 %reduce-scatter.5.cloned.1.call-start = ((), (), s32[]{:S(2)}) async-start(), calls=%async_computation.7 | async-start | bytes 4866048 | tf_op jit(solution)/shard_map/reduce_scatter | solution.py:1204
  187.4 28.2 %collective-permute-start.19 = (bf16[16,64,512]{2,1,0:T(8,128)(2,1)S(1)}, bf16[16,64,512]{2,1,0:T(8,128)(2,1)}, u32[]{:S(2)}, u32[]{:S(2)}) collective-permute-start(bf16[16,64,512]{2,1,0:T(8,128)(2,1)S(1)} %constant_dynamic-update-slice_fusion.9.kv0_ref), channel_id=1, source_target_pairs={{0,1},{1,0},{2,3},{3,2},{4,5},{5,4},{6,7},{7,6},{8,9},{9,8},{10,11... | collective-permute-start | bytes 3145736 | tf_op jit(solution)/shard_map/ppermute | solution.py:98
  187.5 28.1 %collective-permute-start.24 = (bf16[16,64,512]{2,1,0:T(8,128)(2,1)S(1)}, bf16[16,64,512]{2,1,0:T(8,128)(2,1)S(1)}, u32[]{:S(2)}, u32[]{:S(2)}) collective-permute-start(bf16[16,64,512]{2,1,0:T(8,128)(2,1)S(1)} %constant_dynamic-update-slice_fusion.23.kv0_ref), channel_id=1, source_target_pairs={{0,1},{1,0},{2,3},{3,2},{4,5},{5,4},{6,7},{7,6},{8,9},{9,8},{10,11... | collective-permute-start | bytes 3145736 | tf_op jit(solution)/shard_map/ppermute | solution.py:98
  206.5 83.2 %collective-permute-start.43 = (bf16[1,768,1024]{2,1,0:T(8,128)(2,1)}, bf16[1,768,1024]{2,1,0:T(8,128)(2,1)}, u32[]{:S(2)}, u32[]{:S(2)}) collective-permute-start(bf16[1,768,1024]{2,1,0:T(8,128)(2,1)} %convert_element_type.220), channel_id=1, source_target_pairs={{0,16},{16,0},{1,17},{17,1},{2,18},{18,2},{3,19},{19,3},{4,20},{20... | collective-permute-start | bytes 4718600 | tf_op jit(solution)/shard_map/ppermute | solution.py:98
  216.8 21.2 %collective-permute-start.34 = (bf16[16,64,512]{2,1,0:T(8,128)(2,1)S(1)}, bf16[16,64,512]{2,1,0:T(8,128)(2,1)}, u32[]{:S(2)}, u32[]{:S(2)}) collective-permute-start(bf16[16,64,512]{2,1,0:T(8,128)(2,1)S(1)} %constant_dynamic-update-slice_fusion.44.kv0_ref), channel_id=1, source_target_pairs={{0,1},{1,0},{2,3},{3,2},{4,5},{5,4},{6,7},{7,6},{8,9},{9,8},{10,11... | collective-permute-start | bytes 3145736 | tf_op jit(solution)/shard_map/ppermute | solution.py:98
  288.7 21.4 %collective-permute-start.48 = (bf16[8,64,1536]{2,1,0:T(8,128)(2,1)S(1)}, bf16[8,64,1536]{2,1,0:T(8,128)(2,1)S(1)}, u32[]{:S(2)}, u32[]{:S(2)}) collective-permute-start(bf16[8,64,1536]{2,1,0:T(8,128)(2,1)S(1)} %constant_dynamic-update-slice_fusion.51), channel_id=1, source_target_pairs={{0,1},{1,0},{2,3},{3,2},{4,5},{5,4},{6,7},{7,6},{8,9},{9,8},{10,11... | collective-permute-start | bytes 4718600 | tf_op jit(solution)/shard_map/ppermute | solution.py:98
  332.4 21.4 %collective-permute-start.46 = (bf16[4,64,1664]{2,1,0:T(8,128)(2,1)S(1)}, bf16[4,64,1664]{2,1,0:T(8,128)(2,1)S(1)}, u32[]{:S(2)}, u32[]{:S(2)}) collective-permute-start(bf16[4,64,1664]{2,1,0:T(8,128)(2,1)S(1)} %slice.348), channel_id=1, source_target_pairs={{0,2},{1,3},{2,0},{3,1},{4,6},{5,7},{6,4},{7,5},{8,10},{9,11},{10,... | collective-permute-start | bytes 2555912 | tf_op jit(solution)/shard_map/ppermute | solution.py:98
  358.2 20.9 %collective-permute-start.52 = (bf16[2,64,1664]{2,1,0:T(8,128)(2,1)S(1)}, bf16[2,64,1664]{2,1,0:T(8,128)(2,1)S(1)}, u32[]{:S(2)}, u32[]{:S(2)}) collective-permute-start(bf16[2,64,1664]{2,1,0:T(8,128)(2,1)S(1)} %get-tuple-element.202), channel_id=1, source_target_pairs={{0,8},{1,9},{2,10},{3,11},{4,12},{5,13},{6,14},{7,15},{8,0},{9,1},... | collective-permute-start | bytes 1277960 | tf_op jit(solution)/shard_map/ppermute | solution.py:98
  405.3 42.1 %collective-permute-start.75 = (bf16[768,128]{1,0:T(8,128)(2,1)}, bf16[768,128]{1,0:T(8,128)(2,1)}, u32[]{:S(2)}, u32[]{:S(2)}) collective-permute-start(bf16[768,128]{1,0:T(8,128)(2,1)} %constant_dynamic-slice_fusion.19), channel_id=1, source_target_pairs={{0,16},{16,0},{1,17},{17,1},{2,18},{18,2},{3,19},{19,3},{4,20},{20... | collective-permute-start | bytes 589832 | tf_op jit(solution)/shard_map/ppermute | solution.py:98
  407.6 160.3 %collective-permute-start.92 = (bf16[768,1024]{1,0:T(8,128)(2,1)}, bf16[768,1024]{1,0:T(8,128)(2,1)}, u32[]{:S(2)}, u32[]{:S(2)}) collective-permute-start(bf16[768,1024]{1,0:T(8,128)(2,1)} %constant_dynamic-slice_fusion.1), channel_id=1, source_target_pairs={{0,16},{16,0},{1,17},{17,1},{2,18},{18,2},{3,19},{19,3},{4,20},{20... | collective-permute-start | bytes 4718600 | tf_op jit(solution)/shard_map/ppermute | solution.py:98
  419.0 36.3 %collective-permute-start.60 = (bf16[16,64,512]{2,1,0:T(8,128)(2,1)}, bf16[16,64,512]{2,1,0:T(8,128)(2,1)}, u32[]{:S(2)}, u32[]{:S(2)}) collective-permute-start(bf16[16,64,512]{2,1,0:T(8,128)(2,1)} %get-tuple-element.225), channel_id=1, source_target_pairs={{0,1},{1,0},{2,3},{3,2},{4,5},{5,4},{6,7},{7,6},{8,9},{9,8},{10,11... | collective-permute-start | bytes 3145736 | tf_op jit(solution)/shard_map/ppermute | solution.py:98
  427.6 31.7 %collective-permute-start.55 = (bf16[16,64,512]{2,1,0:T(8,128)(2,1)}, bf16[16,64,512]{2,1,0:T(8,128)(2,1)}, u32[]{:S(2)}, u32[]{:S(2)}) collective-permute-start(bf16[16,64,512]{2,1,0:T(8,128)(2,1)} %get-tuple-element.220), channel_id=1, source_target_pairs={{0,1},{1,0},{2,3},{3,2},{4,5},{5,4},{6,7},{7,6},{8,9},{9,8},{10,11... | collective-permute-start | bytes 3145736 | tf_op jit(solution)/shard_map/ppermute | solution.py:98
  438.1 35.7 %collective-permute-start.70 = (bf16[16,64,512]{2,1,0:T(8,128)(2,1)}, bf16[16,64,512]{2,1,0:T(8,128)(2,1)}, u32[]{:S(2)}, u32[]{:S(2)}) collective-permute-start(bf16[16,64,512]{2,1,0:T(8,128)(2,1)} %get-tuple-element.235), channel_id=1, source_target_pairs={{0,1},{1,0},{2,3},{3,2},{4,5},{5,4},{6,7},{7,6},{8,9},{9,8},{10,11... | collective-permute-start | bytes 3145736 | tf_op jit(solution)/shard_map/ppermute | solution.py:98
  447.4 28.8 %collective-permute-start.65 = (bf16[16,64,512]{2,1,0:T(8,128)(2,1)}, bf16[16,64,512]{2,1,0:T(8,128)(2,1)}, u32[]{:S(2)}, u32[]{:S(2)}) collective-permute-start(bf16[16,64,512]{2,1,0:T(8,128)(2,1)} %copy-done.40), channel_id=1, source_target_pairs={{0,1},{1,0},{2,3},{3,2},{4,5},{5,4},{6,7},{7,6},{8,9},{9,8},{10,11... | collective-permute-start | bytes 3145736 | tf_op jit(solution)/shard_map/ppermute | solution.py:98
  453.9 203.6 %reduce-scatter.3.cloned.1.call-start = ((), (), s32[]{:S(2)}) async-start(), calls=%async_computation.6 | async-start | bytes 6684672 | tf_op jit(solution)/shard_map/reduce_scatter | solution.py:1201
  457.9 21.3 %collective-permute-start.61 = (bf16[8,64,512]{2,1,0:T(8,128)(2,1)}, bf16[8,64,512]{2,1,0:T(8,128)(2,1)}, u32[]{:S(2)}, u32[]{:S(2)}) collective-permute-start(bf16[8,64,512]{2,1,0:T(8,128)(2,1)} %slice.377), channel_id=1, source_target_pairs={{0,16},{16,0},{1,17},{17,1},{2,18},{18,2},{3,19},{19,3},{4,20},{20... | collective-permute-start | bytes 1572872 | tf_op jit(solution)/shard_map/ppermute | solution.py:98
  461.9 24.5 %collective-permute-start.56 = (bf16[8,64,512]{2,1,0:T(8,128)(2,1)}, bf16[8,64,512]{2,1,0:T(8,128)(2,1)}, u32[]{:S(2)}, u32[]{:S(2)}) collective-permute-start(bf16[8,64,512]{2,1,0:T(8,128)(2,1)} %slice.368), channel_id=1, source_target_pairs={{0,16},{16,0},{1,17},{17,1},{2,18},{18,2},{3,19},{19,3},{4,20},{20... | collective-permute-start | bytes 1572872 | tf_op jit(solution)/shard_map/ppermute | solution.py:98
  473.9 110.7 %collective-permute-start.86 = (bf16[32,1536]{1,0:T(8,128)(2,1)}, bf16[32,1536]{1,0:T(8,128)(2,1)}, u32[]{:S(2)}, u32[]{:S(2)}) collective-permute-start(bf16[32,1536]{1,0:T(8,128)(2,1)} %constant_dynamic-slice_fusion.8), channel_id=1, source_target_pairs={{0,16},{16,0},{1,17},{17,1},{2,18},{18,2},{3,19},{19,3},{4,20},{20... | collective-permute-start | bytes 294920 | tf_op jit(solution)/shard_map/ppermute | solution.py:98
  476.2 104.4 %collective-permute-start.93 = (bf16[256,1536]{1,0:T(8,128)(2,1)}, bf16[256,1536]{1,0:T(8,128)(2,1)S(1)}, u32[]{:S(2)}, u32[]{:S(2)}) collective-permute-start(bf16[256,1536]{1,0:T(8,128)(2,1)} %constant_dynamic-slice_fusion), channel_id=1, source_target_pairs={{0,16},{16,0},{1,17},{17,1},{2,18},{18,2},{3,19},{19,3},{4,20},{20... | collective-permute-start | bytes 2359304 | tf_op jit(solution)/shard_map/ppermute | solution.py:98
  486.3 21.2 %collective-permute-start.66 = (bf16[8,64,512]{2,1,0:T(8,128)(2,1)S(1)}, bf16[8,64,512]{2,1,0:T(8,128)(2,1)S(1)}, u32[]{:S(2)}, u32[]{:S(2)}) collective-permute-start(bf16[8,64,512]{2,1,0:T(8,128)(2,1)S(1)} %slice.386), channel_id=1, source_target_pairs={{0,2},{1,3},{2,0},{3,1},{4,6},{5,7},{6,4},{7,5},{8,10},{9,11},{10,... | collective-permute-start | bytes 1572872 | tf_op jit(solution)/shard_map/ppermute | solution.py:98
  562.3 30.3 %collective-permute-start.81 = (bf16[2,2,2,2,1,48,1280]{6,5,4,3,2,1,0:T(8,128)(2,1)}, bf16[2,2,2,2,1,48,1280]{6,5,4,3,2,1,0:T(8,128)(2,1)}, u32[]{:S(2)}, u32[]{:S(2)}) collective-permute-start(bf16[2,2,2,2,1,48,1280]{6,5,4,3,2,1,0:T(8,128)(2,1)} %constant_dynamic-slice_fusion.13), channel_id=1, source_target_pairs={{0,1},{1,0},{2,3},{3,2},{4,5},{5,4},{6,7},{7,6},{8,9},{9,8},{10,11... | collective-permute-start | bytes 5898248 | tf_op jit(solution)/shard_map/ppermute | solution.py:98
  568.0 28.1 %collective-permute-start.76 = (bf16[2,2,2,2,1,48,1280]{6,5,4,3,2,1,0:T(8,128)(2,1)S(1)}, bf16[2,2,2,2,1,48,1280]{6,5,4,3,2,1,0:T(8,128)(2,1)S(1)}, u32[]{:S(2)}, u32[]{:S(2)}) collective-permute-start(bf16[2,2,2,2,1,48,1280]{6,5,4,3,2,1,0:T(8,128)(2,1)S(1)} %constant_dynamic-slice_fusion.18), channel_id=1, source_target_pairs={{0,1},{1,0},{2,3},{3,2},{4,5},{5,4},{6,7},{7,6},{8,9},{9,8},{10,11... | collective-permute-start | bytes 5898248 | tf_op jit(solution)/shard_map/ppermute | solution.py:98
  596.4 23.5 %collective-permute-start.77 = (bf16[1,2,2,2,1,48,1280]{6,5,4,3,2,1,0:T(8,128)(2,1)S(1)}, bf16[1,2,2,2,1,48,1280]{6,5,4,3,2,1,0:T(8,128)(2,1)S(1)}, u32[]{:S(2)}, u32[]{:S(2)}) collective-permute-start(bf16[1,2,2,2,1,48,1280]{6,5,4,3,2,1,0:T(8,128)(2,1)S(1)} %constant_dynamic-slice_fusion.17), channel_id=1, source_target_pairs={{0,16},{16,0},{1,17},{17,1},{2,18},{18,2},{3,19},{19,3},{4,20},{20... | collective-permute-start | bytes 2949128 | tf_op jit(solution)/shard_map/ppermute | solution.py:98
  (283 other events, 2432.7 us)
Sparse Core Ops, SparseCore 0:
  11.6 76.3 all-gather.2
  90.8 73.8 all-gather.4
  400.0 114.0 reduce-scatter.4
  518.4 85.0 reduce-scatter.2

commit v4 on v3

--- a/solution.py
+++ b/solution.py
@@ -1299,9 +1299,9 @@
         ]
     )
     grad_halves = after(grad_halves, g_shgu)
-    g_expgu = scatter_head(grad_gate_up[:, : 2 * EXPERT_FF], grad_halves)[None]
-    g_expdown = scatter_head(grad_down[:EXPERT_FF], grad_halves)[None]
-    g_shdown = scatter_head(grad_down[EXPERT_FF : EXPERT_FF + heads_axis * unit], grad_halves)
+    g_expgu = scatter_head(grad_gate_up[:, : 2 * EXPERT_FF], pair_sums[:2])[None]
+    g_expdown = scatter_head(grad_down[:EXPERT_FF], pair_sums[:2])[None]
+    g_shdown = scatter_head(grad_down[EXPERT_FF : EXPERT_FF + heads_axis * unit], pair_sums[:2])
     grad_normed_in = back_dot(grad_halves[0], first_half) + back_dot(grad_halves[1], second_half)
     scaled_in = grad_normed_in * gain_in
     grad_gain_in = jnp.sum(grad_normed_in * inputs * inverse_in, axis=0)

time: 716 us -> 716 us (level)
  no operation moved by 1% of the time
where the time goes in v4:
time: 716 us; the launch traced here: 707 us
  waiting for transfers between devices  251 us (35%)
  other arithmetic  112 us (16%)
  starting transfers between devices  111 us (16%)
  Pallas kernels  84.2 us (12%)
  local copies, waits for them, and re-layouts  79.3 us (11%)
  matrix products  44.9 us (6%)
  between operations  24.7 us (3%)
    ppermute x99, waiting for transfers between devices, swap(): return lax.ppermute(values, name, [(i, i ^ bit) for i in range(size)])  245 us
    ppermute x99, starting transfers between devices, swap(): return lax.ppermute(values, name, [(i, i ^ bit) for i in range(size)])  97 us
    unnamed x448, local copies, waits for them, and re-layouts  36.2 us
    pallas_call x2, Pallas kernels, run_expert(): pl.pallas_call(functools.partial(expert_kernel, blocks), grid_spec=pltpu....  32.1 us
    pallas_call x4, Pallas kernels, attend_back(): pl.pallas_call(attend_back_kernel, grid=(groups,), in_specs=[wide, kv, kv...  19.4 us
    dot_general x7, matrix products, back_dot(): lax.dot_general(left, right, (((1,), (1,)), ((), ())), preferred_element_...  19.2 us
    mul x8, other arithmetic, adam_update(): -learn_rate  17.9 us
    add x28, other arithmetic, act(): total = kept + swap(sent, step)  14.6 us
  transfers between devices with their start and end apart: 107, of which 56 were waited for; matrix products, arithmetic and copies ran while one was open for 25% of the time, Pallas kernels for 12%

profile of v4, /device:TPU:0, one launch (start us, length us, event | category | flops | bytes accessed | tf_op | source)
XLA Modules:
  0.0 707.4 jit_solution(4146003587607671148)
XLA Ops:
  31.2 11.8 %collective-permute-done.5 = bf16[1,2,1,1,1,48,128]{6,5,1,4,3,2,0:T(8,128)(2,1)S(1)} collective-permute-done((bf16[1,2,1,1,1,48,128]{6,5,1,4,3,2,0:T(8,128)(2,1)S(1)}, bf16[1,2,1,1,1,48,128]{6,5,1,4,3,2,0:T(8,128)(2,1)S(1)}, u32[]{:S(2)}, u32[]{:S(2)}) %collective-permute-start.5) | collective-permute-done | bytes 24608 | tf_op jit(solution)/shard_map/ppermute | solution.py:98
  46.9 10.3 %collective-permute-done.8 = bf16[1,2,2,1,1,48,128]{6,5,2,1,4,3,0:T(8,128)(2,1)S(1)} collective-permute-done((bf16[1,2,2,1,1,48,128]{6,5,2,1,4,3,0:T(8,128)(2,1)S(1)}, bf16[1,2,2,1,1,48,128]{6,5,2,1,4,3,0:T(8,128)(2,1)S(1)}, u32[]{:S(2)}, u32[]{:S(2)}) %collective-permute-start.8) | collective-permute-done | bytes 49184 | tf_op jit(solution)/shard_map/ppermute | solution.py:98
  62.8 29.0 %collective-permute-done.11 = bf16[1,2,2,2,1,48,128]{6,5,3,2,1,4,0:T(8,128)(2,1)S(1)} collective-permute-done((bf16[1,2,2,2,1,48,128]{6,5,3,2,1,4,0:T(8,128)(2,1)S(1)}, bf16[1,2,2,2,1,48,128]{6,5,3,2,1,4,0:T(8,128)(2,1)S(1)}, u32[]{:S(2)}, u32[]{:S(2)}) %collective-permute-start.11) | collective-permute-done | bytes 98336 | tf_op jit(solution)/shard_map/ppermute | solution.py:98
  106.6 5.1 broadcast_select_fusion
  123.9 8.1 %collective-permute-done.15 = bf16[1,64,512]{2,1,0:T(8,128)(2,1)} collective-permute-done((bf16[1,64,512]{2,1,0:T(8,128)(2,1)S(1)}, bf16[1,64,512]{2,1,0:T(8,128)(2,1)}, u32[]{:S(2)}, u32[]{:S(2)}) %collective-permute-start.15) | collective-permute-done | bytes 65568 | tf_op jit(solution)/shard_map/ppermute | solution.py:98
  144.8 4.9 all-to-all-start
  154.7 6.3 collective-permute-done.21
  178.2 4.6 collective-permute-done.18
  210.0 5.7 collective-permute-done.28
  225.2 4.3 multiply_reduce_fusion.11
  250.9 9.1 %fusion = f32[2048,640]{1,0:T(8,128)} fusion(bf16[2048,1664]{1,0:T(8,128)(2,1)} %all-gather.5.cloned.1.call-done, bf16[64,1536]{1,0:T(8,128)(2,1)S(1)} %copy-done.151, bf16[512,1536]{1,0:T(8,128)(2,1)} %bitcast_select_fusion.1), kind=kOutput, calls=%fused_computation.3 | convolution fusion | flops 4033413120 | bytes 13303808 | tf_op jit(solution)/shard_map/dot_general | solution.py:48
  260.0 9.7 %collective-permute-done.38 = bf16[2,64,1536]{2,1,0:T(8,128)(2,1)S(1)} collective-permute-done((bf16[2,64,1536]{2,1,0:T(8,128)(2,1)S(1)}, bf16[2,64,1536]{2,1,0:T(8,128)(2,1)S(1)}, u32[]{:S(2)}, u32[]{:S(2)}) %collective-permute-start.38) | collective-permute-done | bytes 393248 | tf_op jit(solution)/shard_map/ppermute | solution.py:98
  273.7 13.5 %collective-permute-done.41 = bf16[4,64,1536]{2,1,0:T(8,128)(2,1)S(1)} collective-permute-done((bf16[4,64,1536]{2,1,0:T(8,128)(2,1)S(1)}, bf16[4,64,1536]{2,1,0:T(8,128)(2,1)S(1)}, u32[]{:S(2)}, u32[]{:S(2)}) %collective-permute-start.41) | collective-permute-done | bytes 786464 | tf_op jit(solution)/shard_map/ppermute | solution.py:98
  293.8 15.8 %expert.2 = (bf16[512,1664]{1,0:T(8,128)(2,1)}, bf16[512,1664]{1,0:T(8,128)(2,1)}, bf16[16,64,640]{2,1,0:T(8,128)(2,1)S(1)}, bf16[1024,1152]{1,0:T(8,128)(2,1)}) custom-call(s32[16]{0:T(128)S(1)} %copy-done.34, bf16[512,1536]{1,0:T(8,128)(2,1)S(1)} %bitcast.248, bf16[512,1536]{1,0:T(8,128)(2,1)S(1)} %bitcast.250, ...), custom_call_target="tpu_custom_call" | custom-call | flops 7247757312 | bytes 12582912 | tf_op jit(solution)/shard_map/expert/pallas_call | solution.py:485
  310.2 16.3 %expert.3 = (bf16[512,1664]{1,0:T(8,128)(2,1)}, bf16[512,1664]{1,0:T(8,128)(2,1)}, bf16[16,64,640]{2,1,0:T(8,128)(2,1)S(1)}, bf16[1024,1152]{1,0:T(8,128)(2,1)}) custom-call(s32[16]{0:T(128)S(1)} %copy-done.35, bf16[512,1536]{1,0:T(8,128)(2,1)S(1)} %bitcast.246, bf16[512,1536]{1,0:T(8,128)(2,1)S(1)} %bitcast.252, ...), custom_call_target="tpu_custom_call" | custom-call | flops 7247757312 | bytes 12582912 | tf_op jit(solution)/shard_map/expert/pallas_call | solution.py:485
  336.8 13.0 %outer_experts.1 = bf16[1536,1152]{1,0:T(8,128)(2,1)} custom-call(bf16[512,1536]{1,0:T(8,128)(2,1)S(1)} %bitcast.249, bf16[512,1536]{1,0:T(8,128)(2,1)S(1)} %bitcast.251, bf16[512,1536]{1,0:T(8,128)(2,1)S(1)} %bitcast.247, bf16[512,1536]{1,0:T(8,128)(2,1)} %bitcast.253, bf16[1024,1152]{1,0:T(8,128)(2,1)} %get-tuple-element.197.right0_ref, ...), custom_call_target="tpu_custom_call" | custom-call | flops 7247757312 | bytes 14548992 | tf_op jit(solution)/shard_map/outer_experts/pallas_call | solution.py:538
  360.9 8.3 %outer_acts.1 = bf16[640,1536]{1,0:T(8,128)(2,1)S(1)} custom-call(bf16[16,64,640]{2,1,0:T(8,128)(2,1)S(1)} %copy-done.37, bf16[16,64,640]{2,1,0:T(8,128)(2,1)S(1)} %copy-done.39, bf16[16,2,64,1664]{3,2,1,0:T(8,128)(2,1)} %bitcast.272), custom_call_target="tpu_custom_call" | custom-call | flops 4026531840 | bytes 10878976 | tf_op jit(solution)/shard_map/outer_acts/pallas_call | solution.py:569
  369.2 7.9 %collective-permute-done.51 = bf16[2,64,1664]{2,1,0:T(8,128)(2,1)S(1)} collective-permute-done((bf16[2,64,1664]{2,1,0:T(8,128)(2,1)S(1)}, bf16[2,64,1664]{2,1,0:T(8,128)(2,1)S(1)}, u32[]{:S(2)}, u32[]{:S(2)}) %collective-permute-start.51) | collective-permute-done | bytes 426016 | tf_op jit(solution)/shard_map/ppermute | solution.py:98
  413.8 5.2 attend_back.5
  421.4 5.3 attend_back.4
  432.9 5.3 attend_back.7
  480.6 5.7 collective-permute-done.56
  489.4 5.8 collective-permute-done.71
  495.3 12.2 %collective-permute-done.66 = bf16[8,64,512]{2,1,0:T(8,128)(2,1)S(1)} collective-permute-done((bf16[8,64,512]{2,1,0:T(8,128)(2,1)S(1)}, bf16[8,64,512]{2,1,0:T(8,128)(2,1)S(1)}, u32[]{:S(2)}, u32[]{:S(2)}) %collective-permute-start.66) | collective-permute-done | bytes 524320 | tf_op jit(solution)/shard_map/ppermute | solution.py:98
  507.7 5.5 collective-permute-done.62
  568.0 7.8 %collective-permute-done.88 = bf16[1,2,2,2,1,48,128]{5,6,4,3,2,1,0:T(8,128)(2,1)S(1)} collective-permute-done((bf16[1,2,2,2,1,48,128]{5,6,4,3,2,1,0:T(8,128)(2,1)S(1)}, bf16[1,2,2,2,1,48,128]{5,6,4,3,2,1,0:T(8,128)(2,1)S(1)}, u32[]{:S(2)}, u32[]{:S(2)}) %collective-permute-start.88) | collective-permute-done | bytes 98336 | tf_op jit(solution)/shard_map/ppermute | solution.py:98
  576.0 4.6 fusion.6
  597.1 18.3 %collective-permute-done.82 = bf16[2,2,2,1,1,48,1280]{6,5,4,3,2,1,0:T(8,128)(2,1)S(1)} collective-permute-done((bf16[2,2,2,1,1,48,1280]{6,5,4,3,2,1,0:T(8,128)(2,1)S(1)}, bf16[2,2,2,1,1,48,1280]{6,5,4,3,2,1,0:T(8,128)(2,1)S(1)}, u32[]{:S(2)}, u32[]{:S(2)}) %collective-permute-start.82) | collective-permute-done | bytes 983072 | tf_op jit(solution)/shard_map/ppermute | solution.py:98
  620.2 7.6 %collective-permute-done.83 = bf16[1,2,2,1,1,48,1280]{6,5,4,3,2,1,0:T(8,128)(2,1)S(1)} collective-permute-done((bf16[1,2,2,1,1,48,1280]{6,5,4,3,2,1,0:T(8,128)(2,1)S(1)}, bf16[1,2,2,1,1,48,1280]{6,5,4,3,2,1,0:T(8,128)(2,1)S(1)}, u32[]{:S(2)}, u32[]{:S(2)}) %collective-permute-start.83) | collective-permute-done | bytes 491552 | tf_op jit(solution)/shard_map/ppermute | solution.py:98
  630.6 6.5 collective-permute-done.84
  640.0 4.4 collective-permute-start.80
  682.4 7.8 %add_multiply_fusion = (f32[1,768,1024]{2,1,0:T(8,128)}, f32[1,768,1024]{2,1,0:T(8,128)}, f32[1,768,1024]{2,1,0:T(8,128)}) fusion(f32[1,768,1024]{2,1,0:T(8,128)S(1)} %copy-done.61, f32[]{:T(128)S(6)} %div.240, bf16[768,1024]{1,0:T(8,128)(2,1)} %collective-permute-done.92, bf16[1536,1024]{1,0:T(8,128)(2,1)} %copy-done.62, s32[]{:T(128)S(6)} %select_n.437, ...), kind=kLoop, calls=%fused_computation.19 | loop fusion | flops 14155776 | bytes 22020104 | tf_op jit(solution)/shard_map/mul | solution.py:78
  (930 shorter events, 397.1 us)
Async XLA Ops:
  7.3 217.9 %all-gather.3.cloned.1.call-start = ((), (), s32[]{:S(2)}) async-start(), calls=%async_computation.4 | async-start | bytes 4866048 | tf_op jit(solution)/shard_map/all_gather | solution.py:1049
  9.1 241.7 %all-gather.5.cloned.1.call-start = ((), (), s32[]{:S(2)}) async-start(), calls=%async_computation.5 | async-start | bytes 7241728 | tf_op jit(solution)/shard_map/all_gather | solution.py:1093
  18.1 169.4 %collective-permute-start.40 = (bf16[1,32,1536]{2,1,0:T(8,128)(2,1)}, bf16[1,32,1536]{2,1,0:T(8,128)(2,1)}, u32[]{:S(2)}, u32[]{:S(2)}) collective-permute-start(bf16[1,32,1536]{2,1,0:T(8,128)(2,1)} %convert_bitcast_fusion.5), channel_id=1, source_target_pairs={{0,16},{16,0},{1,17},{17,1},{2,18},{18,2},{3,19},{19,3},{4,20},{20... | collective-permute-start | bytes 294920 | tf_op jit(solution)/shard_map/ppermute | solution.py:98
  20.5 170.3 %collective-permute-start.39 = (bf16[1,256,1536]{2,1,0:T(8,128)(2,1)}, bf16[1,256,1536]{2,1,0:T(8,128)(2,1)}, u32[]{:S(2)}, u32[]{:S(2)}) collective-permute-start(bf16[1,256,1536]{2,1,0:T(8,128)(2,1)} %convert_element_type.216), channel_id=1, source_target_pairs={{0,16},{16,0},{1,17},{17,1},{2,18},{18,2},{3,19},{19,3},{4,20},{20... | collective-permute-start | bytes 2359304 | tf_op jit(solution)/shard_map/ppermute | solution.py:98
  58.6 33.3 %collective-permute-start.9 = (bf16[1,2,2,2,1,48,1280]{6,5,3,2,1,4,0:T(8,128)(2,1)}, bf16[1,2,2,2,1,48,1280]{6,5,3,2,1,4,0:T(8,128)(2,1)}, u32[]{:S(2)}, u32[]{:S(2)}) collective-permute-start(bf16[1,2,2,2,1,48,1280]{6,5,3,2,1,4,0:T(8,128)(2,1)} %broadcast_select_fusion.5), channel_id=1, source_target_pairs={{0,16},{16,0},{1,17},{17,1},{2,18},{18,2},{3,19},{19,3},{4,20},{20... | collective-permute-start | bytes 2949128 | tf_op jit(solution)/shard_map/ppermute | solution.py:98
  60.2 34.8 %collective-permute-start.10 = (bf16[2,2,2,1,1,48,1280]{6,5,2,1,0,4,3:T(8,128)(2,1)S(1)}, bf16[2,2,2,1,1,48,1280]{6,5,2,1,0,4,3:T(8,128)(2,1)}, u32[]{:S(2)}, u32[]{:S(2)}) collective-permute-start(bf16[2,2,2,1,1,48,1280]{6,5,2,1,0,4,3:T(8,128)(2,1)S(1)} %broadcast_select_fusion.4), channel_id=1, source_target_pairs={{0,2},{1,3},{2,0},{3,1},{4,6},{5,7},{6,4},{7,5},{8,10},{9,11},{10,... | collective-permute-start | bytes 2949128 | tf_op jit(solution)/shard_map/ppermute | solution.py:98
  61.9 29.9 %collective-permute-start.11 = (bf16[1,2,2,2,1,48,128]{6,5,3,2,1,4,0:T(8,128)(2,1)S(1)}, bf16[1,2,2,2,1,48,128]{6,5,3,2,1,4,0:T(8,128)(2,1)S(1)}, u32[]{:S(2)}, u32[]{:S(2)}) collective-permute-start(bf16[1,2,2,2,1,48,128]{6,5,3,2,1,4,0:T(8,128)(2,1)S(1)} %broadcast_select_fusion.13), channel_id=1, source_target_pairs={{0,16},{16,0},{1,17},{17,1},{2,18},{18,2},{3,19},{19,3},{4,20},{20... | collective-permute-start | bytes 294920 | tf_op jit(solution)/shard_map/ppermute | solution.py:98
  137.2 23.7 %collective-permute-start.21 = (bf16[2,64,512]{2,1,0:T(8,128)(2,1)}, bf16[2,64,512]{2,1,0:T(8,128)(2,1)}, u32[]{:S(2)}, u32[]{:S(2)}) collective-permute-start(bf16[2,64,512]{2,1,0:T(8,128)(2,1)} %get-tuple-element.493), channel_id=1, source_target_pairs={{0,4},{1,5},{2,6},{3,7},{4,0},{5,1},{6,2},{7,3},{8,12},{9,13},{10,... | collective-permute-start | bytes 393224 | tf_op jit(solution)/shard_map/ppermute | solution.py:98
  144.8 51.6 %all-to-all-start = ((bf16[16,48,128]{2,1,0:T(8,128)(2,1)}), bf16[16,48,128]{2,1,0:T(8,128)(2,1)}, u32[]{:S(2)}, u32[]{:S(2)}) async-start(bf16[16,48,128]{2,1,0:T(8,128)(2,1)} %copy.243), calls=%async_computation | async-start | bytes 393216 | tf_op jit(solution)/shard_map/all_to_all | solution.py:162
  149.7 500.3 %reduce-scatter.5.cloned.1.call-start = ((), (), s32[]{:S(2)}) async-start(), calls=%async_computation.7 | async-start | bytes 4866048 | tf_op jit(solution)/shard_map/reduce_scatter | solution.py:1204
  187.4 28.2 %collective-permute-start.19 = (bf16[16,64,512]{2,1,0:T(8,128)(2,1)S(1)}, bf16[16,64,512]{2,1,0:T(8,128)(2,1)}, u32[]{:S(2)}, u32[]{:S(2)}) collective-permute-start(bf16[16,64,512]{2,1,0:T(8,128)(2,1)S(1)} %constant_dynamic-update-slice_fusion.9.kv0_ref), channel_id=1, source_target_pairs={{0,1},{1,0},{2,3},{3,2},{4,5},{5,4},{6,7},{7,6},{8,9},{9,8},{10,11... | collective-permute-start | bytes 3145736 | tf_op jit(solution)/shard_map/ppermute | solution.py:98
  187.5 28.1 %collective-permute-start.24 = (bf16[16,64,512]{2,1,0:T(8,128)(2,1)S(1)}, bf16[16,64,512]{2,1,0:T(8,128)(2,1)S(1)}, u32[]{:S(2)}, u32[]{:S(2)}) collective-permute-start(bf16[16,64,512]{2,1,0:T(8,128)(2,1)S(1)} %constant_dynamic-update-slice_fusion.23.kv0_ref), channel_id=1, source_target_pairs={{0,1},{1,0},{2,3},{3,2},{4,5},{5,4},{6,7},{7,6},{8,9},{9,8},{10,11... | collective-permute-start | bytes 3145736 | tf_op jit(solution)/shard_map/ppermute | solution.py:98
  206.5 83.2 %collective-permute-start.43 = (bf16[1,768,1024]{2,1,0:T(8,128)(2,1)}, bf16[1,768,1024]{2,1,0:T(8,128)(2,1)}, u32[]{:S(2)}, u32[]{:S(2)}) collective-permute-start(bf16[1,768,1024]{2,1,0:T(8,128)(2,1)} %convert_element_type.220), channel_id=1, source_target_pairs={{0,16},{16,0},{1,17},{17,1},{2,18},{18,2},{3,19},{19,3},{4,20},{20... | collective-permute-start | bytes 4718600 | tf_op jit(solution)/shard_map/ppermute | solution.py:98
  216.8 21.2 %collective-permute-start.34 = (bf16[16,64,512]{2,1,0:T(8,128)(2,1)S(1)}, bf16[16,64,512]{2,1,0:T(8,128)(2,1)}, u32[]{:S(2)}, u32[]{:S(2)}) collective-permute-start(bf16[16,64,512]{2,1,0:T(8,128)(2,1)S(1)} %constant_dynamic-update-slice_fusion.44.kv0_ref), channel_id=1, source_target_pairs={{0,1},{1,0},{2,3},{3,2},{4,5},{5,4},{6,7},{7,6},{8,9},{9,8},{10,11... | collective-permute-start | bytes 3145736 | tf_op jit(solution)/shard_map/ppermute | solution.py:98
  288.7 21.4 %collective-permute-start.48 = (bf16[8,64,1536]{2,1,0:T(8,128)(2,1)S(1)}, bf16[8,64,1536]{2,1,0:T(8,128)(2,1)S(1)}, u32[]{:S(2)}, u32[]{:S(2)}) collective-permute-start(bf16[8,64,1536]{2,1,0:T(8,128)(2,1)S(1)} %constant_dynamic-update-slice_fusion.51), channel_id=1, source_target_pairs={{0,1},{1,0},{2,3},{3,2},{4,5},{5,4},{6,7},{7,6},{8,9},{9,8},{10,11... | collective-permute-start | bytes 4718600 | tf_op jit(solution)/shard_map/ppermute | solution.py:98
  332.4 21.4 %collective-permute-start.46 = (bf16[4,64,1664]{2,1,0:T(8,128)(2,1)S(1)}, bf16[4,64,1664]{2,1,0:T(8,128)(2,1)S(1)}, u32[]{:S(2)}, u32[]{:S(2)}) collective-permute-start(bf16[4,64,1664]{2,1,0:T(8,128)(2,1)S(1)} %slice.348), channel_id=1, source_target_pairs={{0,2},{1,3},{2,0},{3,1},{4,6},{5,7},{6,4},{7,5},{8,10},{9,11},{10,... | collective-permute-start | bytes 2555912 | tf_op jit(solution)/shard_map/ppermute | solution.py:98
  358.2 20.9 %collective-permute-start.52 = (bf16[2,64,1664]{2,1,0:T(8,128)(2,1)S(1)}, bf16[2,64,1664]{2,1,0:T(8,128)(2,1)S(1)}, u32[]{:S(2)}, u32[]{:S(2)}) collective-permute-start(bf16[2,64,1664]{2,1,0:T(8,128)(2,1)S(1)} %get-tuple-element.202), channel_id=1, source_target_pairs={{0,8},{1,9},{2,10},{3,11},{4,12},{5,13},{6,14},{7,15},{8,0},{9,1},... | collective-permute-start | bytes 1277960 | tf_op jit(solution)/shard_map/ppermute | solution.py:98
  405.3 42.1 %collective-permute-start.75 = (bf16[768,128]{1,0:T(8,128)(2,1)}, bf16[768,128]{1,0:T(8,128)(2,1)}, u32[]{:S(2)}, u32[]{:S(2)}) collective-permute-start(bf16[768,128]{1,0:T(8,128)(2,1)} %constant_dynamic-slice_fusion.19), channel_id=1, source_target_pairs={{0,16},{16,0},{1,17},{17,1},{2,18},{18,2},{3,19},{19,3},{4,20},{20... | collective-permute-start | bytes 589832 | tf_op jit(solution)/shard_map/ppermute | solution.py:98
  407.6 160.3 %collective-permute-start.92 = (bf16[768,1024]{1,0:T(8,128)(2,1)}, bf16[768,1024]{1,0:T(8,128)(2,1)}, u32[]{:S(2)}, u32[]{:S(2)}) collective-permute-start(bf16[768,1024]{1,0:T(8,128)(2,1)} %constant_dynamic-slice_fusion.1), channel_id=1, source_target_pairs={{0,16},{16,0},{1,17},{17,1},{2,18},{18,2},{3,19},{19,3},{4,20},{20... | collective-permute-start | bytes 4718600 | tf_op jit(solution)/shard_map/ppermute | solution.py:98
  419.0 36.3 %collective-permute-start.60 = (bf16[16,64,512]{2,1,0:T(8,128)(2,1)}, bf16[16,64,512]{2,1,0:T(8,128)(2,1)}, u32[]{:S(2)}, u32[]{:S(2)}) collective-permute-start(bf16[16,64,512]{2,1,0:T(8,128)(2,1)} %get-tuple-element.225), channel_id=1, source_target_pairs={{0,1},{1,0},{2,3},{3,2},{4,5},{5,4},{6,7},{7,6},{8,9},{9,8},{10,11... | collective-permute-start | bytes 3145736 | tf_op jit(solution)/shard_map/ppermute | solution.py:98
  427.6 31.7 %collective-permute-start.55 = (bf16[16,64,512]{2,1,0:T(8,128)(2,1)}, bf16[16,64,512]{2,1,0:T(8,128)(2,1)}, u32[]{:S(2)}, u32[]{:S(2)}) collective-permute-start(bf16[16,64,512]{2,1,0:T(8,128)(2,1)} %get-tuple-element.220), channel_id=1, source_target_pairs={{0,1},{1,0},{2,3},{3,2},{4,5},{5,4},{6,7},{7,6},{8,9},{9,8},{10,11... | collective-permute-start | bytes 3145736 | tf_op jit(solution)/shard_map/ppermute | solution.py:98
  438.1 35.7 %collective-permute-start.70 = (bf16[16,64,512]{2,1,0:T(8,128)(2,1)}, bf16[16,64,512]{2,1,0:T(8,128)(2,1)}, u32[]{:S(2)}, u32[]{:S(2)}) collective-permute-start(bf16[16,64,512]{2,1,0:T(8,128)(2,1)} %get-tuple-element.235), channel_id=1, source_target_pairs={{0,1},{1,0},{2,3},{3,2},{4,5},{5,4},{6,7},{7,6},{8,9},{9,8},{10,11... | collective-permute-start | bytes 3145736 | tf_op jit(solution)/shard_map/ppermute | solution.py:98
  447.4 28.8 %collective-permute-start.65 = (bf16[16,64,512]{2,1,0:T(8,128)(2,1)}, bf16[16,64,512]{2,1,0:T(8,128)(2,1)}, u32[]{:S(2)}, u32[]{:S(2)}) collective-permute-start(bf16[16,64,512]{2,1,0:T(8,128)(2,1)} %copy-done.40), channel_id=1, source_target_pairs={{0,1},{1,0},{2,3},{3,2},{4,5},{5,4},{6,7},{7,6},{8,9},{9,8},{10,11... | collective-permute-start | bytes 3145736 | tf_op jit(solution)/shard_map/ppermute | solution.py:98
  453.9 203.6 %reduce-scatter.3.cloned.1.call-start = ((), (), s32[]{:S(2)}) async-start(), calls=%async_computation.6 | async-start | bytes 6684672 | tf_op jit(solution)/shard_map/reduce_scatter | solution.py:1201
  457.9 21.3 %collective-permute-start.61 = (bf16[8,64,512]{2,1,0:T(8,128)(2,1)}, bf16[8,64,512]{2,1,0:T(8,128)(2,1)}, u32[]{:S(2)}, u32[]{:S(2)}) collective-permute-start(bf16[8,64,512]{2,1,0:T(8,128)(2,1)} %slice.377), channel_id=1, source_target_pairs={{0,16},{16,0},{1,17},{17,1},{2,18},{18,2},{3,19},{19,3},{4,20},{20... | collective-permute-start | bytes 1572872 | tf_op jit(solution)/shard_map/ppermute | solution.py:98
  461.9 24.5 %collective-permute-start.56 = (bf16[8,64,512]{2,1,0:T(8,128)(2,1)}, bf16[8,64,512]{2,1,0:T(8,128)(2,1)}, u32[]{:S(2)}, u32[]{:S(2)}) collective-permute-start(bf16[8,64,512]{2,1,0:T(8,128)(2,1)} %slice.368), channel_id=1, source_target_pairs={{0,16},{16,0},{1,17},{17,1},{2,18},{18,2},{3,19},{19,3},{4,20},{20... | collective-permute-start | bytes 1572872 | tf_op jit(solution)/shard_map/ppermute | solution.py:98
  473.9 110.7 %collective-permute-start.86 = (bf16[32,1536]{1,0:T(8,128)(2,1)}, bf16[32,1536]{1,0:T(8,128)(2,1)}, u32[]{:S(2)}, u32[]{:S(2)}) collective-permute-start(bf16[32,1536]{1,0:T(8,128)(2,1)} %constant_dynamic-slice_fusion.8), channel_id=1, source_target_pairs={{0,16},{16,0},{1,17},{17,1},{2,18},{18,2},{3,19},{19,3},{4,20},{20... | collective-permute-start | bytes 294920 | tf_op jit(solution)/shard_map/ppermute | solution.py:98
  476.2 104.4 %collective-permute-start.93 = (bf16[256,1536]{1,0:T(8,128)(2,1)}, bf16[256,1536]{1,0:T(8,128)(2,1)S(1)}, u32[]{:S(2)}, u32[]{:S(2)}) collective-permute-start(bf16[256,1536]{1,0:T(8,128)(2,1)} %constant_dynamic-slice_fusion), channel_id=1, source_target_pairs={{0,16},{16,0},{1,17},{17,1},{2,18},{18,2},{3,19},{19,3},{4,20},{20... | collective-permute-start | bytes 2359304 | tf_op jit(solution)/shard_map/ppermute | solution.py:98
  486.3 21.2 %collective-permute-start.66 = (bf16[8,64,512]{2,1,0:T(8,128)(2,1)S(1)}, bf16[8,64,512]{2,1,0:T(8,128)(2,1)S(1)}, u32[]{:S(2)}, u32[]{:S(2)}) collective-permute-start(bf16[8,64,512]{2,1,0:T(8,128)(2,1)S(1)} %slice.386), channel_id=1, source_target_pairs={{0,2},{1,3},{2,0},{3,1},{4,6},{5,7},{6,4},{7,5},{8,10},{9,11},{10,... | collective-permute-start | bytes 1572872 | tf_op jit(solution)/shard_map/ppermute | solution.py:98
  562.3 30.3 %collective-permute-start.81 = (bf16[2,2,2,2,1,48,1280]{6,5,4,3,2,1,0:T(8,128)(2,1)}, bf16[2,2,2,2,1,48,1280]{6,5,4,3,2,1,0:T(8,128)(2,1)}, u32[]{:S(2)}, u32[]{:S(2)}) collective-permute-start(bf16[2,2,2,2,1,48,1280]{6,5,4,3,2,1,0:T(8,128)(2,1)} %constant_dynamic-slice_fusion.13), channel_id=1, source_target_pairs={{0,1},{1,0},{2,3},{3,2},{4,5},{5,4},{6,7},{7,6},{8,9},{9,8},{10,11... | collective-permute-start | bytes 5898248 | tf_op jit(solution)/shard_map/ppermute | solution.py:98
  568.0 28.1 %collective-permute-start.76 = (bf16[2,2,2,2,1,48,1280]{6,5,4,3,2,1,0:T(8,128)(2,1)S(1)}, bf16[2,2,2,2,1,48,1280]{6,5,4,3,2,1,0:T(8,128)(2,1)S(1)}, u32[]{:S(2)}, u32[]{:S(2)}) collective-permute-start(bf16[2,2,2,2,1,48,1280]{6,5,4,3,2,1,0:T(8,128)(2,1)S(1)} %constant_dynamic-slice_fusion.18), channel_id=1, source_target_pairs={{0,1},{1,0},{2,3},{3,2},{4,5},{5,4},{6,7},{7,6},{8,9},{9,8},{10,11... | collective-permute-start | bytes 5898248 | tf_op jit(solution)/shard_map/ppermute | solution.py:98
  596.4 23.5 %collective-permute-start.77 = (bf16[1,2,2,2,1,48,1280]{6,5,4,3,2,1,0:T(8,128)(2,1)S(1)}, bf16[1,2,2,2,1,48,1280]{6,5,4,3,2,1,0:T(8,128)(2,1)S(1)}, u32[]{:S(2)}, u32[]{:S(2)}) collective-permute-start(bf16[1,2,2,2,1,48,1280]{6,5,4,3,2,1,0:T(8,128)(2,1)S(1)} %constant_dynamic-slice_fusion.17), channel_id=1, source_target_pairs={{0,16},{16,0},{1,17},{17,1},{2,18},{18,2},{3,19},{19,3},{4,20},{20... | collective-permute-start | bytes 2949128 | tf_op jit(solution)/shard_map/ppermute | solution.py:98
  (283 other events, 2432.7 us)
Sparse Core Ops, SparseCore 0:
  11.6 76.3 all-gather.2
  90.8 73.8 all-gather.4
  400.0 114.0 reduce-scatter.4
  518.4 85.0 reduce-scatter.2
